TPU v7x, 32 devices: a whole 2x2x4 slice. The times are simulated.
32 devices in a mesh: section: 2 (over x), dp: 4 (over z), tensor: 4 (over y, core).
Axes of the slice: x: 2, y: 2, z: 4, core: 2. Of those that a mesh axis runs over, the one named last changes fastest.
Arguments:
- activations: bfloat16 [2, 8, 256, 2048], P('section', 'dp', 'tensor'), may hold values from -6 to 6
- ln_gains: bfloat16 [2, 2, 2048], P('section', None, ('dp', 'tensor')), may hold values from 0.099609375 to 1.8984375
- biases: bfloat16 [2, 4, 2048], P('section', None, ('dp', 'tensor')), may hold values from -2 to 2
- w_qkv: bfloat16 [2, 2048, 3, 2048], P('section', 'dp', None, 'tensor'), may hold values from -0.125 to 0.125
- qv_bias: bfloat16 [2, 2, 16, 128], P('section', None, 'tensor', 'dp'), may hold values from -2 to 2
- w_out: bfloat16 [2, 2048, 2048], P('section', 'tensor', 'dp'), may hold values from -0.375 to 0.375
- w_up: bfloat16 [2, 2048, 8192], P('section', 'dp', 'tensor'), may hold values from -0.125 to 0.125
- up_bias: bfloat16 [2, 64, 128], P('section', 'tensor', 'dp'), may hold values from -2 to 2
- w_down: bfloat16 [2, 8192, 2048], P('section', 'tensor', 'dp'), may hold values from -0.09375 to 0.09375
- prefix: int32 [8], P('dp'), may hold values from 25 to 128
Outputs:
- block_ends: float32 [2, 8, 256, 2048], P('section', 'dp', 'tensor')
- ln_gains_grad: float32 [2, 2, 2048], P('section', None, ('dp', 'tensor'))
- biases_grad: float32 [2, 4, 2048], P('section', None, ('dp', 'tensor'))
- w_qkv_grad: float32 [2, 2048, 3, 2048], P('section', 'dp', None, 'tensor')
- qv_bias_grad: float32 [2, 2, 16, 128], P('section', None, 'tensor', 'dp')
- w_out_grad: float32 [2, 2048, 2048], P('section', 'tensor', 'dp')
- w_up_grad: float32 [2, 2048, 8192], P('section', 'dp', 'tensor')
- up_bias_grad: float32 [2, 64, 128], P('section', 'tensor', 'dp')
- w_down_grad: float32 [2, 8192, 2048], P('section', 'tensor', 'dp')
All inputs are finite; a program needn't handle non-finite values.
Results may differ from a plain program's by a relative error of at most 0.02.
Values may be sent and summed in bfloat16 or wider, within the bound.
A program may use at most 192 MiB of HBM per device.

v0:
```python
import jax
import jax.numpy as jnp
from jax import lax
from jax.sharding import PartitionSpec as P


def shifted(block, axis, distance):
    devices = range(lax.axis_size(axis))
    route = [(i - distance, i) for i in devices if i - distance in devices]
    return lax.ppermute(block, axis, route)


def layer_norm(hidden, gain, shift_vec):
    centre = hidden - jnp.mean(hidden, axis=-1, keepdims=True)
    spread = jnp.mean(centre * centre, axis=-1, keepdims=True)
    return centre * lax.rsqrt(spread + 1e-05) * gain + shift_vec


def spread_rows(local_part):
    return lax.all_gather(local_part, "tensor", axis=0, tiled=True)


def collect_rows(term_fn, row_number):
    return lax.psum_scatter(
        term_fn(jnp.int32(0), row_number * lax.axis_size("tensor")).astype(jnp.bfloat16),
        "tensor",
        scatter_dimension=0,
        tiled=True,
    ).astype(jnp.float32)


def spread_grads(local_part):
    return lax.all_gather(local_part, "tensor", axis=0, tiled=True)


def collect_grads(term_fn, row_number):
    return lax.psum_scatter(
        term_fn(jnp.int32(0), row_number * lax.axis_size("tensor")).astype(jnp.bfloat16),
        "tensor",
        scatter_dimension=0,
        tiled=True,
    ).astype(jnp.float32)


def score_block(queries, keys_proj, length, slopes):
    seq_len = queries.shape[0]
    head_dim = queries.shape[2]
    raw_scores = jnp.einsum("qhe,khe->hqk", queries, keys_proj, preferred_element_type=jnp.float32)
    positions = jnp.arange(seq_len)
    offsets = (positions[:, None] - positions[None, :]).astype(jnp.float32)
    allowed = (positions[None, :] <= positions[:, None]) | (positions[None, :] < length)
    scores = raw_scores * head_dim ** (-0.5) - slopes[:, None, None] * offsets
    return jnp.where(allowed, scores, -1e30)


def layer_forward(hidden, length, weights, vectors, slopes):
    w_qkv, w_out, w_up, w_down, qv_bias, up_bias = weights
    gain_rows, bias_rows = vectors
    local_rows = hidden.shape[0]
    num_heads = qv_bias.shape[1]
    head_dim = qv_bias.shape[2]
    width_local = num_heads * head_dim
    normed = spread_rows(layer_norm(hidden, gain_rows[0], bias_rows[0]).astype(jnp.bfloat16))
    seq_len = normed.shape[0]
    proj = jnp.einsum("td,dcf->ctf", normed, w_qkv, preferred_element_type=jnp.float32)
    qv_flat = qv_bias.astype(jnp.float32).reshape(2, width_local)
    queries = (proj[0] + qv_flat[0]).astype(jnp.bfloat16).reshape(seq_len, num_heads, head_dim)
    keys_proj = proj[1].astype(jnp.bfloat16).reshape(seq_len, num_heads, head_dim)
    values_proj = (proj[2] + qv_flat[1]).astype(jnp.bfloat16).reshape(seq_len, num_heads, head_dim)
    scores = score_block(queries, keys_proj, length, slopes)
    peak = jnp.max(scores, axis=-1, keepdims=True)
    expon = jnp.exp(scores - peak)
    totals_row = jnp.sum(expon, axis=-1, keepdims=True)
    attention_probs = (expon / totals_row).astype(jnp.bfloat16)
    log_total = (peak + jnp.log(totals_row))[..., 0]
    mixed_heads = jnp.einsum(
        "hqk,khe->qhe", attention_probs, values_proj, preferred_element_type=jnp.float32
    )
    mixed_heads = mixed_heads.astype(jnp.bfloat16).reshape(seq_len, width_local)

    def attention_term(first_row, row_total):
        return jnp.dot(mixed_heads, w_out, preferred_element_type=jnp.float32)

    middle = hidden + collect_rows(attention_term, local_rows) + bias_rows[2]
    second = spread_rows(layer_norm(middle, gain_rows[1], bias_rows[1]).astype(jnp.bfloat16))
    up_proj = jnp.dot(second, w_up, preferred_element_type=jnp.float32) + up_bias.astype(
        jnp.float32
    ).reshape(-1)
    activated = jax.nn.gelu(up_proj, approximate=True).astype(jnp.bfloat16)

    def feed_term(first_row, row_total):
        return jnp.dot(activated, w_down, preferred_element_type=jnp.float32)

    output = middle + collect_rows(feed_term, local_rows) + bias_rows[3]
    kept = (
        hidden,
        middle,
        normed,
        queries,
        keys_proj,
        values_proj,
        log_total,
        mixed_heads,
        second,
        up_proj,
        activated,
    )
    return (output, kept)


def layer_backward(grad_out, kept, length, weights, vectors, slopes):
    (
        hidden,
        middle,
        normed,
        queries,
        keys_proj,
        values_proj,
        log_total,
        mixed_heads,
        second,
        up_proj,
        activated,
    ) = kept
    w_qkv, w_out, w_up, w_down, qv_bias, up_bias = weights
    gain_rows, bias_rows = vectors
    local_rows = grad_out.shape[0]
    seq_len = normed.shape[0]
    num_heads = qv_bias.shape[1]
    head_dim = qv_bias.shape[2]
    width_local = num_heads * head_dim
    grad_full = spread_grads(grad_out.astype(jnp.bfloat16))
    grad_down_bias = jnp.sum(grad_out, axis=0)
    grad_act = jnp.einsum("td,fd->tf", grad_full, w_down, preferred_element_type=jnp.float32)
    grad_w_down = jnp.einsum("tf,td->fd", activated, grad_full, preferred_element_type=jnp.float32)
    unused_value, gelu_pull = jax.vjp(lambda inner: jax.nn.gelu(inner, approximate=True), up_proj)
    grad_up = gelu_pull(grad_act)[0].astype(jnp.bfloat16)
    grad_up_bias = jnp.sum(grad_up.astype(jnp.float32), axis=0)
    grad_w_up = jnp.einsum("td,tf->df", second, grad_up, preferred_element_type=jnp.float32)

    def second_term(first_row, row_total):
        return jnp.einsum("tf,df->td", grad_up, w_up, preferred_element_type=jnp.float32)

    grad_second = collect_grads(second_term, local_rows)
    unused_second, second_pull = jax.vjp(layer_norm, middle, gain_rows[1], bias_rows[1])
    grad_mid_in, grad_gain_two, grad_bias_two = second_pull(grad_second)
    grad_middle = grad_out + grad_mid_in
    grad_full_two = spread_grads(grad_middle.astype(jnp.bfloat16))
    grad_out_bias = jnp.sum(grad_middle, axis=0)
    grad_mixed = jnp.einsum(
        "td,fd->tf", grad_full_two, w_out, preferred_element_type=jnp.float32
    ).astype(jnp.bfloat16)
    grad_w_out = jnp.einsum(
        "tf,td->fd", mixed_heads, grad_full_two, preferred_element_type=jnp.float32
    )
    grad_heads = grad_mixed.reshape(seq_len, num_heads, head_dim)
    scores = score_block(queries, keys_proj, length, slopes)
    probs = jnp.exp(scores - log_total[..., None])
    grad_probs = jnp.einsum(
        "qhe,khe->hqk", grad_heads, values_proj, preferred_element_type=jnp.float32
    )
    inner_sum = jnp.sum(probs * grad_probs, axis=-1, keepdims=True)
    grad_raw = (probs * (grad_probs - inner_sum) * head_dim ** (-0.5)).astype(jnp.bfloat16)
    grad_query = jnp.einsum(
        "hqk,khe->qhe", grad_raw, keys_proj, preferred_element_type=jnp.float32
    ).astype(jnp.bfloat16)
    grad_key = jnp.einsum(
        "hqk,qhe->khe", grad_raw, queries, preferred_element_type=jnp.float32
    ).astype(jnp.bfloat16)
    grad_value = jnp.einsum(
        "hqk,qhe->khe", probs.astype(jnp.bfloat16), grad_heads, preferred_element_type=jnp.float32
    ).astype(jnp.bfloat16)
    grad_proj = jnp.stack([grad_query, grad_key, grad_value], axis=1).reshape(
        seq_len, 3, width_local
    )
    grad_qv_bias = jnp.stack(
        [
            jnp.sum(grad_query.astype(jnp.float32), axis=0),
            jnp.sum(grad_value.astype(jnp.float32), axis=0),
        ]
    )
    grad_w_qkv = jnp.einsum("td,tcf->dcf", normed, grad_proj, preferred_element_type=jnp.float32)

    def first_term(first_row, row_total):
        return jnp.einsum("tcf,dcf->td", grad_proj, w_qkv, preferred_element_type=jnp.float32)

    grad_normed = collect_grads(first_term, local_rows)
    unused_first, first_pull = jax.vjp(layer_norm, hidden, gain_rows[0], bias_rows[0])
    grad_hid_in, grad_gain_one, grad_bias_one = first_pull(grad_normed)
    grad_hidden = grad_middle + grad_hid_in
    matrix_grads = (
        grad_w_qkv,
        grad_w_out,
        grad_w_up,
        grad_w_down,
        grad_qv_bias,
        grad_up_bias.reshape(up_bias.shape),
    )
    vector_part = (
        jnp.stack([grad_gain_one, grad_gain_two]),
        jnp.stack([grad_bias_one, grad_bias_two, grad_out_bias, grad_down_bias]),
    )
    return (grad_hidden, matrix_grads, vector_part)


def on_device(activations, ln_gains, biases, w_qkv, qv_bias, w_out, w_up, up_bias, w_down, prefix):
    section_index = lax.axis_index("section")
    is_first = section_index == 0
    batches = activations.shape[1]
    own_rows = activations[0].astype(jnp.float32)
    gain_full, bias_full = (
        lax.all_gather(ln_gains[0], ("dp", "tensor"), axis=1, tiled=True),
        lax.all_gather(biases[0], ("dp", "tensor"), axis=1, tiled=True),
    )
    vectors = (gain_full.astype(jnp.float32), bias_full.astype(jnp.float32))
    weights = (
        lax.all_gather(w_qkv[0], "dp", axis=0, tiled=True),
        lax.all_gather(w_out[0], "dp", axis=1, tiled=True),
        lax.all_gather(w_up[0], "dp", axis=0, tiled=True),
        lax.all_gather(w_down[0], "dp", axis=1, tiled=True),
        lax.all_gather(qv_bias[0], "dp", axis=2, tiled=True),
        lax.all_gather(up_bias[0], "dp", axis=1, tiled=True),
    )
    local_heads = qv_bias.shape[2]
    total_heads = local_heads * lax.axis_size("tensor")
    head_ids = lax.axis_index("tensor") * local_heads + jnp.arange(local_heads)
    slopes = jnp.exp2(-8.0 * (head_ids.astype(jnp.float32) + 1.0) / total_heads)
    incoming = jnp.zeros_like(own_rows[0])
    outputs = []
    saved = []
    for moment in range(batches + 1):
        ahead = min(moment, batches - 1)
        behind = max(moment - 1, 0)
        source = jnp.where(is_first, own_rows[ahead], incoming)
        length = jnp.where(is_first, prefix[ahead], prefix[behind])
        result, kept = layer_forward(source, length, weights, vectors, slopes)
        outputs.append(result)
        saved.append(kept)
        if moment < batches:
            incoming = shifted(result.astype(jnp.bfloat16), "section", 1).astype(jnp.float32)
    back_weights = (
        lax.all_gather(w_qkv[0], "dp", axis=0, tiled=True),
        lax.all_gather(w_out[0], "dp", axis=1, tiled=True),
        lax.all_gather(w_up[0], "dp", axis=0, tiled=True),
        lax.all_gather(w_down[0], "dp", axis=1, tiled=True),
        lax.all_gather(qv_bias[0], "dp", axis=2, tiled=True),
        lax.all_gather(up_bias[0], "dp", axis=1, tiled=True),
    )
    stacked = jax.tree.map(lambda *pieces: jnp.stack(pieces), *saved)
    returned = jnp.zeros_like(own_rows[0])
    grad_list = []
    matrix_sums = None
    vector_sums = None
    for moment in range(batches + 1):
        ahead = min(moment, batches - 1)
        behind = max(moment - 1, 0)
        pick = jnp.where(is_first, behind, min(moment + 1, batches))
        kept = jax.tree.map(
            lambda stack_arr: lax.dynamic_index_in_dim(stack_arr, pick, 0, keepdims=False), stacked
        )
        if moment < batches:
            cotangent = own_rows[moment]
        else:
            cotangent = jnp.zeros_like(own_rows[0])
        grad_out = jnp.where(is_first, returned, cotangent)
        length = jnp.where(is_first, prefix[behind], prefix[ahead])
        grad_hidden, matrix_grads, vector_part = layer_backward(
            grad_out, kept, length, back_weights, vectors, slopes
        )
        grad_list.append(grad_hidden)
        if moment == 0:
            matrix_sums = matrix_grads
            vector_sums = vector_part
        else:
            matrix_sums = tuple((older + newer for older, newer in zip(matrix_sums, matrix_grads)))
            vector_sums = tuple((older + newer for older, newer in zip(vector_sums, vector_part)))
        if moment < batches:
            returned = shifted(grad_hidden.astype(jnp.bfloat16), "section", -1).astype(jnp.float32)
    matrix_sums = (
        lax.psum_scatter(
            matrix_sums[0].astype(jnp.bfloat16), "dp", scatter_dimension=0, tiled=True
        ).astype(jnp.float32),
        lax.psum_scatter(
            matrix_sums[1].astype(jnp.bfloat16), "dp", scatter_dimension=1, tiled=True
        ).astype(jnp.float32),
        lax.psum_scatter(
            matrix_sums[2].astype(jnp.bfloat16), "dp", scatter_dimension=0, tiled=True
        ).astype(jnp.float32),
        lax.psum_scatter(
            matrix_sums[3].astype(jnp.bfloat16), "dp", scatter_dimension=1, tiled=True
        ).astype(jnp.float32),
        lax.psum_scatter(
            matrix_sums[4].astype(jnp.bfloat16), "dp", scatter_dimension=2, tiled=True
        ).astype(jnp.float32),
        lax.psum_scatter(
            matrix_sums[5].astype(jnp.bfloat16), "dp", scatter_dimension=1, tiled=True
        ).astype(jnp.float32),
    )
    gain_grad, bias_grad = lax.psum_scatter(
        vector_sums, ("dp", "tensor"), scatter_dimension=1, tiled=True
    )
    block_ends = jnp.stack(
        [jnp.where(is_first, grad_list[index + 1], outputs[index + 1]) for index in range(batches)]
    )
    return (
        block_ends[None],
        gain_grad[None],
        bias_grad[None],
        matrix_sums[0][None],
        matrix_sums[4][None],
        matrix_sums[1][None],
        matrix_sums[2][None],
        matrix_sums[5][None],
        matrix_sums[3][None],
    )


def solution(mesh):
    in_specs = (
        P("section", "dp", "tensor", None),
        P("section", None, ("dp", "tensor")),
        P("section", None, ("dp", "tensor")),
        P("section", "dp", None, "tensor"),
        P("section", None, "tensor", "dp"),
        P("section", "tensor", "dp"),
        P("section", "dp", "tensor"),
        P("section", "tensor", "dp"),
        P("section", "tensor", "dp"),
        P("dp"),
    )
    out_specs = (
        P("section", "dp", "tensor", None),
        P("section", None, ("dp", "tensor")),
        P("section", None, ("dp", "tensor")),
        P("section", "dp", None, "tensor"),
        P("section", None, "tensor", "dp"),
        P("section", "tensor", "dp"),
        P("section", "dp", "tensor"),
        P("section", "tensor", "dp"),
        P("section", "tensor", "dp"),
    )
    return jax.shard_map(
        on_device, mesh=mesh, in_specs=in_specs, out_specs=out_specs, check_vma=False
    )
```

profile of v0, /device:TPU:0, one launch (start us, length us, event | category | flops | bytes accessed | tf_op | source)
XLA Modules:
  0.0 1892.5 jit_solution(7883927738998703399)
XLA Ops:
  7.2 23.4 %all-gather.2 = bf16[1,4,2048]{2,1,0:T(4,128)(2,1)S(1)} all-gather(bf16[1,4,128]{2,1,0:T(4,128)(2,1)} %param.12), channel_id=4, replica_groups=mesh['section'=2,'dp'=4,'tensor'=4] {'dp','tensor'}, dimensions={2}, use_global_device_ids=true | all-gather | bytes 17408 | tf_op jit(solution)/shard_map/all_gather | solution.py:213
  31.8 17.5 all-gather.1
  53.5 13.1 all-gather.4
  69.1 115.0 %all-gather.51.cloned.1.call-done = bf16[1,2048,3,512]{3,1,2,0:T(8,128)(2,1)} async-done(((bf16[1,512,3,512]{3,1,2,0:T(8,128)(2,1)}), bf16[1,2048,3,512]{3,1,2,0:T(8,128)(2,1)}) %all-gather.51.cloned.1.call-update) | async-done | bytes 6291472 | tf_op jit(solution)/shard_map/all_gather | solution.py:217
  196.4 33.4 %all-gather.53.cloned.1.call-done = bf16[1,512,2048]{2,1,0:T(8,128)(2,1)} async-done(((bf16[1,512,512]{2,1,0:T(8,128)(2,1)}), bf16[1,512,2048]{2,1,0:T(8,128)(2,1)}) %all-gather.53.cloned.1.call-update) | async-done | bytes 2097168 | tf_op jit(solution)/shard_map/all_gather | solution.py:218
  233.8 23.1 %reduce-scatter.29.cloned.1.call-done = bf16[64,2048]{1,0:T(8,128)(2,1)} async-done(((bf16[256,2048]{1,0:T(8,128)(2,1)}), bf16[64,2048]{1,0:T(8,128)(2,1)}) %reduce-scatter.29.cloned.1.call-update) | async-done | bytes 262160 | tf_op jit(solution)/shard_map/reduce_scatter | solution.py:24
  260.1 13.3 all-gather.7
  273.4 134.8 %all-gather.55.cloned.1.call-done = bf16[1,2048,2048]{2,1,0:T(8,128)(2,1)} async-done(((bf16[1,512,2048]{2,1,0:T(8,128)(2,1)}), bf16[1,2048,2048]{2,1,0:T(8,128)(2,1)}) %all-gather.55.cloned.1.call-update) | async-done | bytes 8388624 | tf_op jit(solution)/shard_map/all_gather | solution.py:219
  408.2 16.9 all-gather.29.cloned.1.call-done
  425.1 7.4 fusion.48
  432.5 143.9 %all-gather.49.cloned.1.call-done = bf16[1,2048,2048]{2,1,0:T(8,128)(2,1)} async-done(((bf16[1,2048,512]{2,1,0:T(8,128)(2,1)}), bf16[1,2048,2048]{2,1,0:T(8,128)(2,1)}) %all-gather.49.cloned.1.call-update) | async-done | bytes 8388624 | tf_op jit(solution)/shard_map/all_gather | solution.py:245
  576.4 7.5 fusion.66
  584.0 23.2 %reduce-scatter.31.cloned.1.call-done = bf16[64,2048]{1,0:T(8,128)(2,1)} async-done(((bf16[256,2048]{1,0:T(8,128)(2,1)}), bf16[64,2048]{1,0:T(8,128)(2,1)}) %reduce-scatter.31.cloned.1.call-update) | async-done | bytes 262160 | tf_op jit(solution)/shard_map/reduce_scatter | solution.py:24
  620.1 16.2 all-gather.31.cloned.1.call-done
  651.2 25.0 %reduce-scatter.33.cloned.1.call-done = bf16[64,2048]{1,0:T(8,128)(2,1)} async-done(((bf16[256,2048]{1,0:T(8,128)(2,1)}), bf16[64,2048]{1,0:T(8,128)(2,1)}) %reduce-scatter.33.cloned.1.call-update) | async-done | bytes 262160 | tf_op jit(solution)/shard_map/reduce_scatter | solution.py:24
  678.5 16.8 all-gather.33.cloned.1.call-done
  695.4 6.0 fusion.51
  702.7 6.9 fusion.69
  709.7 25.0 %reduce-scatter.35.cloned.1.call-done = bf16[64,2048]{1,0:T(8,128)(2,1)} async-done(((bf16[256,2048]{1,0:T(8,128)(2,1)}), bf16[64,2048]{1,0:T(8,128)(2,1)}) %reduce-scatter.35.cloned.1.call-update) | async-done | bytes 262160 | tf_op jit(solution)/shard_map/reduce_scatter | solution.py:24
  739.1 5.6 collective-permute-done.1
  746.8 17.1 all-gather.35.cloned.1.call-done
  780.6 25.0 %reduce-scatter.37.cloned.1.call-done = bf16[64,2048]{1,0:T(8,128)(2,1)} async-done(((bf16[256,2048]{1,0:T(8,128)(2,1)}), bf16[64,2048]{1,0:T(8,128)(2,1)}) %reduce-scatter.37.cloned.1.call-update) | async-done | bytes 262160 | tf_op jit(solution)/shard_map/reduce_scatter | solution.py:24
  809.1 15.6 all-gather.37.cloned.1.call-done
  824.7 6.2 fusion.54
  835.3 8.2 all-gather.25.cloned.1.call-done
  843.5 8.3 convert_reduce_fusion.2
  852.9 6.8 fusion.75
  874.1 10.7 reduce-scatter.39.cloned.1.call-done
  899.1 7.8 all-gather.39.cloned.1.call-done
  921.1 5.7 fusion.63
  928.9 22.9 %reduce-scatter.41.cloned.1.call-done = bf16[64,2048]{1,0:T(8,128)(2,1)} async-done(((bf16[256,2048]{1,0:T(8,128)(2,1)}), bf16[64,2048]{1,0:T(8,128)(2,1)}) %reduce-scatter.41.cloned.1.call-update) | async-done | bytes 262160 | tf_op jit(solution)/shard_map/reduce_scatter | solution.py:37
  956.8 8.6 collective-permute-done.2
  967.5 15.7 all-gather.41.cloned.1.call-done
  983.2 8.4 convert_reduce_fusion.1
  992.6 6.7 fusion.78
  999.4 25.0 %reduce-scatter.43.cloned.1.call-done = bf16[64,2048]{1,0:T(8,128)(2,1)} async-done(((bf16[256,2048]{1,0:T(8,128)(2,1)}), bf16[64,2048]{1,0:T(8,128)(2,1)}) %reduce-scatter.43.cloned.1.call-update) | async-done | bytes 262160 | tf_op jit(solution)/shard_map/reduce_scatter | solution.py:37
  1033.8 12.8 all-gather.43.cloned.1.call-done
  1068.3 5.8 fusion.60
  1075.1 24.0 %reduce-scatter.45.cloned.1.call-done = bf16[64,2048]{1,0:T(8,128)(2,1)} async-done(((bf16[256,2048]{1,0:T(8,128)(2,1)}), bf16[64,2048]{1,0:T(8,128)(2,1)}) %reduce-scatter.45.cloned.1.call-update) | async-done | bytes 262160 | tf_op jit(solution)/shard_map/reduce_scatter | solution.py:37
  1105.3 8.6 collective-permute-done.3
  1114.7 15.9 all-gather.45.cloned.1.call-done
  1130.6 8.3 convert_reduce_fusion
  1140.0 6.7 fusion.81
  1148.0 23.8 %reduce-scatter.47.cloned.1.call-done = bf16[64,2048]{1,0:T(8,128)(2,1)} async-done(((bf16[256,2048]{1,0:T(8,128)(2,1)}), bf16[64,2048]{1,0:T(8,128)(2,1)}) %reduce-scatter.47.cloned.1.call-update) | async-done | bytes 262160 | tf_op jit(solution)/shard_map/reduce_scatter | solution.py:37
  1179.4 15.3 all-gather.47.cloned.1.call-done
  1209.7 5.7 fusion.57
  1217.5 7.8 fusion.72
  1232.3 8.1 reduce-scatter.49.cloned.1.call-done
  1246.8 5.8 add_convert_fusion.3
  1255.1 6.4 fusion.195
  1261.5 6.3 fusion.193
  1267.8 12.2 add_convert_fusion.2
  1283.3 8.5 fusion.205
  1291.8 8.1 fusion.203
  1300.0 15.8 add_convert_fusion.1
  1322.0 8.2 fusion.200
  1330.2 8.1 fusion.198
  1338.3 15.8 add_convert_fusion
  1359.6 8.6 reduce-scatter.61.cloned.1.call-done
  1369.7 59.0 %reduce-scatter.63.cloned.1.call-done = f32[128,4]{1,0:T(8,128)} async-done(((f32[2048,4]{1,0:T(8,128)}), f32[128,4]{1,0:T(8,128)}) %reduce-scatter.63.cloned.1.call-update) | async-done | bytes 2064
  1430.2 43.6 %reduce-scatter.55.cloned.1.call-done = bf16[512,512]{1,0:T(8,128)(2,1)} async-done(((bf16[512,2048]{1,0:T(8,128)(2,1)}), bf16[512,512]{1,0:T(8,128)(2,1)}) %reduce-scatter.55.cloned.1.call-update) | async-done | bytes 524304 | tf_op jit(solution)/shard_map/reduce_scatter | solution.py:283
  1475.9 110.4 %reduce-scatter.53.cloned.1.call-done = bf16[512,3,512]{2,0,1:T(8,128)(2,1)} async-done(((bf16[2048,3,512]{2,0,1:T(8,128)(2,1)}), bf16[512,3,512]{2,0,1:T(8,128)(2,1)}) %reduce-scatter.53.cloned.1.call-update) | async-done | bytes 1572880 | tf_op jit(solution)/shard_map/reduce_scatter | solution.py:280
  1589.8 144.0 %reduce-scatter.57.cloned.1.call-done = bf16[512,2048]{1,0:T(8,128)(2,1)} async-done(((bf16[2048,2048]{1,0:T(8,128)(2,1)}), bf16[512,2048]{1,0:T(8,128)(2,1)}) %reduce-scatter.57.cloned.1.call-update) | async-done | bytes 2097168 | tf_op jit(solution)/shard_map/reduce_scatter | solution.py:286
  1737.9 143.4 %reduce-scatter.59.cloned.1.call-done = bf16[2048,512]{1,0:T(8,128)(2,1)} async-done(((bf16[2048,2048]{1,0:T(8,128)(2,1)}), bf16[2048,512]{1,0:T(8,128)(2,1)}) %reduce-scatter.59.cloned.1.call-update) | async-done | bytes 2097168 | tf_op jit(solution)/shard_map/reduce_scatter | solution.py:289
  (550 shorter events, 253.7 us)
Async XLA Ops:
  7.2 61.9 %all-gather.27.cloned.1.call-start = ((), (), s32[]{:S(2)}) async-start(), calls=%async_computation.21 | async-start | bytes 1310720 | tf_op jit(solution)/shard_map/all_gather | solution.py:20
  31.8 856.2 %copy-start = (f32[1,2,64,2048]{3,2,1,0:T(8,128)}, f32[1,2,64,2048]{3,2,1,0:T(8,128)S(1)}, u32[]{:S(2)}) copy-start(f32[1,2,64,2048]{3,2,1,0:T(8,128)S(1)} %convert_element_type.478) | copy-start | bytes 3145732
  50.7 16.2 copy-start.120
  51.9 132.2 %all-gather.51.cloned.1.call-start = ((), (), s32[]{:S(2)}) async-start(), calls=%async_computation.49 | async-start | bytes 7864320 | tf_op jit(solution)/shard_map/all_gather | solution.py:217
  52.6 177.2 %all-gather.53.cloned.1.call-start = ((), (), s32[]{:S(2)}) async-start(), calls=%async_computation.50 | async-start | bytes 2621440 | tf_op jit(solution)/shard_map/all_gather | solution.py:218
  53.3 203.5 %reduce-scatter.29.cloned.1.call-start = ((), (), s32[]{:S(2)}) async-start(), calls=%async_computation.22 | async-start | bytes 1310720 | tf_op jit(solution)/shard_map/reduce_scatter | solution.py:24
  66.9 127.3 %copy-start.124 = (f32[4]{0:T(128)}, f32[4]{0:T(128)S(1)}, u32[]{:S(2)}) copy-start(f32[4]{0:T(128)S(1)} %multiply_exponential_fusion) | copy-start | bytes 52
  69.1 125.1 %copy-start.89 = (pred[256,256]{0,1:T(8,128)(4,1)}, pred[256,256]{0,1:T(8,128)(4,1)S(1)}, u32[]{:S(2)}) copy-start(pred[256,256]{0,1:T(8,128)(4,1)S(1)} %fusion.318) | copy-start | bytes 196612
  196.3 36.8 %copy-start.70 = (bf16[4,128,256]{2,1,0:T(8,128)(2,1)}, bf16[4,128,256]{2,1,0:T(8,128)(2,1)S(1)}, u32[]{:S(2)}) copy-start(bf16[4,128,256]{2,1,0:T(8,128)(2,1)S(1)} %convolution_convert_fusion.14) | copy-start | bytes 786436
  233.1 175.1 %all-gather.55.cloned.1.call-start = ((), (), s32[]{:S(2)}) async-start(), calls=%async_computation.51 | async-start | bytes 10485760 | tf_op jit(solution)/shard_map/all_gather | solution.py:219
  233.7 191.4 %all-gather.29.cloned.1.call-start = ((), (), s32[]{:S(2)}) async-start(), calls=%async_computation.23 | async-start | bytes 1310720 | tf_op jit(solution)/shard_map/all_gather | solution.py:20
  258.0 349.2 %copy-start.9 = (f32[64,2048]{1,0:T(8,128)}, f32[64,2048]{1,0:T(8,128)S(1)}, u32[]{:S(2)}) copy-start(f32[64,2048]{1,0:T(8,128)S(1)} %get-tuple-element.64) | copy-start | bytes 1572868
  259.2 317.2 %all-gather.49.cloned.1.call-start = ((), (), s32[]{:S(2)}) async-start(), calls=%async_computation.48 | async-start | bytes 10485760 | tf_op jit(solution)/shard_map/all_gather | solution.py:245
  259.9 347.2 %reduce-scatter.31.cloned.1.call-start = ((), (), s32[]{:S(2)}) async-start(), calls=%async_computation.24 | async-start | bytes 1310720 | tf_op jit(solution)/shard_map/reduce_scatter | solution.py:24
  584.0 52.4 %all-gather.31.cloned.1.call-start = ((), (), s32[]{:S(2)}) async-start(), calls=%async_computation.25 | async-start | bytes 1310720 | tf_op jit(solution)/shard_map/all_gather | solution.py:20
  608.2 8.9 collective-permute-start
  617.3 59.0 %copy-start.8 = (f32[64,2048]{1,0:T(8,128)}, f32[64,2048]{1,0:T(8,128)S(1)}, u32[]{:S(2)}) copy-start(f32[64,2048]{1,0:T(8,128)S(1)} %get-tuple-element.62) | copy-start | bytes 1572868
  618.4 57.8 %reduce-scatter.33.cloned.1.call-start = ((), (), s32[]{:S(2)}) async-start(), calls=%async_computation.26 | async-start | bytes 1310720 | tf_op jit(solution)/shard_map/reduce_scatter | solution.py:24
  651.2 44.2 %all-gather.33.cloned.1.call-start = ((), (), s32[]{:S(2)}) async-start(), calls=%async_computation.27 | async-start | bytes 1310720 | tf_op jit(solution)/shard_map/all_gather | solution.py:20
  677.3 195.2 %copy-start.2 = (f32[64,2048]{1,0:T(8,128)}, f32[64,2048]{1,0:T(8,128)S(1)}, u32[]{:S(2)}) copy-start(f32[64,2048]{1,0:T(8,128)S(1)} %get-tuple-element.60) | copy-start | bytes 1572868
  678.5 56.2 %reduce-scatter.35.cloned.1.call-start = ((), (), s32[]{:S(2)}) async-start(), calls=%async_computation.28 | async-start | bytes 1310720 | tf_op jit(solution)/shard_map/reduce_scatter | solution.py:24
  709.6 54.2 %all-gather.35.cloned.1.call-start = ((), (), s32[]{:S(2)}) async-start(), calls=%async_computation.29 | async-start | bytes 1310720 | tf_op jit(solution)/shard_map/all_gather | solution.py:20
  735.7 8.9 collective-permute-start.1
  744.8 60.7 %copy-start.10 = (f32[64,2048]{1,0:T(8,128)}, f32[64,2048]{1,0:T(8,128)S(1)}, u32[]{:S(2)}) copy-start(f32[64,2048]{1,0:T(8,128)S(1)} %get-tuple-element.58) | copy-start | bytes 1572868
  746.0 59.6 %reduce-scatter.37.cloned.1.call-start = ((), (), s32[]{:S(2)}) async-start(), calls=%async_computation.30 | async-start | bytes 1310720 | tf_op jit(solution)/shard_map/reduce_scatter | solution.py:24
  780.5 44.2 %all-gather.37.cloned.1.call-start = ((), (), s32[]{:S(2)}) async-start(), calls=%async_computation.31 | async-start | bytes 1310720 | tf_op jit(solution)/shard_map/all_gather | solution.py:20
  806.7 24.2 %copy-start.6 = (f32[64,2048]{1,0:T(8,128)}, f32[64,2048]{1,0:T(8,128)S(1)}, u32[]{:S(2)}) copy-start(f32[64,2048]{1,0:T(8,128)S(1)} %get-tuple-element.56) | copy-start | bytes 1572868
  807.8 35.7 %all-gather.25.cloned.1.call-start = ((), (), s32[]{:S(2)}) async-start(), calls=%async_computation.20 | async-start | bytes 1310720 | tf_op jit(solution)/shard_map/all_gather | solution.py:33
  808.6 76.1 %reduce-scatter.39.cloned.1.call-start = ((), (), s32[]{:S(2)}) async-start(), calls=%async_computation.32 | async-start | bytes 1310720 | tf_op jit(solution)/shard_map/reduce_scatter | solution.py:37
  859.7 47.2 %all-gather.39.cloned.1.call-start = ((), (), s32[]{:S(2)}) async-start(), calls=%async_computation.33 | async-start | bytes 1310720 | tf_op jit(solution)/shard_map/all_gather | solution.py:33
  874.1 16.7 copy-start.65
  890.0 61.9 %reduce-scatter.41.cloned.1.call-start = ((), (), s32[]{:S(2)}) async-start(), calls=%async_computation.34 | async-start | bytes 1310720 | tf_op jit(solution)/shard_map/reduce_scatter | solution.py:37
  926.8 56.4 %all-gather.41.cloned.1.call-start = ((), (), s32[]{:S(2)}) async-start(), calls=%async_computation.35 | async-start | bytes 1310720 | tf_op jit(solution)/shard_map/all_gather | solution.py:33
  928.9 38.3 %copy-start.106 = (f32[64]{0:T(128)}, f32[64]{0:T(128)S(1)}, u32[]{:S(2)}) copy-start(f32[64]{0:T(128)S(1)} %broadcast_multiply_fusion.2) | copy-start | bytes 772
  955.5 9.9 collective-permute-start.2
  967.3 57.1 %reduce-scatter.43.cloned.1.call-start = ((), (), s32[]{:S(2)}) async-start(), calls=%async_computation.36 | async-start | bytes 1310720 | tf_op jit(solution)/shard_map/reduce_scatter | solution.py:37
  999.3 47.3 %all-gather.43.cloned.1.call-start = ((), (), s32[]{:S(2)}) async-start(), calls=%async_computation.37 | async-start | bytes 1310720 | tf_op jit(solution)/shard_map/all_gather | solution.py:33
  999.4 28.5 %copy-start.105 = (f32[64]{0:T(128)}, f32[64]{0:T(128)S(1)}, u32[]{:S(2)}) copy-start(f32[64]{0:T(128)S(1)} %broadcast_multiply_fusion.1) | copy-start | bytes 772
  1029.8 69.4 %reduce-scatter.45.cloned.1.call-start = ((), (), s32[]{:S(2)}) async-start(), calls=%async_computation.38 | async-start | bytes 1310720 | tf_op jit(solution)/shard_map/reduce_scatter | solution.py:37
  1074.0 28.9 %copy-start.63 = (bf16[64,2048]{1,0:T(8,128)(2,1)S(1)}, bf16[64,2048]{1,0:T(8,128)(2,1)}, u32[]{:S(2)}) copy-start(bf16[64,2048]{1,0:T(8,128)(2,1)} %reduce-scatter.35.cloned.1.call-done) | copy-start | bytes 786436
  1074.1 56.6 %all-gather.45.cloned.1.call-start = ((), (), s32[]{:S(2)}) async-start(), calls=%async_computation.39 | async-start | bytes 1310720 | tf_op jit(solution)/shard_map/all_gather | solution.py:33
  1104.0 9.9 collective-permute-start.3
  1114.6 57.1 %reduce-scatter.47.cloned.1.call-start = ((), (), s32[]{:S(2)}) async-start(), calls=%async_computation.40 | async-start | bytes 1310720 | tf_op jit(solution)/shard_map/reduce_scatter | solution.py:37
  1146.8 47.9 %all-gather.47.cloned.1.call-start = ((), (), s32[]{:S(2)}) async-start(), calls=%async_computation.41 | async-start | bytes 1310720 | tf_op jit(solution)/shard_map/all_gather | solution.py:33
  1175.6 22.5 %copy-start.115 = (f32[64]{0:T(128)}, f32[64]{0:T(128)S(1)}, u32[]{:S(2)}) copy-start(f32[64]{0:T(128)S(1)} %negate_multiply_fusion.1) | copy-start | bytes 772
  1177.8 62.6 %reduce-scatter.49.cloned.1.call-start = ((), (), s32[]{:S(2)}) async-start(), calls=%async_computation.42 | async-start | bytes 1310720 | tf_op jit(solution)/shard_map/reduce_scatter | solution.py:37
  1179.4 20.8 %copy-start.64 = (bf16[1,256,4,128]{3,2,1,0:T(4,128)(2,1)S(1)}, bf16[1,256,4,128]{3,2,1,0:T(4,128)(2,1)}, u32[]{:S(2)}) copy-start(bf16[1,256,4,128]{3,2,1,0:T(4,128)(2,1)} %get-tuple-element.76) | copy-start | bytes 786436
  1215.4 138.8 %reduce-scatter.67.cloned.1.call-start = ((), (), s32[]{:S(2)}) async-start(), calls=%async_computation.55 | async-start | bytes 40960
  1216.2 139.4 %reduce-scatter.65.cloned.1.call-start = ((), (), s32[]{:S(2)}) async-start(), calls=%async_computation.54 | async-start | bytes 40960
  1217.4 139.7 %reduce-scatter.51.cloned.1.call-start = ((), (), s32[]{:S(2)}) async-start(), calls=%async_computation.43 | async-start | bytes 1310720 | tf_op jit(solution)/shard_map/reduce_scatter | solution.py:24
  1225.3 143.0 %reduce-scatter.61.cloned.1.call-start = ((), (), s32[]{:S(2)}) async-start(), calls=%async_computation.52 | async-start | bytes 1114112
  1225.3 15.1 copy-start.107
  1229.5 14.2 copy-start.95
  1229.5 14.2 copy-start.96
  1229.5 14.2 copy-start.97
  1229.5 14.2 copy-start.98
  1229.5 14.2 copy-start.99
  1232.3 13.0 copy-start.93
  1232.3 13.0 copy-start.94
  1245.2 183.6 %reduce-scatter.63.cloned.1.call-start = ((), (), s32[]{:S(2)}) async-start(), calls=%async_computation.53 | async-start | bytes 1114112
  1246.8 227.0 %reduce-scatter.55.cloned.1.call-start = ((), (), s32[]{:S(2)}) async-start(), calls=%async_computation.45 | async-start | bytes 2621440 | tf_op jit(solution)/shard_map/reduce_scatter | solution.py:283
  1252.7 333.6 %reduce-scatter.53.cloned.1.call-start = ((), (), s32[]{:S(2)}) async-start(), calls=%async_computation.44 | async-start | bytes 7864320 | tf_op jit(solution)/shard_map/reduce_scatter | solution.py:280
  1280.1 453.7 %reduce-scatter.57.cloned.1.call-start = ((), (), s32[]{:S(2)}) async-start(), calls=%async_computation.46 | async-start | bytes 10485760 | tf_op jit(solution)/shard_map/reduce_scatter | solution.py:286
  1315.8 565.6 %reduce-scatter.59.cloned.1.call-start = ((), (), s32[]{:S(2)}) async-start(), calls=%async_computation.47 | async-start | bytes 10485760 | tf_op jit(solution)/shard_map/reduce_scatter | solution.py:289
  (104 other events, 488.9 us)
Sparse Core Ops, SparseCore 0:
  52.0 15.0 all-gather.26
  68.7 115.3 all-gather.50
  185.6 44.1 all-gather.52
  233.2 23.5 reduce-scatter.28
  258.4 149.7 all-gather.54
  410.3 14.7 all-gather.28
  426.7 149.6 all-gather.48
  584.1 23.0 reduce-scatter.30
  618.5 17.7 all-gather.30
  651.3 24.8 reduce-scatter.32
  678.6 16.7 all-gather.32
  709.8 24.8 reduce-scatter.34
  746.1 17.7 all-gather.34
  780.6 24.8 reduce-scatter.36
  808.0 16.7 all-gather.36
  826.8 16.7 all-gather.24
  859.8 24.8 reduce-scatter.38
  890.1 16.7 all-gather.38
  926.9 24.8 reduce-scatter.40
  967.4 15.8 all-gather.40
  999.4 24.8 reduce-scatter.42
  1029.9 16.7 all-gather.42
  1074.2 24.8 reduce-scatter.44
  1114.8 15.8 all-gather.44
  1146.9 24.8 reduce-scatter.46
  1177.9 16.7 all-gather.46
  1215.5 24.8 reduce-scatter.48
  1242.7 18.8 reduce-scatter.66
  1263.9 17.0 reduce-scatter.64
  1284.1 23.0 reduce-scatter.50
  1310.8 57.3 reduce-scatter.60
  1372.3 56.3 reduce-scatter.62
  1430.9 42.8 reduce-scatter.54
  1476.2 110.0 reduce-scatter.52
  1588.8 144.9 reduce-scatter.56
  1736.1 145.1 reduce-scatter.58
where the time goes:
time: 1900 us; the launch traced here: 1890 us
  waiting for transfers between devices  1360 us (72%)
  matrix products  277 us (15%)
  other arithmetic  85.5 us (4%)
  local copies, waits for them, and re-layouts  69.6 us (4%)
  blocking collectives  67.2 us (4%)
  between operations  19.2 us (1%)
    reduce_scatter x1, waiting for transfers between devices, on_device(): lax.psum_scatter(matrix_sums[2].astype(jnp.bfloat16), 'dp', scatter_dimen...  144 us
    all_gather x1, waiting for transfers between devices, on_device(): lax.all_gather(w_down[0], 'dp', axis=1, tiled=True)  144 us
    reduce_scatter x1, waiting for transfers between devices, on_device(): lax.psum_scatter(matrix_sums[3].astype(jnp.bfloat16), 'dp', scatter_dimen...  143 us
    all_gather x1, waiting for transfers between devices, on_device(): lax.all_gather(w_up[0], 'dp', axis=0, tiled=True)  135 us
    reduce_scatter x6, waiting for transfers between devices, collect_rows(): lax.psum_scatter(term_fn(jnp.int32(0), row_number * lax.axis_size('tensor...  121 us
    all_gather x1, waiting for transfers between devices, on_device(): lax.all_gather(w_qkv[0], 'dp', axis=0, tiled=True)  115 us
    reduce_scatter x6, waiting for transfers between devices, collect_grads(): lax.psum_scatter(term_fn(jnp.int32(0), row_number * lax.axis_size('tensor...  114 us
    reduce_scatter x1, waiting for transfers between devices, on_device(): lax.psum_scatter(matrix_sums[0].astype(jnp.bfloat16), 'dp', scatter_dimen...  110 us
  transfers between devices with their start and end apart: 40, of which 36 were waited for; matrix products, arithmetic and copies ran while one was open for 11% of the time, Pallas kernels for 0%

commit v1 on v0

v1 whole, which is shorter than its diff:
```python
import jax
import jax.numpy as jnp
from jax import lax
from jax.sharding import PartitionSpec as P

BF = jnp.bfloat16
F32 = jnp.float32


def hop(block, axis, pairs):
    return lax.ppermute(block, axis, pairs)


def swap(block, axis, distance):
    return lax.ppermute(block, axis, [(i, i ^ distance) for i in range(lax.axis_size(axis))])


def after(value, *others):
    return lax.optimization_barrier((value,) + others)[0]


def dslice(block, start, size, axis):
    return lax.dynamic_slice_in_dim(block, start, size, axis)


def layer_norm(hidden, gain, shift_vec):
    centre = hidden - jnp.mean(hidden, axis=-1, keepdims=True)
    spread = jnp.mean(centre * centre, axis=-1, keepdims=True)
    return centre * lax.rsqrt(spread + 1e-05) * gain + shift_vec


def layer_norm_back(hidden, gain, grad):
    centre = hidden - jnp.mean(hidden, axis=-1, keepdims=True)
    spread = jnp.mean(centre * centre, axis=-1, keepdims=True)
    scale = lax.rsqrt(spread + 1e-05)
    unit = centre * scale
    scaled = grad * gain
    inner = jnp.mean(scaled * unit, axis=-1, keepdims=True)
    back = (scaled - jnp.mean(scaled, axis=-1, keepdims=True) - unit * inner) * scale
    return back, jnp.sum(grad * unit, axis=0), jnp.sum(grad, axis=0)


def spread_rows(rows):
    other = swap(rows, "tensor", 2)
    near = swap(rows, "tensor", 1)
    far = swap(other, "tensor", 1)
    return jnp.concatenate([rows, near, other, far], axis=0)


def collect_rows(terms):
    size = terms.shape[0] // 4
    part = terms.reshape(4, size, -1)
    got = swap(jnp.stack([part[1], part[3]]).astype(BF), "tensor", 1).astype(F32)
    away = swap((part[2] + got[1]).astype(BF), "tensor", 2).astype(F32)
    return part[0] + got[0] + away


def spread_pair(rows):
    size = rows.shape[0]
    half = size // 2
    plane = swap(rows, "dp", 1)
    chip = swap(rows, "tensor", 2)
    corner_a = swap(plane[:half], "tensor", 2)
    corner_b = swap(chip[half:], "dp", 1)
    near = swap(rows, "tensor", 1)
    rest = jnp.concatenate([chip, plane, corner_a, corner_b], axis=0)
    far = swap(rest, "tensor", 1)
    return jnp.concatenate([rows, rest, near, far], axis=0)


def collect_pair(terms):
    size = terms.shape[0] // 8
    half = size // 2
    got = swap(terms[4 * size :].astype(BF), "tensor", 1).astype(F32)
    total = terms[: 4 * size] + got
    own, chip, plane, corner = (total[i * size : (i + 1) * size] for i in range(4))
    one = swap(corner[:half].astype(BF), "tensor", 2).astype(F32)
    two = swap(corner[half:].astype(BF), "dp", 1).astype(F32)
    plane = jnp.concatenate([plane[:half] + one, plane[half:]], axis=0)
    chip = jnp.concatenate([chip[:half], chip[half:] + two], axis=0)
    return own + swap(chip.astype(BF), "tensor", 2).astype(F32) + swap(plane.astype(BF), "dp", 1).astype(F32)


def gather_line(pack, layer, is_layer):
    count = lax.axis_size("dp")
    plane = lax.axis_index("dp")
    half = pack.shape[0] // 2
    away = hop(pack[half:], "section", [(layer, 1 - layer)])
    held = jnp.where(is_layer, pack[:half], away)
    right, left = held, held
    rights, lefts = [], []
    for step in range(1, count):
        right = hop(right, "dp", [(i, i + 1) for i in range(step - 1, count - 1)])
        left = hop(left, "dp", [(i + 1, i) for i in range(count - step)])
        rights.append(right)
        lefts.append(left)
    full = jnp.zeros((count,) + pack.shape, pack.dtype)
    full = lax.dynamic_update_slice(full, pack[None], (plane, 0, 0))
    for step in range(1, count):
        block = rights[step - 1] + lefts[count - step - 1]
        home = hop(block, "section", [(1 - layer, layer)])
        both = jnp.concatenate([block, home], axis=0)
        full = lax.dynamic_update_slice(full, both[None], (lax.rem(plane - step + count, count), 0, 0))
    return full


def gather_pair(own, sends, layer, is_layer):
    count = lax.axis_size("dp")
    plane = lax.axis_index("dp")
    half = own.shape[0] // 2
    full = jnp.zeros((count,) + own.shape, own.dtype)
    full = lax.dynamic_update_slice(full, own[None], (plane, 0, 0))
    for distance in range(1, count):
        block = sends[distance & 1]
        away = hop(block[half:], "section", [(layer, 1 - layer)])
        held = jnp.where(is_layer, block[:half], away)
        got = swap(held, "dp", distance)
        home = hop(got, "section", [(1 - layer, layer)])
        both = jnp.concatenate([got, home], axis=0)
        full = lax.dynamic_update_slice(full, both[None], (plane ^ distance, 0, 0))
    return full


def scatter_line(full, layer, is_layer):
    count = lax.axis_size("dp")
    plane = lax.axis_index("dp")
    half = full.shape[1] // 2

    def block(offset):
        return dslice(full, lax.rem(plane + offset, count), 1, 0)[0]

    own = block(0).astype(F32)
    held = {}
    for offset in range(1, count):
        piece = block(offset)
        away = hop(piece[half:], "section", [(layer, 1 - layer)])
        held[offset] = jnp.where(is_layer, piece[:half], away)
    right = left = None
    for step in range(count - 1):
        to_right, to_left = held[count - 1 - step], held[step + 1]
        if right is not None:
            to_right = (to_right.astype(F32) + right.astype(F32)).astype(BF)
            to_left = (to_left.astype(F32) + left.astype(F32)).astype(BF)
        right = hop(to_right, "dp", [(i, i + 1) for i in range(step + 1)])
        left = hop(to_left, "dp", [(i, i - 1) for i in range(count - 1, count - 2 - step, -1)])
    total = right.astype(F32) + left.astype(F32)
    home = hop(total.astype(BF), "section", [(1 - layer, layer)]).astype(F32)
    return own + jnp.concatenate([total, home], axis=0)


def scatter_pair(full, layer, is_layer):
    count = lax.axis_size("dp")
    plane = lax.axis_index("dp")
    half = full.shape[1] // 2
    sums = [None, None]
    for distance in range(1, count):
        piece = dslice(full, plane ^ distance, 1, 0)[0]
        away = hop(piece[half:], "section", [(layer, 1 - layer)])
        held = jnp.where(is_layer, piece[:half], away)
        got = swap(held, "dp", distance).astype(F32)
        odd = distance & 1
        sums[odd] = got if sums[odd] is None else sums[odd] + got
    own = dslice(full, plane, 1, 0)[0].astype(F32)
    results = []
    for part in sums:
        home = hop(part.astype(BF), "section", [(1 - layer, layer)]).astype(F32)
        results.append(jnp.concatenate([part, home], axis=0))
    return own + results[0], results[1]


def score_block(queries, keys, length, slopes, positions):
    raw = jnp.einsum("qhe,khe->hqk", queries, keys, preferred_element_type=F32)
    offsets = (positions[:, None] - positions[None, :]).astype(F32)
    allowed = (positions[None, :] <= positions[:, None]) | (positions[None, :] < length)
    scores = raw * queries.shape[2] ** (-0.5) - slopes[:, None, None] * offsets
    return jnp.where(allowed, scores, -1e30)


def attend(proj, qv_bias, length, slopes, positions):
    heads, size = qv_bias.shape[1:]
    seq_len = proj.shape[0]
    flat = qv_bias.astype(F32).reshape(2, heads * size)
    wide = heads * size
    queries = (proj[:, :wide] + flat[0]).astype(BF).reshape(seq_len, heads, size)
    keys = proj[:, wide : 2 * wide].astype(BF).reshape(seq_len, heads, size)
    values = (proj[:, 2 * wide :] + flat[1]).astype(BF).reshape(seq_len, heads, size)
    scores = score_block(queries, keys, length, slopes, positions)
    peak = jnp.max(scores, axis=-1, keepdims=True)
    expon = jnp.exp(scores - peak)
    total = jnp.sum(expon, axis=-1, keepdims=True)
    probs = (expon / total).astype(BF)
    mixed = jnp.einsum("hqk,khe->qhe", probs, values, preferred_element_type=F32)
    mixed = mixed.astype(BF).reshape(seq_len, wide)
    return mixed, (queries, keys, values, (peak + jnp.log(total))[..., 0])


def attend_back(grad_mixed, kept, length, slopes, positions):
    queries, keys, values, log_total = kept
    seq_len, heads, size = queries.shape
    grad_heads = grad_mixed.reshape(seq_len, heads, size)
    scores = score_block(queries, keys, length, slopes, positions)
    probs = jnp.exp(scores - log_total[..., None])
    grad_probs = jnp.einsum("qhe,khe->hqk", grad_heads, values, preferred_element_type=F32)
    inner = jnp.sum(probs * grad_probs, axis=-1, keepdims=True)
    grad_raw = (probs * (grad_probs - inner) * size ** (-0.5)).astype(BF)
    grad_q = jnp.einsum("hqk,khe->qhe", grad_raw, keys, preferred_element_type=F32).astype(BF)
    grad_k = jnp.einsum("hqk,qhe->khe", grad_raw, queries, preferred_element_type=F32).astype(BF)
    grad_v = jnp.einsum(
        "hqk,qhe->khe", probs.astype(BF), grad_heads, preferred_element_type=F32
    ).astype(BF)
    return jnp.concatenate([g.reshape(seq_len, heads * size) for g in (grad_q, grad_k, grad_v)], axis=1)


def forward(hidden, lengths, weights, gains, shifts, qv_bias, up_bias, slopes, positions):
    w_qkv, w_out, w_up, w_down = weights
    normed, heads, mixed_all, middle, second = [], [], [], [], []
    for seq, rows in enumerate(hidden):
        full = spread_rows(layer_norm(rows, gains[0], shifts[0]).astype(BF))
        proj = jnp.dot(full, w_qkv, preferred_element_type=F32)
        mixed, kept = attend(proj, qv_bias, lengths[seq], slopes, positions)
        branch = jnp.einsum("tf,zfd->tzd", mixed, w_out, preferred_element_type=F32)
        mid = rows + collect_rows(branch.reshape(full.shape)) + shifts[2]
        normed.append(full)
        heads.append(kept)
        mixed_all.append(mixed)
        middle.append(mid)
        second.append(layer_norm(mid, gains[1], shifts[1]).astype(BF))
    second = spread_pair(jnp.concatenate(second, axis=0))
    up = jnp.dot(second, w_up, preferred_element_type=F32) + up_bias
    act = jax.nn.gelu(up, approximate=True).astype(BF)
    branch = jnp.einsum("tf,zfd->tzd", act, w_down, preferred_element_type=F32)
    branch = collect_pair(branch.reshape(second.shape))
    output = jnp.concatenate(middle, axis=0) + branch + shifts[3]
    return output, (hidden, normed, heads, mixed_all, middle, second, up, act)


def backward(grad_out, grad_pair, kept, lengths, weights, gains, slopes, positions, planes):
    hidden, normed, heads, mixed_all, middle, second, up, act = kept
    w_qkv, w_out, w_up, w_down = weights
    width = grad_out.shape[1]
    part = width // planes
    rows = hidden[0].shape[0]
    grad_down_bias = jnp.sum(grad_out, axis=0)
    blocks = grad_pair.reshape(-1, planes, part)
    grad_act = jnp.einsum("tzd,zfd->tf", blocks, w_down, preferred_element_type=F32)
    unused, pull = jax.vjp(lambda v: jax.nn.gelu(v, approximate=True), up)
    grad_up = pull(grad_act)[0].astype(BF)
    grad_second = jnp.einsum("tf,df->td", grad_up, w_up, preferred_element_type=F32)
    grad_w_down = jnp.einsum("tf,tzd->zfd", act, blocks, preferred_element_type=F32).astype(BF)
    grad_w_up = jnp.einsum("td,tf->df", second, grad_up, preferred_element_type=F32).astype(BF)
    grad_up_bias = jnp.sum(grad_up.astype(F32), axis=0)
    grad_second = collect_pair(grad_second)
    back, gain_two, shift_two = layer_norm_back(jnp.concatenate(middle, axis=0), gains[1], grad_second)
    grad_middle = grad_out + back
    grad_out_bias = jnp.sum(grad_middle, axis=0)
    grad_proj_all, grad_mid_all, grad_normed = [], [], []
    for seq in range(len(hidden)):
        full = spread_rows(grad_middle[seq * rows : (seq + 1) * rows].astype(BF))
        mid = full.reshape(-1, planes, part)
        grad_mixed = jnp.einsum("tzd,zfd->tf", mid, w_out, preferred_element_type=F32).astype(BF)
        grad_proj = attend_back(grad_mixed, heads[seq], lengths[seq], slopes, positions)
        term = jnp.einsum("tf,df->td", grad_proj, w_qkv, preferred_element_type=F32)
        grad_normed.append(collect_rows(term))
        grad_proj_all.append(grad_proj)
        grad_mid_all.append(mid)
    grad_proj = jnp.concatenate(grad_proj_all, axis=0)
    grad_w_out = jnp.einsum(
        "tf,tzd->zfd",
        jnp.concatenate(mixed_all, axis=0),
        jnp.concatenate(grad_mid_all, axis=0),
        preferred_element_type=F32,
    ).astype(BF)
    grad_w_qkv = jnp.einsum(
        "td,tf->df", jnp.concatenate(normed, axis=0), grad_proj, preferred_element_type=F32
    ).astype(BF)
    proj_sums = jnp.sum(grad_proj.astype(F32), axis=0)
    back, gain_one, shift_one = layer_norm_back(
        jnp.concatenate(hidden, axis=0), gains[0], jnp.concatenate(grad_normed, axis=0)
    )
    vectors = jnp.stack([gain_one, gain_two, shift_one, shift_two, grad_out_bias, grad_down_bias])
    return (
        grad_middle + back,
        (grad_w_qkv, grad_w_out, grad_w_up, grad_w_down),
        (vectors, proj_sums, grad_up_bias),
    )


def on_device(activations, ln_gains, biases, w_qkv, qv_bias, w_out, w_up, up_bias, w_down, prefix):
    is_first = lax.axis_index("section") == 0
    plane = lax.axis_index("dp")
    place = lax.axis_index("tensor")
    planes = lax.axis_size("dp")
    tensors = lax.axis_size("tensor")
    odd = plane % 2 == 1
    seqs, rows, width = activations.shape[1:]
    heads, size_part = qv_bias.shape[2:]
    size = size_part * planes
    wide = heads * size
    deep = w_qkv.shape[1]
    units = w_up.shape[2]
    half = units // 2
    own = activations[0]

    flat = jnp.concatenate([v.reshape(-1) for v in (ln_gains, biases, qv_bias, up_bias)])
    everyone = lax.all_gather(flat, ("dp", "tensor"), axis=0)
    lane = width // (planes * tensors)
    cut = 6 * lane
    features = everyone[:, :cut].reshape(-1, 6, lane).swapaxes(0, 1).reshape(6, width).astype(F32)
    gains, shifts = features[:2], features[2:]
    mine = everyone.reshape(planes, tensors, -1)
    mine = lax.dynamic_index_in_dim(mine, place, 1, keepdims=False)[:, cut:]
    qv_full = mine[:, : 2 * heads * size_part].reshape(planes, 2, heads, size_part)
    qv_full = qv_full.transpose(1, 2, 0, 3).reshape(2, heads, size)
    up_full = mine[:, 2 * heads * size_part :].reshape(planes, up_bias.shape[1], up_bias.shape[2])
    up_full = up_full.transpose(1, 0, 2).reshape(units).astype(F32)
    up_own = jnp.where(odd, up_full[half:], up_full[:half])

    head_ids = place * heads + jnp.arange(heads)
    slopes = jnp.exp2(-8.0 * (head_ids.astype(F32) + 1.0) / (heads * tensors))
    positions = jnp.concatenate([(place ^ j) * rows + jnp.arange(rows) for j in range(tensors)])

    pack = jnp.concatenate([w_qkv[0].reshape(deep, 3 * wide), w_out[0].reshape(deep, wide)], axis=1)
    up_parts = (w_up[0][:, :half], w_up[0][:, half:])
    down_parts = (w_down[0][:half], w_down[0][half:])
    up_keep = jnp.where(odd, up_parts[1], up_parts[0])
    up_send = jnp.where(odd, up_parts[0], up_parts[1])
    down_keep = jnp.where(odd, down_parts[1], down_parts[0])
    down_send = jnp.where(odd, down_parts[0], down_parts[1])

    def gather(layer, pack, up_keep, up_send, down_keep, down_send):
        is_layer = is_first if layer == 0 else ~is_first
        line = gather_line(pack, layer, is_layer)
        up = gather_pair(up_keep, (up_keep, up_send), layer, is_layer)
        down = gather_pair(down_keep, (down_keep, down_send), layer, is_layer)
        full_out = line[:, :, 3 * wide :].reshape(planes, wide, deep)
        return (
            line[:, :, : 3 * wide].reshape(planes * deep, 3 * wide),
            full_out,
            up.reshape(planes * deep, half),
            down,
        )

    shards = (pack, up_keep, up_send, down_keep, down_send)
    first_weights = gather(0, *shards)
    shards = lax.optimization_barrier((shards, first_weights[3]))[0]
    second_weights = gather(1, *shards)

    common = (gains, shifts, qv_full, up_own, slopes, positions)
    source = [own[s].astype(F32) for s in range(seqs)]
    grad_top = own.reshape(seqs * rows, width)
    grad_top_pair = spread_pair(grad_top)
    output, kept_first = forward(source, prefix, first_weights, *common)
    carried = hop(output.astype(BF), "section", [(0, 1)]).astype(F32)
    source = [carried[s * rows : (s + 1) * rows] for s in range(seqs)]
    output, kept_second = forward(source, prefix, second_weights, *common)

    back_common = (gains, slopes, positions, planes)
    grad_mid, grads_top, sums_top = backward(
        grad_top.astype(F32), grad_top_pair, kept_second, prefix, second_weights, *back_common
    )

    def scatter(layer, grads):
        is_layer = is_first if layer == 0 else ~is_first
        g_qkv, g_out, g_up, g_down = grads
        down = scatter_pair(g_down, layer, is_layer)
        up = scatter_pair(g_up.reshape(planes, deep, half), layer, is_layer)
        line = jnp.concatenate(
            [g_qkv.reshape(planes, deep, 3 * wide), g_out.reshape(planes, deep, wide)], axis=2
        )
        line = scatter_line(line, layer, is_layer)
        return line, up, down

    scattered_top = scatter(1, grads_top)
    returned = hop(grad_mid.astype(BF), "section", [(1, 0)])
    grad_low, grads_low, sums_low = backward(
        returned.astype(F32), spread_pair(returned), kept_first, prefix, first_weights, *back_common
    )
    scattered_low = scatter(0, grads_low)

    line, up, down = jax.tree.map(lambda a, b: jnp.where(is_first, a, b), scattered_low, scattered_top)
    vectors, proj_sums, up_sums = jax.tree.map(lambda a, b: jnp.where(is_first, a, b), sums_low, sums_top)
    up_grad = jnp.where(odd, jnp.concatenate([up[1], up[0]], axis=1), jnp.concatenate(up, axis=1))
    down_grad = jnp.where(odd, jnp.concatenate([down[1], down[0]], axis=0), jnp.concatenate(down, axis=0))

    vec = vectors.reshape(6, planes * tensors, lane).swapaxes(0, 1).reshape(planes * tensors, cut)
    qv_sums = jnp.stack([proj_sums[:wide], proj_sums[2 * wide :]]).reshape(2, heads, planes, size_part)
    qv_sums = qv_sums.transpose(2, 0, 1, 3).reshape(planes, -1)
    zero = jnp.zeros_like(up_sums)
    up_sums = jnp.where(odd, jnp.concatenate([zero, up_sums]), jnp.concatenate([up_sums, zero]))
    up_sums = up_sums.reshape(up_bias.shape[1], planes, up_bias.shape[2]).transpose(1, 0, 2).reshape(planes, -1)
    own_part = jnp.concatenate([qv_sums, up_sums], axis=1)[:, None, :]
    own_part = jnp.where((jnp.arange(tensors) == place)[None, :, None], own_part, 0.0)
    message = jnp.concatenate([vec, own_part.reshape(planes * tensors, -1)], axis=1)
    small = lax.psum_scatter(message, ("dp", "tensor"), scatter_dimension=0, tiled=False)
    mid = cut + 2 * heads * size_part

    ends = jnp.where(is_first, grad_low, output).reshape(seqs, rows, width)
    return (
        ends[None],
        small[: 2 * lane].reshape(1, 2, lane),
        small[2 * lane : cut].reshape(1, 4, lane),
        line[:, : 3 * wide].reshape(1, deep, 3, wide),
        small[cut:mid].reshape(1, 2, heads, size_part),
        line[:, 3 * wide :].reshape(1, wide, deep),
        up_grad[None],
        small[mid:].reshape(1, up_bias.shape[1], up_bias.shape[2]),
        down_grad[None],
    )


def solution(mesh):
    in_specs = (
        P("section", "dp", "tensor", None),
        P("section", None, ("dp", "tensor")),
        P("section", None, ("dp", "tensor")),
        P("section", "dp", None, "tensor"),
        P("section", None, "tensor", "dp"),
        P("section", "tensor", "dp"),
        P("section", "dp", "tensor"),
        P("section", "tensor", "dp"),
        P("section", "tensor", "dp"),
        P("dp"),
    )
    out_specs = (
        P("section", "dp", "tensor", None),
        P("section", None, ("dp", "tensor")),
        P("section", None, ("dp", "tensor")),
        P("section", "dp", None, "tensor"),
        P("section", None, "tensor", "dp"),
        P("section", "tensor", "dp"),
        P("section", "dp", "tensor"),
        P("section", "tensor", "dp"),
        P("section", "tensor", "dp"),
    )
    return jax.shard_map(
        on_device, mesh=mesh, in_specs=in_specs, out_specs=out_specs, check_vma=False
    )
```

time: 1900 us -> 1720 us (0.905)
  waiting for transfers between devices: 1360 us -> 668 us
  starting transfers between devices: 12.7 us -> 370 us
  local copies, waits for them, and re-layouts: 69.6 us -> 209 us
  other arithmetic: 85.5 us -> 207 us
  matrix products: 277 us -> 211 us
  blocking collectives: 67.2 us -> 23.4 us
    reduce_scatter x16 -> x0, waiting for transfers between devices: 677 us -> none  [the longest x1 144 us: on_device(): lax.psum_scatter(matrix_sums[2].astype(jnp.bfloat16), 'dp', scatter_dimen...]
    all_gather x16 -> x0, waiting for transfers between devices: 585 us -> none  [the longest x1 144 us: on_device(): lax.all_gather(w_down[0], 'dp', axis=1, tiled=True)]
    ppermute x4 -> x190, waiting for transfers between devices: 28.3 us -> 587 us  [the longest x82 393 us: hop(): return lax.ppermute(block, axis, pairs)]
    ppermute x4 -> x190, starting transfers between devices: 9.33 us -> 370 us  [the longest x82 232 us: hop(): return lax.ppermute(block, axis, pairs)]
    slice x10 -> x86, local copies, waits for them, and re-layouts: 4.52 us -> 75.3 us  [the longest x4 15.7 us: collect_pair(): total = terms[:4 * size] + got]
    dot_general x57 -> x56, matrix products: 277 us -> 211 us  [the longest x4 22.8 us: backward(): term = jnp.einsum('tf,df->td', grad_proj, w_qkv, preferred_element_type=F32)]
    select_n x0 -> x33, other arithmetic: none -> 46.1 us  [the longest x6 9.09 us: on_device(): jnp.where(is_first, a, b)]
    all_gather x4 -> x1, blocking collectives: 67.2 us -> 23.4 us  [on_device(): everyone = lax.all_gather(flat, ('dp', 'tensor'), axis=0)]
  transfers between devices with their start and end apart: 40 -> 191, of which waited for: 36 -> 71; matrix products, arithmetic and copies ran while one was open for 11% -> 30% of each run, Pallas kernels for 0% -> 0%
where the time goes in v1:
time: 1720 us; the launch traced here: 1710 us
  waiting for transfers between devices  668 us (39%)
  starting transfers between devices  370 us (22%)
  matrix products  211 us (12%)
  local copies, waits for them, and re-layouts  209 us (12%)
  other arithmetic  207 us (12%)
  blocking collectives  23.4 us (1%)
  between operations  19.1 us (1%)
    ppermute x82, waiting for transfers between devices, hop(): return lax.ppermute(block, axis, pairs)  393 us
    ppermute x82, starting transfers between devices, hop(): return lax.ppermute(block, axis, pairs)  232 us
    ppermute x108, waiting for transfers between devices, swap(): lax.ppermute(block, axis, [(i, i ^ distance) for i in range(lax.axis_size...  194 us
    ppermute x108, starting transfers between devices, swap(): lax.ppermute(block, axis, [(i, i ^ distance) for i in range(lax.axis_size...  138 us
    unnamed x2, waiting for transfers between devices  80.8 us
    unnamed x460, local copies, waits for them, and re-layouts  54.8 us
  transfers between devices with their start and end apart: 191, of which 71 were waited for; matrix products, arithmetic and copies ran while one was open for 30% of the time, Pallas kernels for 0%

profile of v1, /device:TPU:0, one launch (start us, length us, event | category | flops | bytes accessed | tf_op | source)
XLA Modules:
  0.0 1707.5 jit_solution(355810218183458713)
XLA Ops:
  9.5 23.4 %all-gather.1 = bf16[16,1,1536]{2,1,0:T(2,128)(2,1)S(1)} all-gather(bf16[1,1,1536]{2,1,0:T(2,128)(2,1)S(1)} %reshape.1052), channel_id=2, replica_groups=mesh['section'=2,'dp'=4,'tensor'=4] {'dp','tensor'}, dimensions={0}, use_global_device_ids=true | all-gather | bytes 52224 | tf_op jit(solution)/shard_map/all_gather | solution.py:305
  64.5 17.3 %collective-permute-done.25 = bf16[256,2048]{1,0:T(8,128)(2,1)} collective-permute-done((bf16[256,2048]{1,0:T(8,128)(2,1)}, bf16[256,2048]{1,0:T(8,128)(2,1)}, u32[]{:S(2)}, u32[]{:S(2)}) %collective-permute-start.25) | collective-permute-done | bytes 1048608 | tf_op jit(solution)/shard_map/ppermute | solution.py:11
  98.2 12.5 collective-permute-done.27
  125.4 11.0 collective-permute-done.28
  163.0 7.5 collective-permute-done.48
  214.3 14.5 collective-permute-done.32
  232.0 17.6 %collective-permute-done.34 = bf16[256,2048]{1,0:T(8,128)(2,1)} collective-permute-done((bf16[256,2048]{1,0:T(8,128)(2,1)}, bf16[256,2048]{1,0:T(8,128)(2,1)}, u32[]{:S(2)}, u32[]{:S(2)}) %collective-permute-start.34) | collective-permute-done | bytes 1048608 | tf_op jit(solution)/shard_map/ppermute | solution.py:11
  310.5 11.3 collective-permute-done.49
  325.2 6.8 collective-permute-done.43
  335.5 11.8 collective-permute-done.52
  363.4 10.2 collective-permute-done.55
  378.8 6.3 fusion.455
  421.5 13.6 collective-permute-done.66
  459.1 9.3 collective-permute-done.68
  475.0 10.2 collective-permute-done.91
  487.4 14.2 collective-permute-done.69
  514.5 9.1 collective-permute-done.14
  546.4 14.7 collective-permute-done.72
  571.5 12.6 collective-permute-done.74
  628.9 7.8 collective-permute-done.90
  637.4 9.8 collective-permute-done.93
  650.2 23.9 %collective-permute-done.18 = bf16[512,512]{0,1:T(8,128)(2,1)S(1)} collective-permute-done((bf16[512,512]{0,1:T(8,128)(2,1)S(1)}, bf16[512,512]{0,1:T(8,128)(2,1)S(1)}, u32[]{:S(2)}, u32[]{:S(2)}) %collective-permute-start.18) | collective-permute-done | bytes 524320 | tf_op jit(solution)/shard_map/ppermute | solution.py:15
  690.2 20.5 %collective-permute-done.16 = bf16[512,512]{0,1:T(8,128)(2,1)S(1)} collective-permute-done((bf16[512,512]{0,1:T(8,128)(2,1)S(1)}, bf16[512,512]{0,1:T(8,128)(2,1)S(1)}, u32[]{:S(2)}, u32[]{:S(2)}) %collective-permute-start.16) | collective-permute-done | bytes 524320 | tf_op jit(solution)/shard_map/ppermute | solution.py:11
  713.0 7.4 collective-permute-done.21
  736.8 6.5 fusion.456
  743.3 11.0 convert_reduce_fusion
  788.9 6.7 fusion.57
  809.1 10.4 collective-permute-done.171
  829.3 6.7 collective-permute-done.164
  836.1 11.6 collective-permute-done.166
  903.6 10.5 collective-permute-done.105
  921.7 6.7 convolution_convert_fusion.4
  940.7 7.8 collective-permute-done.113
  950.8 10.6 convolution_convert_fusion
  972.7 6.7 copy.484
  979.4 8.3 convolution_convert_fusion.5
  987.8 7.3 convert_reduce_fusion.1
  1000.0 8.6 fusion.458
  1017.3 6.7 collective-permute-start.158
  1030.2 5.7 collective-permute-done.158
  1040.3 6.8 collective-permute-done.160
  1051.5 6.8 collective-permute-done.168
  1070.3 10.5 collective-permute-done.176
  1083.0 7.7 collective-permute-done.184
  1097.5 33.8 %collective-permute-start.185 = (bf16[512,512]{0,1:T(8,128)(2,1)S(1)}, bf16[512,512]{0,1:T(8,128)(2,1)S(1)}, u32[]{:S(2)}, u32[]{:S(2)}) collective-permute-start(bf16[512,512]{0,1:T(8,128)(2,1)S(1)} %fusion.242), channel_id=1, source_target_pairs={{0,8},{4,12},{8,0},{12,4},{1,9},{5,13},{9,1},{13,5},{2,10},{6,14},... | collective-permute-start | bytes 1572872 | tf_op jit(solution)/shard_map/ppermute | solution.py:15
  1140.6 14.3 collective-permute-done.159
  1156.3 13.6 collective-permute-done.161
  1169.9 24.1 %collective-permute-start.119 = (bf16[64,2048]{1,0:T(8,128)(2,1)S(1)}, bf16[64,2048]{1,0:T(8,128)(2,1)S(1)}, u32[]{:S(2)}, u32[]{:S(2)}) collective-permute-start(bf16[64,2048]{1,0:T(8,128)(2,1)S(1)} %get-tuple-element.172), channel_id=1, source_target_pairs={{0,4},{4,0},{8,12},{12,8},{1,5},{5,1},{9,13},{13,9},{2,6},{6,2},{1... | collective-permute-start | bytes 786440 | tf_op jit(solution)/shard_map/ppermute | solution.py:15
  1211.2 27.6 %collective-permute-done.172 = bf16[256,1024]{1,0:T(8,128)(2,1)} collective-permute-done((bf16[256,1024]{1,0:T(8,128)(2,1)S(1)}, bf16[256,1024]{1,0:T(8,128)(2,1)}, u32[]{:S(2)}, u32[]{:S(2)}) %collective-permute-start.172) | collective-permute-done | bytes 524320 | tf_op jit(solution)/shard_map/ppermute | solution.py:15
  1310.7 6.6 fusion.454
  1317.4 7.4 convert_reduce_fusion.2
  1324.8 10.9 convolution_convert_fusion.1
  1353.2 7.4 collective-permute-start.140
  1365.2 6.6 fusion.453
  1391.2 6.5 collective-permute-done.149
  1399.0 6.6 collective-permute-done.151
  1417.2 10.8 collective-permute-done.141
  1434.6 15.8 collective-permute-done.152
  1454.5 16.7 collective-permute-done.142
  1486.5 24.9 %collective-permute-start.143 = (bf16[256,2048]{1,0:T(8,128)(2,1)}, bf16[256,2048]{1,0:T(8,128)(2,1)}, u32[]{:S(2)}, u32[]{:S(2)}) collective-permute-start(bf16[256,2048]{1,0:T(8,128)(2,1)} %get-tuple-element.83), channel_id=1, source_target_pairs={{0,4},{4,8},{8,12},{1,5},{5,9},{9,13},{2,6},{6,10},{10,14},{3,7},{... | collective-permute-start | bytes 3145736 | tf_op jit(solution)/shard_map/ppermute | solution.py:11
  1514.0 22.0 %collective-permute-start.156 = (bf16[256,2048]{1,0:T(8,128)(2,1)}, bf16[256,2048]{1,0:T(8,128)(2,1)}, u32[]{:S(2)}, u32[]{:S(2)}) collective-permute-start(bf16[256,2048]{1,0:T(8,128)(2,1)} %add_convert_fusion), channel_id=1, source_target_pairs={{12,8},{8,4},{4,0},{13,9},{9,5},{5,1},{14,10},{10,6},{6,2},{15,11}... | collective-permute-start | bytes 3145736 | tf_op jit(solution)/shard_map/ppermute | solution.py:11
  1544.2 18.6 %collective-permute-done.156 = bf16[256,2048]{1,0:T(8,128)(2,1)} collective-permute-done((bf16[256,2048]{1,0:T(8,128)(2,1)}, bf16[256,2048]{1,0:T(8,128)(2,1)}, u32[]{:S(2)}, u32[]{:S(2)}) %collective-permute-start.156) | collective-permute-done | bytes 1048608 | tf_op jit(solution)/shard_map/ppermute | solution.py:11
  1570.7 14.6 collective-permute-done.146
  1599.6 80.8 %all-reduce.5.cloned.1.call-done = f32[16,1536]{1,0:T(8,128)} async-done(((f32[16,1536]{1,0:T(8,128)}), f32[16,1536]{1,0:T(8,128)}) %all-reduce.5.cloned.1.call-update) | async-done | bytes 98320
  (1247 shorter events, 851.7 us)
Async XLA Ops:
  7.2 1673.3 %all-reduce.5.cloned.1.call-start = ((), (), s32[]{:S(2)}) async-start(), calls=%async_computation | async-start | bytes 196608
  37.4 104.5 %collective-permute-start.22 = (bf16[64,2048]{1,0:T(8,128)(2,1)}, bf16[64,2048]{1,0:T(8,128)(2,1)}, u32[]{:S(2)}, u32[]{:S(2)}) collective-permute-start(bf16[64,2048]{1,0:T(8,128)(2,1)} %get-tuple-element.88), channel_id=1, source_target_pairs={{0,1},{1,0},{2,3},{3,2},{4,5},{5,4},{6,7},{7,6},{8,9},{9,8},{10,11... | collective-permute-start | bytes 786440 | tf_op jit(solution)/shard_map/ppermute | solution.py:15
  37.8 110.6 %collective-permute-start.23 = (bf16[64,2048]{1,0:T(8,128)(2,1)}, bf16[64,2048]{1,0:T(8,128)(2,1)}, u32[]{:S(2)}, u32[]{:S(2)}) collective-permute-start(bf16[64,2048]{1,0:T(8,128)(2,1)} %get-tuple-element.88), channel_id=1, source_target_pairs={{0,2},{1,3},{2,0},{3,1},{4,6},{5,7},{6,4},{7,5},{8,10},{9,11},{10,... | collective-permute-start | bytes 786440 | tf_op jit(solution)/shard_map/ppermute | solution.py:15
  44.2 107.2 %collective-permute-start.6 = (bf16[512,512]{0,1:T(8,128)(2,1)}, bf16[512,512]{0,1:T(8,128)(2,1)}, u32[]{:S(2)}, u32[]{:S(2)}) collective-permute-start(bf16[512,512]{0,1:T(8,128)(2,1)} %slice_bitcast_fusion.51), channel_id=1, source_target_pairs={{0,16},{1,17},{2,18},{3,19},{4,20},{5,21},{6,22},{7,23},{8,24},{9,... | collective-permute-start | bytes 1572872 | tf_op jit(solution)/shard_map/ppermute | solution.py:11
  122.9 37.5 %collective-permute-start.31 = (bf16[256,2048]{1,0:T(8,128)(2,1)}, bf16[256,2048]{1,0:T(8,128)(2,1)}, u32[]{:S(2)}, u32[]{:S(2)}) collective-permute-start(bf16[256,2048]{1,0:T(8,128)(2,1)} %collective-permute-done.26), channel_id=1, source_target_pairs={{4,8},{8,12},{5,9},{9,13},{6,10},{10,14},{7,11},{11,15},{20,24},{2... | collective-permute-start | bytes 3145736 | tf_op jit(solution)/shard_map/ppermute | solution.py:11
  136.4 37.7 %collective-permute-start.29 = (bf16[256,2048]{1,0:T(8,128)(2,1)}, bf16[256,2048]{1,0:T(8,128)(2,1)}, u32[]{:S(2)}, u32[]{:S(2)}) collective-permute-start(bf16[256,2048]{1,0:T(8,128)(2,1)} %collective-permute-done.28), channel_id=1, source_target_pairs={{4,0},{5,1},{6,2},{7,3},{20,16},{21,17},{22,18},{23,19}} | collective-permute-start | bytes 3145736 | tf_op jit(solution)/shard_map/ppermute | solution.py:11
  160.4 37.4 %collective-permute-start.33 = (bf16[256,2048]{1,0:T(8,128)(2,1)}, bf16[256,2048]{1,0:T(8,128)(2,1)}, u32[]{:S(2)}, u32[]{:S(2)}) collective-permute-start(bf16[256,2048]{1,0:T(8,128)(2,1)} %collective-permute-done.31), channel_id=1, source_target_pairs={{8,12},{9,13},{10,14},{11,15},{24,28},{25,29},{26,30},{27,31}} | collective-permute-start | bytes 3145736 | tf_op jit(solution)/shard_map/ppermute | solution.py:11
  183.3 45.5 %collective-permute-start.32 = (bf16[256,2048]{1,0:T(8,128)(2,1)}, bf16[256,2048]{1,0:T(8,128)(2,1)}, u32[]{:S(2)}, u32[]{:S(2)}) collective-permute-start(bf16[256,2048]{1,0:T(8,128)(2,1)} %add.730), channel_id=1, source_target_pairs={{16,0},{17,1},{18,2},{19,3},{20,4},{21,5},{22,6},{23,7},{24,8},{25... | collective-permute-start | bytes 3145736 | tf_op jit(solution)/shard_map/ppermute | solution.py:11
  188.4 110.6 %collective-permute-start.7 = (bf16[512,512]{0,1:T(8,128)(2,1)}, bf16[512,512]{0,1:T(8,128)(2,1)}, u32[]{:S(2)}, u32[]{:S(2)}) collective-permute-start(bf16[512,512]{0,1:T(8,128)(2,1)} %fusion.310), channel_id=1, source_target_pairs={{0,4},{4,0},{8,12},{12,8},{1,5},{5,1},{9,13},{13,9},{2,6},{6,2},{1... | collective-permute-start | bytes 1572872 | tf_op jit(solution)/shard_map/ppermute | solution.py:15
  200.7 48.9 %collective-permute-start.34 = (bf16[256,2048]{1,0:T(8,128)(2,1)}, bf16[256,2048]{1,0:T(8,128)(2,1)}, u32[]{:S(2)}, u32[]{:S(2)}) collective-permute-start(bf16[256,2048]{1,0:T(8,128)(2,1)} %add.733), channel_id=1, source_target_pairs={{16,0},{17,1},{18,2},{19,3},{20,4},{21,5},{22,6},{23,7},{24,8},{25... | collective-permute-start | bytes 3145736 | tf_op jit(solution)/shard_map/ppermute | solution.py:11
  203.3 105.8 %collective-permute-start.12 = (bf16[512,512]{0,1:T(8,128)(2,1)}, bf16[512,512]{0,1:T(8,128)(2,1)}, u32[]{:S(2)}, u32[]{:S(2)}) collective-permute-start(bf16[512,512]{0,1:T(8,128)(2,1)} %fusion.310), channel_id=1, source_target_pairs={{0,12},{4,8},{8,4},{12,0},{1,13},{5,9},{9,5},{13,1},{2,14},{6,10},... | collective-permute-start | bytes 1572872 | tf_op jit(solution)/shard_map/ppermute | solution.py:15
  232.0 77.1 %collective-permute-start.10 = (bf16[512,512]{0,1:T(8,128)(2,1)}, bf16[512,512]{0,1:T(8,128)(2,1)}, u32[]{:S(2)}, u32[]{:S(2)}) collective-permute-start(bf16[512,512]{0,1:T(8,128)(2,1)} %fusion.309), channel_id=1, source_target_pairs={{0,8},{4,12},{8,0},{12,4},{1,9},{5,13},{9,1},{13,5},{2,10},{6,14},... | collective-permute-start | bytes 1572872 | tf_op jit(solution)/shard_map/ppermute | solution.py:15
  309.1 38.2 %collective-permute-start.52 = (bf16[256,1024]{1,0:T(8,128)(2,1)S(1)}, bf16[256,1024]{1,0:T(8,128)(2,1)S(1)}, u32[]{:S(2)}, u32[]{:S(2)}) collective-permute-start(bf16[256,1024]{1,0:T(8,128)(2,1)S(1)} %copy-done.122), channel_id=1, source_target_pairs={{0,8},{4,12},{8,0},{12,4},{1,9},{5,13},{9,1},{13,5},{2,10},{6,14},... | collective-permute-start | bytes 1572872 | tf_op jit(solution)/shard_map/ppermute | solution.py:15
  309.1 39.0 %collective-permute-start.11 = (bf16[512,512]{0,1:T(8,128)(2,1)}, bf16[512,512]{0,1:T(8,128)(2,1)S(1)}, u32[]{:S(2)}, u32[]{:S(2)}) collective-permute-start(bf16[512,512]{0,1:T(8,128)(2,1)} %collective-permute-done.10), channel_id=1, source_target_pairs={{16,0},{17,1},{18,2},{19,3},{20,4},{21,5},{22,6},{23,7},{24,8},{25... | collective-permute-start | bytes 1572872 | tf_op jit(solution)/shard_map/ppermute | solution.py:11
  353.0 172.9 %collective-permute-start.5 = (bf16[384,2048]{1,0:T(8,128)(2,1)}, bf16[384,2048]{1,0:T(8,128)(2,1)}, u32[]{:S(2)}, u32[]{:S(2)}) collective-permute-start(bf16[384,2048]{1,0:T(8,128)(2,1)} %pad_maximum_fusion.1), channel_id=1, source_target_pairs={{0,1},{1,0},{2,3},{3,2},{4,5},{5,4},{6,7},{7,6},{8,9},{9,8},{10,11... | collective-permute-start | bytes 4718600 | tf_op jit(solution)/shard_map/ppermute | solution.py:15
  355.0 51.3 %collective-permute-start.65 = (bf16[256,2048]{1,0:T(8,128)(2,1)}, bf16[256,2048]{1,0:T(8,128)(2,1)}, u32[]{:S(2)}, u32[]{:S(2)}) collective-permute-start(bf16[256,2048]{1,0:T(8,128)(2,1)} %slice.1028), channel_id=1, source_target_pairs={{16,0},{17,1},{18,2},{19,3},{20,4},{21,5},{22,6},{23,7},{24,8},{25... | collective-permute-start | bytes 3145736 | tf_op jit(solution)/shard_map/ppermute | solution.py:11
  398.8 50.4 %collective-permute-start.56 = (bf16[512,2048]{1,0:T(8,128)(2,1)}, bf16[512,2048]{1,0:T(8,128)(2,1)}, u32[]{:S(2)}, u32[]{:S(2)}) collective-permute-start(bf16[512,2048]{1,0:T(8,128)(2,1)} %copy.359), channel_id=1, source_target_pairs={{0,1},{1,0},{2,3},{3,2},{4,5},{5,4},{6,7},{7,6},{8,9},{9,8},{10,11... | collective-permute-start | bytes 6291464 | tf_op jit(solution)/shard_map/ppermute | solution.py:15
  402.2 53.6 %collective-permute-start.88 = (bf16[256,1024]{1,0:T(8,128)(2,1)}, bf16[256,1024]{1,0:T(8,128)(2,1)}, u32[]{:S(2)}, u32[]{:S(2)}) collective-permute-start(bf16[256,1024]{1,0:T(8,128)(2,1)} %slice.1057), channel_id=1, source_target_pairs={{16,0},{17,1},{18,2},{19,3},{20,4},{21,5},{22,6},{23,7},{24,8},{25... | collective-permute-start | bytes 1572872 | tf_op jit(solution)/shard_map/ppermute | solution.py:11
  435.0 51.5 %collective-permute-start.71 = (bf16[256,2048]{1,0:T(8,128)(2,1)}, bf16[256,2048]{1,0:T(8,128)(2,1)}, u32[]{:S(2)}, u32[]{:S(2)}) collective-permute-start(bf16[256,2048]{1,0:T(8,128)(2,1)} %collective-permute-done.66), channel_id=1, source_target_pairs={{4,8},{8,12},{5,9},{9,13},{6,10},{10,14},{7,11},{11,15},{20,24},{2... | collective-permute-start | bytes 3145736 | tf_op jit(solution)/shard_map/ppermute | solution.py:11
  513.9 103.8 %collective-permute-start.89 = (bf16[256,1024]{1,0:T(8,128)(2,1)}, bf16[256,1024]{1,0:T(8,128)(2,1)}, u32[]{:S(2)}, u32[]{:S(2)}) collective-permute-start(bf16[256,1024]{1,0:T(8,128)(2,1)} %slice_select_fusion.4), channel_id=1, source_target_pairs={{0,4},{4,0},{8,12},{12,8},{1,5},{5,1},{9,13},{13,9},{2,6},{6,2},{1... | collective-permute-start | bytes 1572872 | tf_op jit(solution)/shard_map/ppermute | solution.py:15
  525.9 101.0 %collective-permute-start.94 = (bf16[256,1024]{1,0:T(8,128)(2,1)}, bf16[256,1024]{1,0:T(8,128)(2,1)}, u32[]{:S(2)}, u32[]{:S(2)}) collective-permute-start(bf16[256,1024]{1,0:T(8,128)(2,1)} %slice_select_fusion.4), channel_id=1, source_target_pairs={{0,12},{4,8},{8,4},{12,0},{1,13},{5,9},{9,5},{13,1},{2,14},{6,10},... | collective-permute-start | bytes 1572872 | tf_op jit(solution)/shard_map/ppermute | solution.py:15
  533.5 86.2 %collective-permute-start.92 = (bf16[256,1024]{1,0:T(8,128)(2,1)}, bf16[256,1024]{1,0:T(8,128)(2,1)}, u32[]{:S(2)}, u32[]{:S(2)}) collective-permute-start(bf16[256,1024]{1,0:T(8,128)(2,1)} %slice_select_fusion.3), channel_id=1, source_target_pairs={{0,8},{4,12},{8,0},{12,4},{1,9},{5,13},{9,1},{13,5},{2,10},{6,14},... | collective-permute-start | bytes 1572872 | tf_op jit(solution)/shard_map/ppermute | solution.py:15
  617.8 57.9 %collective-permute-start.15 = (bf16[512,512]{0,1:T(8,128)(2,1)S(1)}, bf16[512,512]{0,1:T(8,128)(2,1)S(1)}, u32[]{:S(2)}, u32[]{:S(2)}) collective-permute-start(bf16[512,512]{0,1:T(8,128)(2,1)S(1)} %copy-done.124), channel_id=1, source_target_pairs={{0,4},{4,0},{8,12},{12,8},{1,5},{5,1},{9,13},{13,9},{2,6},{6,2},{1... | collective-permute-start | bytes 1572872 | tf_op jit(solution)/shard_map/ppermute | solution.py:15
  626.7 50.3 %collective-permute-start.20 = (bf16[512,512]{0,1:T(8,128)(2,1)S(1)}, bf16[512,512]{0,1:T(8,128)(2,1)S(1)}, u32[]{:S(2)}, u32[]{:S(2)}) collective-permute-start(bf16[512,512]{0,1:T(8,128)(2,1)S(1)} %copy-done.124), channel_id=1, source_target_pairs={{0,12},{4,8},{8,4},{12,0},{1,13},{5,9},{9,5},{13,1},{2,14},{6,10},... | collective-permute-start | bytes 1572872 | tf_op jit(solution)/shard_map/ppermute | solution.py:15
  626.9 47.3 %collective-permute-start.18 = (bf16[512,512]{0,1:T(8,128)(2,1)S(1)}, bf16[512,512]{0,1:T(8,128)(2,1)S(1)}, u32[]{:S(2)}, u32[]{:S(2)}) collective-permute-start(bf16[512,512]{0,1:T(8,128)(2,1)S(1)} %copy-done.123), channel_id=1, source_target_pairs={{0,8},{4,12},{8,0},{12,4},{1,9},{5,13},{9,1},{13,5},{2,10},{6,14},... | collective-permute-start | bytes 1572872 | tf_op jit(solution)/shard_map/ppermute | solution.py:15
  636.7 41.7 %collective-permute-start.76 = (bf16[64,2048]{1,0:T(8,128)(2,1)S(1)}, bf16[64,2048]{1,0:T(8,128)(2,1)S(1)}, u32[]{:S(2)}, u32[]{:S(2)}) collective-permute-start(bf16[64,2048]{1,0:T(8,128)(2,1)S(1)} %fusion.284), channel_id=1, source_target_pairs={{0,2},{1,3},{2,0},{3,1},{4,6},{5,7},{6,4},{7,5},{8,10},{9,11},{10,... | collective-permute-start | bytes 786440 | tf_op jit(solution)/shard_map/ppermute | solution.py:15
  678.4 42.0 %collective-permute-start.21 = (bf16[512,512]{0,1:T(8,128)(2,1)S(1)}, bf16[512,512]{0,1:T(8,128)(2,1)S(1)}, u32[]{:S(2)}, u32[]{:S(2)}) collective-permute-start(bf16[512,512]{0,1:T(8,128)(2,1)S(1)} %collective-permute-done.20), channel_id=1, source_target_pairs={{0,16},{1,17},{2,18},{3,19},{4,20},{5,21},{6,22},{7,23},{8,24},{9,... | collective-permute-start | bytes 1572872 | tf_op jit(solution)/shard_map/ppermute | solution.py:11
  682.6 38.9 %collective-permute-start.83 = (bf16[128,2048]{1,0:T(8,128)(2,1)S(1)}, bf16[128,2048]{1,0:T(8,128)(2,1)S(1)}, u32[]{:S(2)}, u32[]{:S(2)}) collective-permute-start(bf16[128,2048]{1,0:T(8,128)(2,1)S(1)} %pad_maximum_fusion.21), channel_id=1, source_target_pairs={{0,4},{4,0},{8,12},{12,8},{1,5},{5,1},{9,13},{13,9},{2,6},{6,2},{1... | collective-permute-start | bytes 1572872 | tf_op jit(solution)/shard_map/ppermute | solution.py:15
  785.8 39.7 %collective-permute-start.98 = (bf16[128,2048]{1,0:T(8,128)(2,1)}, bf16[128,2048]{1,0:T(8,128)(2,1)}, u32[]{:S(2)}, u32[]{:S(2)}) collective-permute-start(bf16[128,2048]{1,0:T(8,128)(2,1)} %pad_maximum_fusion.22), channel_id=1, source_target_pairs={{0,2},{1,3},{2,0},{3,1},{4,6},{5,7},{6,4},{7,5},{8,10},{9,11},{10,... | collective-permute-start | bytes 1572872 | tf_op jit(solution)/shard_map/ppermute | solution.py:15
  787.1 38.4 %collective-permute-start.100 = (bf16[128,2048]{1,0:T(8,128)(2,1)}, bf16[128,2048]{1,0:T(8,128)(2,1)S(1)}, u32[]{:S(2)}, u32[]{:S(2)}) collective-permute-start(bf16[128,2048]{1,0:T(8,128)(2,1)} %pad_maximum_fusion.23), channel_id=1, source_target_pairs={{0,4},{4,0},{8,12},{12,8},{1,5},{5,1},{9,13},{13,9},{2,6},{6,2},{1... | collective-permute-start | bytes 1572872 | tf_op jit(solution)/shard_map/ppermute | solution.py:15
  809.1 42.8 %collective-permute-start.133 = (bf16[512,2048]{1,0:T(8,128)(2,1)}, bf16[512,2048]{1,0:T(8,128)(2,1)S(1)}, u32[]{:S(2)}, u32[]{:S(2)}) collective-permute-start(bf16[512,2048]{1,0:T(8,128)(2,1)} %copy.466), channel_id=1, source_target_pairs={{0,1},{1,0},{2,3},{3,2},{4,5},{5,4},{6,7},{7,6},{8,9},{9,8},{10,11... | collective-permute-start | bytes 6291464 | tf_op jit(solution)/shard_map/ppermute | solution.py:15
  849.1 79.3 %collective-permute-start.167 = (bf16[256,1024]{1,0:T(8,128)(2,1)}, bf16[256,1024]{1,0:T(8,128)(2,1)}, u32[]{:S(2)}, u32[]{:S(2)}) collective-permute-start(bf16[256,1024]{1,0:T(8,128)(2,1)} %get-tuple-element.211), channel_id=1, source_target_pairs={{0,16},{1,17},{2,18},{3,19},{4,20},{5,21},{6,22},{7,23},{8,24},{9,... | collective-permute-start | bytes 1572872 | tf_op jit(solution)/shard_map/ppermute | solution.py:11
  899.2 38.5 %collective-permute-start.134 = (bf16[64,2048]{1,0:T(8,128)(2,1)S(1)}, bf16[64,2048]{1,0:T(8,128)(2,1)S(1)}, u32[]{:S(2)}, u32[]{:S(2)}) collective-permute-start(bf16[64,2048]{1,0:T(8,128)(2,1)S(1)} %get-tuple-element.180), channel_id=1, source_target_pairs={{0,4},{4,0},{8,12},{12,8},{1,5},{5,1},{9,13},{13,9},{2,6},{6,2},{1... | collective-permute-start | bytes 786440 | tf_op jit(solution)/shard_map/ppermute | solution.py:15
  899.3 38.4 %collective-permute-start.136 = (bf16[64,2048]{1,0:T(8,128)(2,1)S(1)}, bf16[64,2048]{1,0:T(8,128)(2,1)S(1)}, u32[]{:S(2)}, u32[]{:S(2)}) collective-permute-start(bf16[64,2048]{1,0:T(8,128)(2,1)S(1)} %get-tuple-element.179), channel_id=1, source_target_pairs={{0,2},{1,3},{2,0},{3,1},{4,6},{5,7},{6,4},{7,5},{8,10},{9,11},{10,... | collective-permute-start | bytes 786440 | tf_op jit(solution)/shard_map/ppermute | solution.py:15
  1010.8 51.3 %collective-permute-start.179 = (bf16[512,512]{0,1:T(8,128)(2,1)}, bf16[512,512]{0,1:T(8,128)(2,1)}, u32[]{:S(2)}, u32[]{:S(2)}) collective-permute-start(bf16[512,512]{0,1:T(8,128)(2,1)} %slice_bitcast_fusion.19), channel_id=1, source_target_pairs={{16,0},{17,1},{18,2},{19,3},{20,4},{21,5},{22,6},{23,7},{24,8},{25... | collective-permute-start | bytes 1572872 | tf_op jit(solution)/shard_map/ppermute | solution.py:11
  1013.2 50.1 %collective-permute-start.181 = (bf16[512,512]{0,1:T(8,128)(2,1)}, bf16[512,512]{0,1:T(8,128)(2,1)}, u32[]{:S(2)}, u32[]{:S(2)}) collective-permute-start(bf16[512,512]{0,1:T(8,128)(2,1)} %slice_bitcast_fusion.17), channel_id=1, source_target_pairs={{16,0},{17,1},{18,2},{19,3},{20,4},{21,5},{22,6},{23,7},{24,8},{25... | collective-permute-start | bytes 1572872 | tf_op jit(solution)/shard_map/ppermute | solution.py:11
  1062.1 73.9 %collective-permute-start.118 = (bf16[512,2048]{1,0:T(8,128)(2,1)S(1)}, bf16[512,2048]{1,0:T(8,128)(2,1)S(1)}, u32[]{:S(2)}, u32[]{:S(2)}) collective-permute-start(bf16[512,2048]{1,0:T(8,128)(2,1)S(1)} %copy-done.84), channel_id=1, source_target_pairs={{0,1},{1,0},{2,3},{3,2},{4,5},{5,4},{6,7},{7,6},{8,9},{9,8},{10,11... | collective-permute-start | bytes 6291464 | tf_op jit(solution)/shard_map/ppermute | solution.py:15
  1082.9 48.6 %collective-permute-start.175 = (bf16[512,512]{0,1:T(8,128)(2,1)S(1)}, bf16[512,512]{0,1:T(8,128)(2,1)S(1)}, u32[]{:S(2)}, u32[]{:S(2)}) collective-permute-start(bf16[512,512]{0,1:T(8,128)(2,1)S(1)} %fusion.246), channel_id=1, source_target_pairs={{0,4},{4,0},{8,12},{12,8},{1,5},{5,1},{9,13},{13,9},{2,6},{6,2},{1... | collective-permute-start | bytes 1572872 | tf_op jit(solution)/shard_map/ppermute | solution.py:15
  1090.7 42.8 %collective-permute-start.177 = (bf16[512,512]{0,1:T(8,128)(2,1)S(1)}, bf16[512,512]{0,1:T(8,128)(2,1)S(1)}, u32[]{:S(2)}, u32[]{:S(2)}) collective-permute-start(bf16[512,512]{0,1:T(8,128)(2,1)S(1)} %fusion.245), channel_id=1, source_target_pairs={{0,12},{4,8},{8,4},{12,0},{1,13},{5,9},{9,5},{13,1},{2,14},{6,10},... | collective-permute-start | bytes 1572872 | tf_op jit(solution)/shard_map/ppermute | solution.py:15
  1092.7 108.2 %collective-permute-start.188 = (bf16[512,512]{0,1:T(8,128)(2,1)S(1)}, bf16[512,512]{0,1:T(8,128)(2,1)S(1)}, u32[]{:S(2)}, u32[]{:S(2)}) collective-permute-start(bf16[512,512]{0,1:T(8,128)(2,1)S(1)} %fusion.241), channel_id=1, source_target_pairs={{0,8},{4,12},{8,0},{12,4},{1,9},{5,13},{9,1},{13,5},{2,10},{6,14},... | collective-permute-start | bytes 1572872 | tf_op jit(solution)/shard_map/ppermute | solution.py:15
  1097.5 106.3 %collective-permute-start.185 = (bf16[512,512]{0,1:T(8,128)(2,1)S(1)}, bf16[512,512]{0,1:T(8,128)(2,1)S(1)}, u32[]{:S(2)}, u32[]{:S(2)}) collective-permute-start(bf16[512,512]{0,1:T(8,128)(2,1)S(1)} %fusion.242), channel_id=1, source_target_pairs={{0,8},{4,12},{8,0},{12,4},{1,9},{5,13},{9,1},{13,5},{2,10},{6,14},... | collective-permute-start | bytes 1572872 | tf_op jit(solution)/shard_map/ppermute | solution.py:15
  1133.5 36.4 %collective-permute-start.161 = (bf16[256,1024]{1,0:T(8,128)(2,1)S(1)}, bf16[256,1024]{1,0:T(8,128)(2,1)S(1)}, u32[]{:S(2)}, u32[]{:S(2)}) collective-permute-start(bf16[256,1024]{1,0:T(8,128)(2,1)S(1)} %get-tuple-element.153), channel_id=1, source_target_pairs={{0,12},{4,8},{8,4},{12,0},{1,13},{5,9},{9,5},{13,1},{2,14},{6,10},... | collective-permute-start | bytes 1572872 | tf_op jit(solution)/shard_map/ppermute | solution.py:15
  1136.0 58.0 %collective-permute-start.183 = (bf16[512,512]{0,1:T(8,128)(2,1)S(1)}, bf16[512,512]{0,1:T(8,128)(2,1)S(1)}, u32[]{:S(2)}, u32[]{:S(2)}) collective-permute-start(bf16[512,512]{0,1:T(8,128)(2,1)S(1)} %get-tuple-element.207), channel_id=1, source_target_pairs={{0,16},{1,17},{2,18},{3,19},{4,20},{5,21},{6,22},{7,23},{8,24},{9,... | collective-permute-start | bytes 1572872 | tf_op jit(solution)/shard_map/ppermute | solution.py:11
  1154.9 41.7 %collective-permute-start.178 = (bf16[512,512]{0,1:T(8,128)(2,1)S(1)}, bf16[512,512]{0,1:T(8,128)(2,1)S(1)}, u32[]{:S(2)}, u32[]{:S(2)}) collective-permute-start(bf16[512,512]{0,1:T(8,128)(2,1)S(1)} %get-tuple-element.209), channel_id=1, source_target_pairs={{16,0},{17,1},{18,2},{19,3},{20,4},{21,5},{22,6},{23,7},{24,8},{25... | collective-permute-start | bytes 1572872 | tf_op jit(solution)/shard_map/ppermute | solution.py:11
  1196.6 42.2 %collective-permute-start.172 = (bf16[256,1024]{1,0:T(8,128)(2,1)S(1)}, bf16[256,1024]{1,0:T(8,128)(2,1)}, u32[]{:S(2)}, u32[]{:S(2)}) collective-permute-start(bf16[256,1024]{1,0:T(8,128)(2,1)S(1)} %copy-done.118), channel_id=1, source_target_pairs={{0,8},{4,12},{8,0},{12,4},{1,9},{5,13},{9,1},{13,5},{2,10},{6,14},... | collective-permute-start | bytes 1572872 | tf_op jit(solution)/shard_map/ppermute | solution.py:15
  1200.9 54.4 %collective-permute-start.169 = (bf16[256,1024]{1,0:T(8,128)(2,1)}, bf16[256,1024]{1,0:T(8,128)(2,1)}, u32[]{:S(2)}, u32[]{:S(2)}) collective-permute-start(bf16[256,1024]{1,0:T(8,128)(2,1)} %get-tuple-element.152), channel_id=1, source_target_pairs={{0,8},{4,12},{8,0},{12,4},{1,9},{5,13},{9,1},{13,5},{2,10},{6,14},... | collective-permute-start | bytes 1572872 | tf_op jit(solution)/shard_map/ppermute | solution.py:15
  1203.8 52.1 %collective-permute-start.162 = (bf16[256,1024]{1,0:T(8,128)(2,1)S(1)}, bf16[256,1024]{1,0:T(8,128)(2,1)S(1)}, u32[]{:S(2)}, u32[]{:S(2)}) collective-permute-start(bf16[256,1024]{1,0:T(8,128)(2,1)S(1)} %get-tuple-element.213), channel_id=1, source_target_pairs={{16,0},{17,1},{18,2},{19,3},{20,4},{21,5},{22,6},{23,7},{24,8},{25... | collective-permute-start | bytes 1572872 | tf_op jit(solution)/shard_map/ppermute | solution.py:11
  1255.3 335.6 %collective-permute-start.135 = (bf16[128,2048]{1,0:T(8,128)(2,1)}, bf16[128,2048]{1,0:T(8,128)(2,1)}, u32[]{:S(2)}, u32[]{:S(2)}) collective-permute-start(bf16[128,2048]{1,0:T(8,128)(2,1)} %pad_maximum_fusion.30), channel_id=1, source_target_pairs={{0,2},{1,3},{2,0},{3,1},{4,6},{5,7},{6,4},{7,5},{8,10},{9,11},{10,... | collective-permute-start | bytes 1572872 | tf_op jit(solution)/shard_map/ppermute | solution.py:15
  1349.8 47.9 %collective-permute-start.149 = (bf16[256,2048]{1,0:T(8,128)(2,1)}, bf16[256,2048]{1,0:T(8,128)(2,1)}, u32[]{:S(2)}, u32[]{:S(2)}) collective-permute-start(bf16[256,2048]{1,0:T(8,128)(2,1)} %slice_bitcast_fusion.3), channel_id=1, source_target_pairs={{16,0},{17,1},{18,2},{19,3},{20,4},{21,5},{22,6},{23,7},{24,8},{25... | collective-permute-start | bytes 3145736 | tf_op jit(solution)/shard_map/ppermute | solution.py:11
  1361.6 53.9 %collective-permute-start.139 = (bf16[256,2048]{1,0:T(8,128)(2,1)}, bf16[256,2048]{1,0:T(8,128)(2,1)}, u32[]{:S(2)}, u32[]{:S(2)}) collective-permute-start(bf16[256,2048]{1,0:T(8,128)(2,1)} %slice_bitcast_fusion.9), channel_id=1, source_target_pairs={{0,16},{1,17},{2,18},{3,19},{4,20},{5,21},{6,22},{7,23},{8,24},{9,... | collective-permute-start | bytes 3145736 | tf_op jit(solution)/shard_map/ppermute | solution.py:11
  1386.0 42.0 %collective-permute-start.141 = (bf16[256,2048]{1,0:T(8,128)(2,1)}, bf16[256,2048]{1,0:T(8,128)(2,1)}, u32[]{:S(2)}, u32[]{:S(2)}) collective-permute-start(bf16[256,2048]{1,0:T(8,128)(2,1)} %fusion.132), channel_id=1, source_target_pairs={{0,4},{1,5},{2,6},{3,7},{16,20},{17,21},{18,22},{19,23}} | collective-permute-start | bytes 3145736 | tf_op jit(solution)/shard_map/ppermute | solution.py:11
  1397.7 36.9 %collective-permute-start.148 = (bf16[256,2048]{1,0:T(8,128)(2,1)}, bf16[256,2048]{1,0:T(8,128)(2,1)}, u32[]{:S(2)}, u32[]{:S(2)}) collective-permute-start(bf16[256,2048]{1,0:T(8,128)(2,1)} %slice_bitcast_fusion.5), channel_id=1, source_target_pairs={{16,0},{17,1},{18,2},{19,3},{20,4},{21,5},{22,6},{23,7},{24,8},{25... | collective-permute-start | bytes 3145736 | tf_op jit(solution)/shard_map/ppermute | solution.py:11
  1408.6 41.9 %collective-permute-start.152 = (bf16[256,2048]{1,0:T(8,128)(2,1)}, bf16[256,2048]{1,0:T(8,128)(2,1)}, u32[]{:S(2)}, u32[]{:S(2)}) collective-permute-start(bf16[256,2048]{1,0:T(8,128)(2,1)} %fusion.27), channel_id=1, source_target_pairs={{0,4},{4,8},{1,5},{5,9},{2,6},{6,10},{3,7},{7,11},{16,20},{20,24},... | collective-permute-start | bytes 3145736 | tf_op jit(solution)/shard_map/ppermute | solution.py:11
  1415.5 38.0 %collective-permute-start.138 = (bf16[256,2048]{1,0:T(8,128)(2,1)}, bf16[256,2048]{1,0:T(8,128)(2,1)S(1)}, u32[]{:S(2)}, u32[]{:S(2)}) collective-permute-start(bf16[256,2048]{1,0:T(8,128)(2,1)} %slice_bitcast_fusion.11), channel_id=1, source_target_pairs={{0,16},{1,17},{2,18},{3,19},{4,20},{5,21},{6,22},{7,23},{8,24},{9,... | collective-permute-start | bytes 3145736 | tf_op jit(solution)/shard_map/ppermute | solution.py:11
  1429.8 41.4 %collective-permute-start.142 = (bf16[256,2048]{1,0:T(8,128)(2,1)S(1)}, bf16[256,2048]{1,0:T(8,128)(2,1)S(1)}, u32[]{:S(2)}, u32[]{:S(2)}) collective-permute-start(bf16[256,2048]{1,0:T(8,128)(2,1)S(1)} %fusion.25), channel_id=1, source_target_pairs={{0,4},{4,8},{1,5},{5,9},{2,6},{6,10},{3,7},{7,11},{16,20},{20,24},... | collective-permute-start | bytes 3145736 | tf_op jit(solution)/shard_map/ppermute | solution.py:11
  1434.6 39.7 %collective-permute-start.126 = (bf16[2,64,2048]{2,1,0:T(8,128)(2,1)S(1)}, bf16[2,64,2048]{2,1,0:T(8,128)(2,1)S(1)}, u32[]{:S(2)}, u32[]{:S(2)}) collective-permute-start(bf16[2,64,2048]{2,1,0:T(8,128)(2,1)S(1)} %pad_maximum_fusion.28), channel_id=1, source_target_pairs={{0,1},{1,0},{2,3},{3,2},{4,5},{5,4},{6,7},{7,6},{8,9},{9,8},{10,11... | collective-permute-start | bytes 1572872 | tf_op jit(solution)/shard_map/ppermute | solution.py:15
  1480.1 58.5 %collective-permute-start.132 = (bf16[64,2048]{1,0:T(8,128)(2,1)S(1)}, bf16[64,2048]{1,0:T(8,128)(2,1)S(1)}, u32[]{:S(2)}, u32[]{:S(2)}) collective-permute-start(bf16[64,2048]{1,0:T(8,128)(2,1)S(1)} %fusion.256), channel_id=1, source_target_pairs={{0,2},{1,3},{2,0},{3,1},{4,6},{5,7},{6,4},{7,5},{8,10},{9,11},{10,... | collective-permute-start | bytes 786440 | tf_op jit(solution)/shard_map/ppermute | solution.py:15
  1481.5 59.5 %collective-permute-start.153 = (bf16[256,2048]{1,0:T(8,128)(2,1)}, bf16[256,2048]{1,0:T(8,128)(2,1)S(1)}, u32[]{:S(2)}, u32[]{:S(2)}) collective-permute-start(bf16[256,2048]{1,0:T(8,128)(2,1)} %get-tuple-element.77), channel_id=1, source_target_pairs={{0,4},{4,8},{8,12},{1,5},{5,9},{9,13},{2,6},{6,10},{10,14},{3,7},{... | collective-permute-start | bytes 3145736 | tf_op jit(solution)/shard_map/ppermute | solution.py:11
  1486.5 84.2 %collective-permute-start.143 = (bf16[256,2048]{1,0:T(8,128)(2,1)}, bf16[256,2048]{1,0:T(8,128)(2,1)}, u32[]{:S(2)}, u32[]{:S(2)}) collective-permute-start(bf16[256,2048]{1,0:T(8,128)(2,1)} %get-tuple-element.83), channel_id=1, source_target_pairs={{0,4},{4,8},{8,12},{1,5},{5,9},{9,13},{2,6},{6,10},{10,14},{3,7},{... | collective-permute-start | bytes 3145736 | tf_op jit(solution)/shard_map/ppermute | solution.py:11
  1514.0 48.8 %collective-permute-start.156 = (bf16[256,2048]{1,0:T(8,128)(2,1)}, bf16[256,2048]{1,0:T(8,128)(2,1)}, u32[]{:S(2)}, u32[]{:S(2)}) collective-permute-start(bf16[256,2048]{1,0:T(8,128)(2,1)} %add_convert_fusion), channel_id=1, source_target_pairs={{12,8},{8,4},{4,0},{13,9},{9,5},{5,1},{14,10},{10,6},{6,2},{15,11}... | collective-permute-start | bytes 3145736 | tf_op jit(solution)/shard_map/ppermute | solution.py:11
  1538.6 46.6 %collective-permute-start.146 = (bf16[256,2048]{1,0:T(8,128)(2,1)}, bf16[256,2048]{1,0:T(8,128)(2,1)}, u32[]{:S(2)}, u32[]{:S(2)}) collective-permute-start(bf16[256,2048]{1,0:T(8,128)(2,1)} %add_convert_fusion.2), channel_id=1, source_target_pairs={{12,8},{8,4},{4,0},{13,9},{9,5},{5,1},{14,10},{10,6},{6,2},{15,11}... | collective-permute-start | bytes 3145736 | tf_op jit(solution)/shard_map/ppermute | solution.py:11
  1541.0 55.0 %collective-permute-start.137 = (bf16[128,2048]{1,0:T(8,128)(2,1)}, bf16[128,2048]{1,0:T(8,128)(2,1)}, u32[]{:S(2)}, u32[]{:S(2)}) collective-permute-start(bf16[128,2048]{1,0:T(8,128)(2,1)} %pad_maximum_fusion.31), channel_id=1, source_target_pairs={{0,4},{4,0},{8,12},{12,8},{1,5},{5,1},{9,13},{13,9},{2,6},{6,2},{1... | collective-permute-start | bytes 1572872 | tf_op jit(solution)/shard_map/ppermute | solution.py:15
  1566.1 119.6 %collective-permute-start.157 = (bf16[256,2048]{1,0:T(8,128)(2,1)}, bf16[256,2048]{1,0:T(8,128)(2,1)}, u32[]{:S(2)}, u32[]{:S(2)}) collective-permute-start(bf16[256,2048]{1,0:T(8,128)(2,1)} %get-tuple-element.166), channel_id=1, source_target_pairs={{0,16},{1,17},{2,18},{3,19},{4,20},{5,21},{6,22},{7,23},{8,24},{9,... | collective-permute-start | bytes 3145736 | tf_op jit(solution)/shard_map/ppermute | solution.py:11
  1588.9 98.4 %collective-permute-start.147 = (bf16[256,2048]{1,0:T(8,128)(2,1)}, bf16[256,2048]{1,0:T(8,128)(2,1)}, u32[]{:S(2)}, u32[]{:S(2)}) collective-permute-start(bf16[256,2048]{1,0:T(8,128)(2,1)} %get-tuple-element.168), channel_id=1, source_target_pairs={{16,0},{17,1},{18,2},{19,3},{20,4},{21,5},{22,6},{23,7},{24,8},{25... | collective-permute-start | bytes 3145736 | tf_op jit(solution)/shard_map/ppermute | solution.py:11
  (334 other events, 6373.5 us)
Sparse Core Ops, SparseCore 0:
  1591.0 89.3 all-reduce.4

commit v2 on v1

--- a/solution.py
+++ b/solution.py
@@ -1,6 +1,11 @@
+import functools
+
 import jax
 import jax.numpy as jnp
+import numpy as np
 from jax import lax
+from jax.experimental import pallas as pl
+from jax.experimental.pallas import tpu as pltpu
 from jax.sharding import PartitionSpec as P
 
 BF = jnp.bfloat16
@@ -81,91 +86,503 @@
     return own + swap(chip.astype(BF), "tensor", 2).astype(F32) + swap(plane.astype(BF), "dp", 1).astype(F32)
 
 
-def gather_line(pack, layer, is_layer):
+def scatter_line(full):
     count = lax.axis_size("dp")
     plane = lax.axis_index("dp")
-    half = pack.shape[0] // 2
-    away = hop(pack[half:], "section", [(layer, 1 - layer)])
-    held = jnp.where(is_layer, pack[:half], away)
-    right, left = held, held
-    rights, lefts = [], []
-    for step in range(1, count):
-        right = hop(right, "dp", [(i, i + 1) for i in range(step - 1, count - 1)])
-        left = hop(left, "dp", [(i + 1, i) for i in range(count - step)])
-        rights.append(right)
-        lefts.append(left)
-    full = jnp.zeros((count,) + pack.shape, pack.dtype)
-    full = lax.dynamic_update_slice(full, pack[None], (plane, 0, 0))
-    for step in range(1, count):
-        block = rights[step - 1] + lefts[count - step - 1]
-        home = hop(block, "section", [(1 - layer, layer)])
-        both = jnp.concatenate([block, home], axis=0)
-        full = lax.dynamic_update_slice(full, both[None], (lax.rem(plane - step + count, count), 0, 0))
-    return full
-
-
-def gather_pair(own, sends, layer, is_layer):
-    count = lax.axis_size("dp")
-    plane = lax.axis_index("dp")
-    half = own.shape[0] // 2
-    full = jnp.zeros((count,) + own.shape, own.dtype)
-    full = lax.dynamic_update_slice(full, own[None], (plane, 0, 0))
-    for distance in range(1, count):
-        block = sends[distance & 1]
-        away = hop(block[half:], "section", [(layer, 1 - layer)])
-        held = jnp.where(is_layer, block[:half], away)
-        got = swap(held, "dp", distance)
-        home = hop(got, "section", [(1 - layer, layer)])
-        both = jnp.concatenate([got, home], axis=0)
-        full = lax.dynamic_update_slice(full, both[None], (plane ^ distance, 0, 0))
-    return full
-
-
-def scatter_line(full, layer, is_layer):
-    count = lax.axis_size("dp")
-    plane = lax.axis_index("dp")
-    half = full.shape[1] // 2
 
     def block(offset):
         return dslice(full, lax.rem(plane + offset, count), 1, 0)[0]
 
     own = block(0).astype(F32)
-    held = {}
-    for offset in range(1, count):
-        piece = block(offset)
-        away = hop(piece[half:], "section", [(layer, 1 - layer)])
-        held[offset] = jnp.where(is_layer, piece[:half], away)
     right = left = None
     for step in range(count - 1):
-        to_right, to_left = held[count - 1 - step], held[step + 1]
+        to_right, to_left = block(count - 1 - step), block(step + 1)
         if right is not None:
             to_right = (to_right.astype(F32) + right.astype(F32)).astype(BF)
             to_left = (to_left.astype(F32) + left.astype(F32)).astype(BF)
         right = hop(to_right, "dp", [(i, i + 1) for i in range(step + 1)])
         left = hop(to_left, "dp", [(i, i - 1) for i in range(count - 1, count - 2 - step, -1)])
-    total = right.astype(F32) + left.astype(F32)
-    home = hop(total.astype(BF), "section", [(1 - layer, layer)]).astype(F32)
-    return own + jnp.concatenate([total, home], axis=0)
-
-
-def scatter_pair(full, layer, is_layer):
+    return own + right.astype(F32) + left.astype(F32)
+
+
+def scatter_pair(full):
     count = lax.axis_size("dp")
     plane = lax.axis_index("dp")
-    half = full.shape[1] // 2
-    sums = [None, None]
+    sums = [dslice(full, plane, 1, 0)[0].astype(F32), None]
     for distance in range(1, count):
         piece = dslice(full, plane ^ distance, 1, 0)[0]
-        away = hop(piece[half:], "section", [(layer, 1 - layer)])
-        held = jnp.where(is_layer, piece[:half], away)
-        got = swap(held, "dp", distance).astype(F32)
+        got = swap(piece, "dp", distance).astype(F32)
         odd = distance & 1
         sums[odd] = got if sums[odd] is None else sums[odd] + got
-    own = dslice(full, plane, 1, 0)[0].astype(F32)
-    results = []
-    for part in sums:
-        home = hop(part.astype(BF), "section", [(1 - layer, layer)]).astype(F32)
-        results.append(jnp.concatenate([part, home], axis=0))
-    return own + results[0], results[1]
+    return sums
+
+
+MESH = pl.DeviceIdType.MESH
+NT = (((1,), (1,)), ((), ()))
+TN = (((0,), (0,)), ((), ()))
+
+
+def dot(a, b, dims=(((1,), (0,)), ((), ()))):
+    return lax.dot_general(a, b, dims, preferred_element_type=F32)
+
+
+def remote(src, dst, send_sem, recv_sem, device):
+    return pltpu.make_async_remote_copy(
+        src_ref=src, dst_ref=dst, send_sem=send_sem, recv_sem=recv_sem, device_id=device, device_id_type=MESH
+    )
+
+
+def when(condition):
+    return True if condition is True else condition
+
+
+def greet(devices):
+    barrier = pltpu.get_barrier_semaphore()
+    for device in devices:
+        pl.semaphore_signal(barrier, inc=1, device_id=device, device_id_type=MESH)
+    pl.semaphore_wait(barrier, len(devices))
+
+
+def tiles(count, body):
+    def step(i, carry):
+        body(i)
+        return carry
+
+    lax.fori_loop(0, count, step, 0)
+
+
+def rows_of(i, size):
+    return pl.ds(pl.multiple_of(i * size, size), size)
+
+
+def norm_rows(value, gain, shift_vec):
+    centre = value - jnp.mean(value, axis=-1, keepdims=True)
+    spread = jnp.mean(centre * centre, axis=-1, keepdims=True)
+    return centre * lax.rsqrt(spread + 1e-05) * gain + shift_vec
+
+
+def spots(base, shape, dim, rows):
+    index = lax.broadcasted_iota(jnp.int32, shape, dim)
+    return ((index // rows) ^ base) * rows + lax.rem(index, rows)
+
+
+def gelu_parts(v):
+    cube = v * v * v
+    inner = np.float32(np.sqrt(2 / np.pi)) * (v + 0.044715 * cube)
+    return jnp.tanh(inner)
+
+
+def masked_scores(raw, slope, length, place, rows, size):
+    gap = spots(place, raw.shape, 0, rows) - spots(place, raw.shape, 1, rows)
+    open_ = (gap >= 0) | (spots(place, raw.shape, 1, rows) < length)
+    scores = raw * np.float32(size ** (-0.5)) - slope * gap.astype(F32)
+    return jnp.where(open_, scores, -1e30)
+
+
+def forward_kernel(
+    dims, x_in, vec, qvb, upb, prefix, slopes, wq_in, wo_in, wu_in, wd_in,
+    out, wq, wo, wu, wd, x_out, mid_out, nb_out, qkv_out, mix_out, sec_out, up_out, act_out,
+    carry, carry_send, hid, mid, nb, qkv, mix, sec, up, act, outv,
+    vq, vo, vu, vd, s1, r1, part, sy, ry, part8, sc, rc, s8, r8,
+    line_s, line_r, pair_s, pair_r, own_sem, load_sem, keep_sem, carry_s, carry_r,
+    ag_s, ag_r, rs_s, rs_r, ag8_s, ag8_r, f8_s, f8_r, c8_s, c8_r, rs8_s, rs8_r,
+):
+    n, seqs, heads, size, rows, deep, half = dims
+    R = seqs * rows
+    wide = heads * size
+    D = n * deep
+    sect, z, t = lax.axis_index("section"), lax.axis_index("dp"), lax.axis_index("tensor")
+    me = (sect, z, t)
+    core = (sect, z, t ^ 1)
+    chip = (sect, z, t ^ 2)
+    plane = (sect, z ^ 1, t)
+    diag = (sect, z ^ 1, t ^ 2)
+    across = (1 - sect, z, t)
+    greet([(sect, z ^ k, t) for k in range(1, n)] + [core, chip, diag, across])
+
+    zl = z & 1
+    mine = [
+        pltpu.make_async_copy(wq_in, wq.at[:, pl.ds(pl.multiple_of(z * deep, deep), deep)], own_sem.at[0]),
+        pltpu.make_async_copy(wo_in, wo.at[z], own_sem.at[1]),
+        pltpu.make_async_copy(
+            wu_in.at[:, pl.ds(pl.multiple_of(zl * half, half), half)],
+            wu.at[pl.ds(pl.multiple_of(z * deep, deep), deep)], own_sem.at[2]),
+        pltpu.make_async_copy(
+            wd_in.at[pl.ds(pl.multiple_of(zl * half, half), half)], wd.at[z], own_sem.at[3]),
+    ]
+
+    def slot(a, b):
+        if a == 0:
+            return wq.at[:, pl.ds(pl.multiple_of(b * deep, deep), deep)]
+        return wo.at[b]
+
+    def line(a, side, step, b):
+        to = (sect, z + 1 - 2 * side, t)
+        src = (wq_in, wo_in)[a] if step == 1 else slot(a, b)
+        i = (a * 2 + side) * (n - 1) + step - 1
+        return remote(src, slot(a, b), line_s.at[i], line_r.at[i], to)
+
+    def line_send(a, side, step):
+        b = z - (step - 1) if side == 0 else z + (step - 1)
+        ok = (b >= 0) & (z < n - 1) if side == 0 else (b <= n - 1) & (z > 0)
+        return ok, lambda: line(a, side, step, b)
+
+    def line_recv(a, side, step):
+        b = z - step if side == 0 else z + step
+        ok = (b >= 0) if side == 0 else (b <= n - 1)
+        return ok, lambda: line(a, side, step, b)
+
+    def pair(a, k):
+        h = (z ^ k) & 1
+        to = (sect, z ^ k, t)
+        i = a * (n - 1) + k - 1
+        if a == 0:
+            src = wu_in.at[:, pl.ds(pl.multiple_of(h * half, half), half)]
+            dst = wu.at[pl.ds(pl.multiple_of(z * deep, deep), deep)]
+        else:
+            src = wd_in.at[pl.ds(pl.multiple_of(h * half, half), half)]
+            dst = wd.at[z]
+        return remote(src, dst, pair_s.at[i], pair_r.at[i], to)
+
+    def pair_recv(a, k):
+        i = a * (n - 1) + k - 1
+        if a == 0:
+            src = wu_in.at[:, pl.ds(0, half)]
+            dst = wu.at[pl.ds(pl.multiple_of((z ^ k) * deep, deep), deep)]
+        else:
+            src = wd_in.at[pl.ds(0, half)]
+            dst = wd.at[z ^ k]
+        return remote(src, dst, pair_s.at[i], pair_r.at[i], (sect, z ^ k, t))
+
+    for a in range(2):
+        for side in range(2):
+            ok, make = line_send(a, side, 1)
+
+            @pl.when(ok)
+            def _():
+                make().start()
+
+    for copy in mine:
+        copy.start()
+
+    tile = 32
+
+    def first_norm():
+        def body(i):
+            sl = rows_of(i, tile)
+            v = hid[sl, :].astype(F32)
+            nb[0, sl, :] = norm_rows(v, vec[0:1, :], vec[2:3, :]).astype(BF)
+
+        tiles(R // tile, body)
+
+    def ag(i):
+        src, to = ((0, core), (0, chip), (2, core))[i]
+        dst = (1, 2, 3)[i]
+        return remote(nb.at[src], nb.at[dst], ag_s.at[i], ag_r.at[i], to)
+
+    @pl.when(sect == 0)
+    def _():
+        hid[...] = x_in[...]
+        first_norm()
+        ag(1).start()
+        ag(0).start()
+        ag(1).wait_recv()
+        ag(2).start()
+
+    for step in range(1, n):
+        for a in range(2):
+            for side in range(2):
+                ok, make = line_recv(a, side, step)
+
+                @pl.when(ok)
+                def _():
+                    make().wait_recv()
+
+                if step < n - 1:
+                    ok, make = line_send(a, side, step + 1)
+
+                    @pl.when(ok)
+                    def _():
+                        make().start()
+
+        if step == n - 2 or n == 2:
+            for a in range(2):
+                for k in range(n - 1, 0, -1):
+                    pair(a, k).start()
+
+    for copy in mine:
+        copy.wait()
+    load_q = pltpu.make_async_copy(wq, vq, load_sem.at[0])
+    load_o = pltpu.make_async_copy(wo, vo, load_sem.at[1])
+    load_q.start()
+    load_o.start()
+
+    @pl.when(sect == 1)
+    def _():
+        remote(carry_send, carry, carry_s, carry_r, across).wait_recv()
+        hid[...] = carry[...]
+        first_norm()
+        ag(1).start()
+        ag(0).start()
+        ag(1).wait_recv()
+        ag(2).start()
+
+    ag(0).wait_recv()
+    ag(2).wait_recv()
+    load_q.wait()
+    load_o.wait()
+    keeps = []
+
+    def keep(src, dst):
+        copy = pltpu.make_async_copy(src, dst, keep_sem.at[len(keeps)])
+        copy.start()
+        keeps.append(copy)
+
+    keep(hid, x_out)
+    keep(nb, nb_out)
+
+    tn = min(256, wide)
+    for c in range(3):
+        def body(i):
+            j = lax.rem(i, wide // tn)
+            b = i // (wide // tn)
+            cols = rows_of(j, tn)
+            lhs = jnp.concatenate([nb[2 * b], nb[2 * b + 1]], axis=0)
+            got = dot(lhs, vq[c, :, cols]) + qvb[c : c + 1, cols]
+            got = got.astype(BF)
+            qkv[2 * b, :, pl.ds(pl.multiple_of(c * wide + j * tn, tn), tn)] = got[:R]
+            qkv[2 * b + 1, :, pl.ds(pl.multiple_of(c * wide + j * tn, tn), tn)] = got[R:]
+
+        tiles(2 * (wide // tn), body)
+    keep(qkv, qkv_out)
+
+    def head(i):
+        s, h = i // heads, lax.rem(i, heads)
+        pos = rows_of(s, rows)
+
+        def part_of(c):
+            cols = pl.ds(pl.multiple_of(c * wide + h * size, size), size)
+            return jnp.concatenate([qkv[j, pos, cols] for j in range(4)], axis=0)
+
+        raw = dot(part_of(0), part_of(1), NT)
+        scores = masked_scores(raw, slopes[h], prefix[s], t, rows, size)
+        expon = jnp.exp(scores - jnp.max(scores, axis=-1, keepdims=True))
+        probs = (expon / jnp.sum(expon, axis=-1, keepdims=True)).astype(BF)
+        got = dot(probs, part_of(2)).astype(BF)
+        for j in range(4):
+            mix[j, pos, rows_of(h, size)] = got[j * rows : (j + 1) * rows]
+
+    tiles(seqs * heads, head)
+    keep(mix, mix_out)
+
+    def project(pair_of, put):
+        lhs_blocks = pair_of
+
+        def body(i):
+            lhs = jnp.concatenate([mix[lhs_blocks[0]], mix[lhs_blocks[1]]], axis=0)
+            got = dot(lhs, vo[i])
+            put(rows_of(i, deep), got)
+
+        tiles(n, body)
+
+    def put_send(cols, got):
+        s1[0, :, cols] = got[:R].astype(BF)
+        s1[1, :, cols] = got[R:].astype(BF)
+
+    def put_part(cols, got):
+        part[0, :, cols] = got[:R]
+        part[1, :, cols] = got[R:]
+
+    to_core = remote(s1, r1, rs_s.at[0], rs_r.at[0], core)
+    to_chip = remote(sy, ry, rs_s.at[1], rs_r.at[1], chip)
+    project((3, 1), put_send)
+    to_core.start()
+    project((2, 0), put_part)
+    to_core.wait_recv()
+
+    def add_chip(i):
+        sl = rows_of(i, tile)
+        sy[sl, :] = (part[0, sl, :] + r1[0, sl, :].astype(F32)).astype(BF)
+
+    tiles(R // tile, add_chip)
+    to_chip.start()
+    to_chip.wait_recv()
+
+    def middle_body(i):
+        sl = rows_of(i, tile)
+        v = hid[sl, :].astype(F32) + part[1, sl, :] + r1[1, sl, :].astype(F32)
+        v = v + ry[sl, :].astype(F32) + vec[4:5, :]
+        mid[sl, :] = v
+        sec[0, sl, :] = norm_rows(v, vec[1:2, :], vec[3:4, :]).astype(BF)
+
+    tiles(R // tile, middle_body)
+    keep(mid, mid_out)
+
+    targets = (None, chip, plane, diag)
+
+    def ag8(i):
+        return remote(sec.at[0], sec.at[i], ag8_s.at[i], ag8_r.at[i], targets[i])
+
+    def forward8(i):
+        return remote(sec.at[i], sec.at[4 + i], f8_s.at[i], f8_r.at[i], core)
+
+    def core8(i):
+        return remote(sc.at[i], rc.at[i], c8_s.at[i], c8_r.at[i], core)
+
+    def rs8(i):
+        return remote(s8.at[i], r8.at[i], rs8_s.at[i], rs8_r.at[i], targets[i])
+
+    order = (0, 2, 1, 3)
+    for i in order[1:]:
+        ag8(i).start()
+    forward8(0).start()
+
+    for a in range(2):
+        for k in range(n - 1, 0, -1):
+            pair_recv(a, k).wait_recv()
+    load_u = pltpu.make_async_copy(wu, vu, load_sem.at[2])
+    load_d = pltpu.make_async_copy(wd, vd, load_sem.at[3])
+    load_u.start()
+    load_d.start()
+    load_u.wait()
+    load_d.wait()
+
+    tu = min(256, half)
+
+    def group(i):
+        if i:
+            ag8(i).wait_recv()
+            forward8(i).start()
+        forward8(i).wait_recv()
+
+        def up_body(j):
+            cols = rows_of(j, tu)
+            lhs = jnp.concatenate([sec[i], sec[4 + i]], axis=0)
+            v = dot(lhs, vu[:, cols]) + upb[:, cols]
+            g = (0.5 * v * (1.0 + gelu_parts(v))).astype(BF)
+            up[i, :, cols] = v[:R]
+            up[4 + i, :, cols] = v[R:]
+            act[i, :, cols] = g[:R]
+            act[4 + i, :, cols] = g[R:]
+
+        tiles(half // tu, up_body)
+
+        def down_body(j):
+            cols = rows_of(j, deep)
+            lhs = jnp.concatenate([act[i], act[4 + i]], axis=0)
+            got = dot(lhs, vd[j])
+            part8[i, :, cols] = got[:R]
+            sc[i, :, cols] = got[R:].astype(BF)
+
+        tiles(n, down_body)
+        core8(i).start()
+
+    def reduce(i):
+        core8(i).wait_recv()
+        if i == 0:
+            return
+
+        def body(j):
+            sl = rows_of(j, tile)
+            s8[i, sl, :] = (part8[i, sl, :] + rc[i, sl, :].astype(F32)).astype(BF)
+
+        tiles(R // tile, body)
+        rs8(i).start()
+
+    for number, i in enumerate(order):
+        group(i)
+        if number:
+            reduce(order[number - 1])
+    reduce(order[-1])
+    keep(sec, sec_out)
+    keep(up, up_out)
+    keep(act, act_out)
+    for i in order[1:]:
+        rs8(i).wait_recv()
+
+    def out_body(j):
+        sl = rows_of(j, tile)
+        v = mid[sl, :] + part8[0, sl, :] + rc[0, sl, :].astype(F32)
+        for i in (1, 2, 3):
+            v = v + r8[i, sl, :].astype(F32)
+        v = v + vec[5:6, :]
+        outv[sl, :] = v
+        carry_send[sl, :] = v.astype(BF)
+
+    tiles(R // tile, out_body)
+    over = remote(carry_send, carry, carry_s, carry_r, across)
+
+    @pl.when(sect == 0)
+    def _():
+        over.start()
+
+    keep(outv, out)
+
+    for step in range(1, n):
+        for a in range(2):
+            for side in range(2):
+                ok, make = line_send(a, side, step)
+
+                @pl.when(ok)
+                def _():
+                    make().wait_send()
+
+    for a in range(2):
+        for k in range(n - 1, 0, -1):
+            pair(a, k).wait_send()
+    for i in range(3):
+        ag(i).wait_send()
+    to_core.wait_send()
+    to_chip.wait_send()
+    for i in range(4):
+        if i:
+            ag8(i).wait_send()
+            rs8(i).wait_send()
+        forward8(i).wait_send()
+        core8(i).wait_send()
+
+    @pl.when(sect == 0)
+    def _():
+        over.wait_send()
+
+    for copy in keeps:
+        copy.wait()
+
+
+def run_forward(dims, x, vec, qvb, upb, prefix, slopes, wq, wo, wu, wd):
+    n, seqs, heads, size, rows, deep, half = dims
+    R, wide, D = seqs * rows, heads * size, n * deep
+    V = lambda shape, dtype: pltpu.VMEM(shape, dtype)
+    S = lambda *shape: jax.ShapeDtypeStruct(shape[:-1], shape[-1])
+    any_ = pl.BlockSpec(memory_space=pl.ANY)
+    vm = pl.BlockSpec(memory_space=pltpu.VMEM)
+    sm = pl.BlockSpec(memory_space=pltpu.SMEM)
+    dma = lambda k: pltpu.SemaphoreType.DMA((k,))
+    outs = (
+        S(R, D, F32), S(3, D, wide, BF), S(n, wide, deep, BF), S(D, half, BF), S(n, half, deep, BF),
+        S(R, D, BF), S(R, D, F32), S(4, R, D, BF), S(4, R, 3 * wide, BF), S(4, R, wide, BF),
+        S(8, R, D, BF), S(8, R, half, F32), S(8, R, half, BF),
+    )
+    scratch = [
+        V((R, D), BF), V((R, D), BF), V((R, D), BF), V((R, D), F32), V((4, R, D), BF), V((4, R, 3 * wide), BF),
+        V((4, R, wide), BF), V((8, R, D), BF), V((8, R, half), F32), V((8, R, half), BF), V((R, D), F32),
+        V((3, D, wide), BF), V((n, wide, deep), BF), V((D, half), BF), V((n, half, deep), BF),
+        V((2, R, D), BF), V((2, R, D), BF), V((2, R, D), F32), V((R, D), BF), V((R, D), BF),
+        V((4, R, D), F32), V((4, R, D), BF), V((4, R, D), BF), V((4, R, D), BF), V((4, R, D), BF),
+        dma(4 * (n - 1)), dma(4 * (n - 1)), dma(2 * (n - 1)), dma(2 * (n - 1)), dma(4), dma(4), dma(9),
+        pltpu.SemaphoreType.DMA(()), pltpu.SemaphoreType.DMA(()),
+        dma(3), dma(3), dma(2), dma(2), dma(4), dma(4), dma(4), dma(4), dma(4), dma(4), dma(4), dma(4),
+    ]
+    return pl.pallas_call(
+        functools.partial(forward_kernel, dims),
+        out_shape=outs,
+        in_specs=[vm, vm, vm, vm, sm, sm, any_, any_, any_, any_],
+        out_specs=(any_,) * len(outs),
+        scratch_shapes=scratch,
+        compiler_params=pltpu.CompilerParams(
+            collective_id=0, has_side_effects=True, vmem_limit_bytes=60 * 1024 * 1024
+        ),
+    )(x, vec, qvb, upb, prefix, slopes, wq, wo, wu, wd)
 
 
 def score_block(queries, keys, length, slopes, positions):
@@ -174,24 +591,6 @@
     allowed = (positions[None, :] <= positions[:, None]) | (positions[None, :] < length)
     scores = raw * queries.shape[2] ** (-0.5) - slopes[:, None, None] * offsets
     return jnp.where(allowed, scores, -1e30)
-
-
-def attend(proj, qv_bias, length, slopes, positions):
-    heads, size = qv_bias.shape[1:]
-    seq_len = proj.shape[0]
-    flat = qv_bias.astype(F32).reshape(2, heads * size)
-    wide = heads * size
-    queries = (proj[:, :wide] + flat[0]).astype(BF).reshape(seq_len, heads, size)
-    keys = proj[:, wide : 2 * wide].astype(BF).reshape(seq_len, heads, size)
-    values = (proj[:, 2 * wide :] + flat[1]).astype(BF).reshape(seq_len, heads, size)
-    scores = score_block(queries, keys, length, slopes, positions)
-    peak = jnp.max(scores, axis=-1, keepdims=True)
-    expon = jnp.exp(scores - peak)
-    total = jnp.sum(expon, axis=-1, keepdims=True)
-    probs = (expon / total).astype(BF)
-    mixed = jnp.einsum("hqk,khe->qhe", probs, values, preferred_element_type=F32)
-    mixed = mixed.astype(BF).reshape(seq_len, wide)
-    return mixed, (queries, keys, values, (peak + jnp.log(total))[..., 0])
 
 
 def attend_back(grad_mixed, kept, length, slopes, positions):
@@ -209,29 +608,6 @@
         "hqk,qhe->khe", probs.astype(BF), grad_heads, preferred_element_type=F32
     ).astype(BF)
     return jnp.concatenate([g.reshape(seq_len, heads * size) for g in (grad_q, grad_k, grad_v)], axis=1)
-
-
-def forward(hidden, lengths, weights, gains, shifts, qv_bias, up_bias, slopes, positions):
-    w_qkv, w_out, w_up, w_down = weights
-    normed, heads, mixed_all, middle, second = [], [], [], [], []
-    for seq, rows in enumerate(hidden):
-        full = spread_rows(layer_norm(rows, gains[0], shifts[0]).astype(BF))
-        proj = jnp.dot(full, w_qkv, preferred_element_type=F32)
-        mixed, kept = attend(proj, qv_bias, lengths[seq], slopes, positions)
-        branch = jnp.einsum("tf,zfd->tzd", mixed, w_out, preferred_element_type=F32)
-        mid = rows + collect_rows(branch.reshape(full.shape)) + shifts[2]
-        normed.append(full)
-        heads.append(kept)
-        mixed_all.append(mixed)
-        middle.append(mid)
-        second.append(layer_norm(mid, gains[1], shifts[1]).astype(BF))
-    second = spread_pair(jnp.concatenate(second, axis=0))
-    up = jnp.dot(second, w_up, preferred_element_type=F32) + up_bias
-    act = jax.nn.gelu(up, approximate=True).astype(BF)
-    branch = jnp.einsum("tf,zfd->tzd", act, w_down, preferred_element_type=F32)
-    branch = collect_pair(branch.reshape(second.shape))
-    output = jnp.concatenate(middle, axis=0) + branch + shifts[3]
-    return output, (hidden, normed, heads, mixed_all, middle, second, up, act)
 
 
 def backward(grad_out, grad_pair, kept, lengths, weights, gains, slopes, positions, planes):
@@ -319,65 +695,53 @@
     slopes = jnp.exp2(-8.0 * (head_ids.astype(F32) + 1.0) / (heads * tensors))
     positions = jnp.concatenate([(place ^ j) * rows + jnp.arange(rows) for j in range(tensors)])
 
-    pack = jnp.concatenate([w_qkv[0].reshape(deep, 3 * wide), w_out[0].reshape(deep, wide)], axis=1)
-    up_parts = (w_up[0][:, :half], w_up[0][:, half:])
-    down_parts = (w_down[0][:half], w_down[0][half:])
-    up_keep = jnp.where(odd, up_parts[1], up_parts[0])
-    up_send = jnp.where(odd, up_parts[0], up_parts[1])
-    down_keep = jnp.where(odd, down_parts[1], down_parts[0])
-    down_send = jnp.where(odd, down_parts[0], down_parts[1])
-
-    def gather(layer, pack, up_keep, up_send, down_keep, down_send):
-        is_layer = is_first if layer == 0 else ~is_first
-        line = gather_line(pack, layer, is_layer)
-        up = gather_pair(up_keep, (up_keep, up_send), layer, is_layer)
-        down = gather_pair(down_keep, (down_keep, down_send), layer, is_layer)
-        full_out = line[:, :, 3 * wide :].reshape(planes, wide, deep)
-        return (
-            line[:, :, : 3 * wide].reshape(planes * deep, 3 * wide),
-            full_out,
-            up.reshape(planes * deep, half),
-            down,
-        )
-
-    shards = (pack, up_keep, up_send, down_keep, down_send)
-    first_weights = gather(0, *shards)
-    shards = lax.optimization_barrier((shards, first_weights[3]))[0]
-    second_weights = gather(1, *shards)
-
-    common = (gains, shifts, qv_full, up_own, slopes, positions)
-    source = [own[s].astype(F32) for s in range(seqs)]
-    grad_top = own.reshape(seqs * rows, width)
-    grad_top_pair = spread_pair(grad_top)
-    output, kept_first = forward(source, prefix, first_weights, *common)
-    carried = hop(output.astype(BF), "section", [(0, 1)]).astype(F32)
-    source = [carried[s * rows : (s + 1) * rows] for s in range(seqs)]
-    output, kept_second = forward(source, prefix, second_weights, *common)
-
+    dims = (planes, seqs, heads, size, rows, deep, half)
+    vec = jnp.concatenate([features, jnp.zeros((2, width), F32)], axis=0)
+    flat_qv = qv_full.astype(F32).reshape(2, wide)
+    qvb = jnp.stack([flat_qv[0], jnp.zeros_like(flat_qv[0]), flat_qv[1]])
+    got = run_forward(
+        dims, own.reshape(seqs * rows, width), vec, qvb, up_own[None], prefix, slopes,
+        w_qkv[0].transpose(1, 0, 2), w_out[0], w_up[0], w_down[0],
+    )
+    output, wq, wo, wu, wd, hid, mid, nb, qkv, mix, sec, up, act = got
+    R = seqs * rows
+    def per_seq(a):
+        a = a.reshape(4, seqs, rows, -1)
+        return [a[:, s].reshape(4 * rows, -1) for s in range(seqs)]
+    heads_kept = []
+    for s, v in enumerate(per_seq(qkv)):
+        q, k, w = (v[:, c * wide : (c + 1) * wide].reshape(4 * rows, heads, size) for c in range(3))
+        sc = score_block(q, k, prefix[s], slopes, positions)
+        heads_kept.append((q, k, w, jax.nn.logsumexp(sc, axis=-1)))
+    hid = hid.astype(F32)
+    kept = (
+        [hid[s * rows : (s + 1) * rows] for s in range(seqs)], per_seq(nb), heads_kept, per_seq(mix),
+        [mid[s * rows : (s + 1) * rows] for s in range(seqs)], sec.reshape(8 * R, width),
+        up.reshape(8 * R, half), act.reshape(8 * R, half),
+    )
+    full_q = wq.transpose(1, 0, 2).reshape(planes * deep, 3 * wide)
+    weights = (full_q, wo, wu, wd)
     back_common = (gains, slopes, positions, planes)
+    grad_top = own.reshape(R, width)
     grad_mid, grads_top, sums_top = backward(
-        grad_top.astype(F32), grad_top_pair, kept_second, prefix, second_weights, *back_common
-    )
-
-    def scatter(layer, grads):
-        is_layer = is_first if layer == 0 else ~is_first
+        grad_top.astype(F32), spread_pair(grad_top), kept, prefix, weights, *back_common
+    )
+    returned = hop(grad_mid.astype(BF), "section", [(1, 0)])
+    grad_low, grads_low, sums_low = backward(
+        returned.astype(F32), spread_pair(returned), kept, prefix, weights, *back_common
+    )
+
+    def scatter(grads):
         g_qkv, g_out, g_up, g_down = grads
-        down = scatter_pair(g_down, layer, is_layer)
-        up = scatter_pair(g_up.reshape(planes, deep, half), layer, is_layer)
+        down = scatter_pair(g_down)
+        up = scatter_pair(g_up.reshape(planes, deep, half))
         line = jnp.concatenate(
             [g_qkv.reshape(planes, deep, 3 * wide), g_out.reshape(planes, deep, wide)], axis=2
         )
-        line = scatter_line(line, layer, is_layer)
+        line = scatter_line(line)
         return line, up, down
 
-    scattered_top = scatter(1, grads_top)
-    returned = hop(grad_mid.astype(BF), "section", [(1, 0)])
-    grad_low, grads_low, sums_low = backward(
-        returned.astype(F32), spread_pair(returned), kept_first, prefix, first_weights, *back_common
-    )
-    scattered_low = scatter(0, grads_low)
-
-    line, up, down = jax.tree.map(lambda a, b: jnp.where(is_first, a, b), scattered_low, scattered_top)
+    line, up, down = scatter(jax.tree.map(lambda a, b: jnp.where(is_first, a, b), grads_low, grads_top))
     vectors, proj_sums, up_sums = jax.tree.map(lambda a, b: jnp.where(is_first, a, b), sums_low, sums_top)
     up_grad = jnp.where(odd, jnp.concatenate([up[1], up[0]], axis=1), jnp.concatenate(up, axis=1))
     down_grad = jnp.where(odd, jnp.concatenate([down[1], down[0]], axis=0), jnp.concatenate(down, axis=0))

time: 1720 us -> 1240 us (0.72)
  Pallas kernels: 0 us -> 341 us
  waiting for transfers between devices: 668 us -> 400 us
  starting transfers between devices: 370 us -> 127 us
  other arithmetic: 207 us -> 69.6 us
  local copies, waits for them, and re-layouts: 209 us -> 108 us
  matrix products: 211 us -> 140 us
    pallas_call x0 -> x1, Pallas kernels: none -> 341 us  [run_forward(): pl.pallas_call(functools.partial(forward_kernel, dims), out_shape=outs, i...]
    ppermute x82 -> x7, waiting for transfers between devices: 393 us -> 148 us  [hop(): return lax.ppermute(block, axis, pairs)]
    ppermute x82 -> x7, starting transfers between devices: 232 us -> 17.5 us  [hop(): return lax.ppermute(block, axis, pairs)]
    ppermute x108 -> x48, waiting for transfers between devices: 194 us -> 92.6 us  [swap(): lax.ppermute(block, axis, [(i, i ^ distance) for i in range(lax.axis_size...]
    unnamed x2, waiting for transfers between devices: 80.8 us -> 159 us
    dot_general x16 -> x0, matrix products: 54.8 us -> none  [the longest x4 15 us: forward(): branch = jnp.einsum('tf,zfd->tzd', mixed, w_out, preferred_element_type=F32)]
    dynamic_update_slice x21 -> x0, other arithmetic: 32.7 us -> none  [the longest x6 15.5 us: gather_line(): lax.dynamic_update_slice(full, both[None], (lax.rem(plane - step + count,...]
    slice x45 -> x18, local copies, waits for them, and re-layouts: 53.1 us -> 20.4 us  [the longest x8 13.3 us: on_device(): v[:, c * wide:(c + 1) * wide].reshape(4 * rows, heads, size)]
  transfers between devices with their start and end apart: 191 -> 56, of which waited for: 71 -> 22; matrix products, arithmetic and copies ran while one was open for 30% -> 17% of each run, Pallas kernels for 0% -> 28%
where the time goes in v2:
time: 1240 us; the launch traced here: 1230 us
  waiting for transfers between devices  400 us (32%)
  Pallas kernels  341 us (28%)
  matrix products  140 us (11%)
  starting transfers between devices  127 us (10%)
  local copies, waits for them, and re-layouts  108 us (9%)
  other arithmetic  69.6 us (6%)
  blocking collectives  24.7 us (2%)
  between operations  16.2 us (1%)
    pallas_call x1, Pallas kernels, run_forward(): pl.pallas_call(functools.partial(forward_kernel, dims), out_shape=outs, i...  341 us
    unnamed x2, waiting for transfers between devices  159 us
    ppermute x7, waiting for transfers between devices, hop(): return lax.ppermute(block, axis, pairs)  148 us
    ppermute x48, starting transfers between devices, swap(): lax.ppermute(block, axis, [(i, i ^ distance) for i in range(lax.axis_size...  109 us
    ppermute x48, waiting for transfers between devices, swap(): lax.ppermute(block, axis, [(i, i ^ distance) for i in range(lax.axis_size...  92.6 us
    unnamed x180, local copies, waits for them, and re-layouts  26.5 us
  transfers between devices with their start and end apart: 56, of which 22 were waited for; matrix products, arithmetic and copies ran while one was open for 17% of the time, Pallas kernels for 28%

profile of v2, /device:TPU:0, one launch (start us, length us, event | category | flops | bytes accessed | tf_op | source)
XLA Modules:
  0.0 1225.6 jit_solution(6616836664315027385)
XLA Ops:
  7.2 3.0 collective-permute-start
  14.1 24.7 %all-gather.1 = bf16[16,1,1536]{2,1,0:T(2,128)(2,1)S(1)} all-gather(bf16[1,1,1536]{2,1,0:T(2,128)(2,1)S(1)} %reshape.679), channel_id=2, replica_groups=mesh['section'=2,'dp'=4,'tensor'=4] {'dp','tensor'}, dimensions={0}, use_global_device_ids=true | all-gather | bytes 52224 | tf_op jit(solution)/shard_map/all_gather | solution.py:681
  42.1 340.7 %shard_map.169 = (f32[128,2048]{1,0:T(8,128)}, bf16[3,2048,512]{2,1,0:T(8,128)(2,1)}, bf16[4,512,512]{2,1,0:T(8,128)(2,1)}, bf16[2048,1024]{1,0:T(8,128)(2,1)}, ...) custom-call(bf16[128,2048]{1,0:T(8,128)(2,1)} %bitcast.395, ...), custom_call_target="tpu_custom_call" | custom-call | tf_op jit(solution)/shard_map/pallas_call | solution.py:576
  382.8 2.7 fusion.202
  405.9 8.0 convert_reduce_fusion
  413.9 4.6 fusion.218
  428.4 4.9 collective-permute-done.7
  437.1 10.9 collective-permute-done.10
  453.1 6.2 collective-permute-done.17
  459.6 8.9 copy.209
  475.6 3.4 fusion.68
  480.8 2.3 fusion.220
  483.2 2.9 convolution_convert_fusion.9
  486.1 2.9 convolution_convert_fusion.10
  493.3 2.4 copy.276
  495.7 3.4 fusion.67
  505.4 3.5 convolution_convert_fusion.12
  509.0 3.5 convolution_convert_fusion.13
  512.5 4.9 fusion.213
  518.0 4.6 fusion.215
  523.1 2.5 collective-permute-start.20
  527.5 5.3 collective-permute-done.20
  532.9 5.2 collective-permute-done.15
  540.7 116.0 %collective-permute-done.21 = bf16[128,2048]{1,0:T(8,128)(2,1)S(1)} collective-permute-done((bf16[128,2048]{1,0:T(8,128)(2,1)S(1)}, bf16[128,2048]{1,0:T(8,128)(2,1)S(1)}, u32[]{:S(2)}, u32[]{:S(2)}) %collective-permute-start.21) | collective-permute-done | bytes 524320 | tf_op jit(solution)/shard_map/ppermute | solution.py:16
  659.3 10.4 collective-permute-done.23
  672.4 3.9 collective-permute-done.24
  684.5 6.6 copy.280
  691.1 12.5 %convert_reduce_fusion.1 = (f32[1024]{0:T(1024)}, bf16[1024,1024]{1,0:T(8,128)(2,1)S(1)}) fusion(f32[8,128,1024]{2,1,0:T(8,128)} %get-tuple-element.23, bf16[1024,4,512]{0,2,1:T(8,128)(2,1)} %bitcast.404, bf16[4,1024,512]{2,1,0:T(8,128)(2,1)} %get-tuple-element.22), kind=kOutput, calls=%fused_computation.52 | convolution fusion | flops 4318034944 | bytes 14684160 | tf_op jit(solution)/shard_map/tzd,zfd->tf/dot_general | solution.py:621
  703.6 4.5 fusion.221
  708.2 3.3 copy-done.10
  718.4 6.7 fusion.196
  728.3 10.7 convolution_convert_fusion
  745.6 6.3 fusion.225
  751.9 3.9 collective-permute-done.32
  763.4 6.3 convert_select_fusion
  771.0 3.6 dynamic-slice_bitcast_fusion.2
  782.6 2.7 fusion.70
  793.8 2.7 fusion.69
  802.6 7.9 broadcast_select_fusion
  810.5 8.8 copy.244
  819.4 2.4 fusion.29
  823.6 3.6 collective-permute-start.43
  827.2 5.1 fusion.224
  832.4 5.0 convert_select_fusion.1
  843.8 3.7 collective-permute-done.52
  847.6 67.1 %collective-permute-start.49 = (bf16[512,1024]{1,0:T(8,128)(2,1)}, bf16[512,1024]{1,0:T(8,128)(2,1)}, u32[]{:S(2)}, u32[]{:S(2)}) collective-permute-start(bf16[512,1024]{1,0:T(8,128)(2,1)} %get-tuple-element.110), channel_id=1, source_target_pairs={{0,4},{4,0},{8,12},{12,8},{1,5},{5,1},{9,13},{13,9},{2,6},{6,2},{1... | collective-permute-start | bytes 3145736 | tf_op jit(solution)/shard_map/ppermute | solution.py:20
  918.6 3.3 collective-permute-start.44
  923.8 2.7 maximum_select_fusion.1
  926.5 5.3 copy.249
  931.9 4.8 collective-permute-done.51
  938.6 20.0 %collective-permute-done.49 = bf16[512,1024]{1,0:T(8,128)(2,1)} collective-permute-done((bf16[512,1024]{1,0:T(8,128)(2,1)}, bf16[512,1024]{1,0:T(8,128)(2,1)}, u32[]{:S(2)}, u32[]{:S(2)}) %collective-permute-start.49) | collective-permute-done | bytes 1048608 | tf_op jit(solution)/shard_map/ppermute | solution.py:20
  960.5 2.8 maximum_select_fusion
  963.4 6.1 fusion.216
  969.4 32.0 %collective-permute-done.44 = bf16[512,2048]{0,1:T(8,128)(2,1)} collective-permute-done((bf16[512,2048]{0,1:T(8,128)(2,1)}, bf16[512,2048]{0,1:T(8,128)(2,1)}, u32[]{:S(2)}, u32[]{:S(2)}) %collective-permute-start.44) | collective-permute-done | bytes 2097184 | tf_op jit(solution)/shard_map/ppermute | solution.py:16
  1001.4 3.6 add_convert_fusion.1
  1007.0 3.1 fusion.217
  1022.2 5.9 collective-permute-done.42
  1029.2 4.9 collective-permute-start.45
  1034.2 3.5 add_convert_fusion
  1041.1 2.9 fusion.80
  1044.0 159.1 %all-reduce.6.cloned.1.call-done = f32[16,1536]{1,0:T(8,128)} async-done(((f32[16,1536]{1,0:T(8,128)}), f32[16,1536]{1,0:T(8,128)}) %all-reduce.6.cloned.1.call-update) | async-done | bytes 98320
  1208.6 3.5 fusion.10
  1213.5 2.4 copy.247
  1215.8 2.5 copy.248
  (452 shorter events, 175.8 us)
Async XLA Ops:
  7.2 1196.0 %all-reduce.6.cloned.1.call-start = ((), (), s32[]{:S(2)}) async-start(), calls=%async_computation | async-start | bytes 196608
  7.2 383.7 %collective-permute-start = (bf16[128,2048]{1,0:T(8,128)(2,1)}, bf16[128,2048]{1,0:T(8,128)(2,1)S(1)}, u32[]{:S(2)}, u32[]{:S(2)}) collective-permute-start(bf16[128,2048]{1,0:T(8,128)(2,1)} %bitcast.392), channel_id=1, source_target_pairs={{0,2},{1,3},{2,0},{3,1},{4,6},{5,7},{6,4},{7,5},{8,10},{9,11},{10,... | collective-permute-start | bytes 1572872 | tf_op jit(solution)/shard_map/ppermute | solution.py:20
  10.3 379.5 %collective-permute-start.1 = (bf16[128,2048]{1,0:T(8,128)(2,1)}, bf16[128,2048]{1,0:T(8,128)(2,1)S(1)}, u32[]{:S(2)}, u32[]{:S(2)}) collective-permute-start(bf16[128,2048]{1,0:T(8,128)(2,1)} %bitcast.393), channel_id=1, source_target_pairs={{0,4},{4,0},{8,12},{12,8},{1,5},{5,1},{9,13},{13,9},{2,6},{6,2},{1... | collective-permute-start | bytes 1572872 | tf_op jit(solution)/shard_map/ppermute | solution.py:20
  11.8 391.7 %collective-permute-start.4 = (bf16[128,2048]{1,0:T(8,128)(2,1)}, bf16[128,2048]{1,0:T(8,128)(2,1)}, u32[]{:S(2)}, u32[]{:S(2)}) collective-permute-start(bf16[128,2048]{1,0:T(8,128)(2,1)} %bitcast.394), channel_id=1, source_target_pairs={{0,1},{1,0},{2,3},{3,2},{4,5},{5,4},{6,7},{7,6},{8,9},{9,8},{10,11... | collective-permute-start | bytes 1572872 | tf_op jit(solution)/shard_map/ppermute | solution.py:20
  390.4 10.5 collective-permute-start.2
  391.7 9.3 collective-permute-start.3
  402.0 3.5 collective-permute-start.5
  418.8 4.3 collective-permute-start.6
  420.3 28.8 %copy-start.56 = (f32[128]{0:T(128)}, f32[128]{0:T(128)S(1)}, u32[]{:S(2)}) copy-start(f32[128]{0:T(128)S(1)} %add_rsqrt_fusion.1) | copy-start | bytes 1540
  424.3 8.9 collective-permute-start.7
  426.4 8.3 collective-permute-start.9
  428.4 23.9 %copy-start.2 = (f32[4,256,256]{1,2,0:T(8,128)}, f32[4,256,256]{1,2,0:T(8,128)S(1)}, u32[]{:S(2)}) copy-start(f32[4,256,256]{1,2,0:T(8,128)S(1)} %get-tuple-element.169) | copy-start | bytes 3145732
  434.8 13.1 %collective-permute-start.10 = (bf16[128,2048]{1,0:T(8,128)(2,1)S(1)}, bf16[128,2048]{1,0:T(8,128)(2,1)S(1)}, u32[]{:S(2)}, u32[]{:S(2)}) collective-permute-start(bf16[128,2048]{1,0:T(8,128)(2,1)S(1)} %pad_maximum_fusion.12), channel_id=1, source_target_pairs={{0,4},{4,0},{8,12},{12,8},{1,5},{5,1},{9,13},{13,9},{2,6},{6,2},{1... | collective-permute-start | bytes 1572872 | tf_op jit(solution)/shard_map/ppermute | solution.py:20
  435.3 13.2 %collective-permute-start.8 = (bf16[128,2048]{1,0:T(8,128)(2,1)S(1)}, bf16[128,2048]{1,0:T(8,128)(2,1)S(1)}, u32[]{:S(2)}, u32[]{:S(2)}) collective-permute-start(bf16[128,2048]{1,0:T(8,128)(2,1)S(1)} %pad_maximum_fusion.11), channel_id=1, source_target_pairs={{0,2},{1,3},{2,0},{3,1},{4,6},{5,7},{6,4},{7,5},{8,10},{9,11},{10,... | collective-permute-start | bytes 1572872 | tf_op jit(solution)/shard_map/ppermute | solution.py:20
  450.7 8.6 collective-permute-start.17
  452.4 18.7 %collective-permute-start.16 = (bf16[64,2048]{1,0:T(8,128)(2,1)}, bf16[64,2048]{1,0:T(8,128)(2,1)}, u32[]{:S(2)}, u32[]{:S(2)}) collective-permute-start(bf16[64,2048]{1,0:T(8,128)(2,1)} %get-tuple-element.149), channel_id=1, source_target_pairs={{0,1},{1,0},{2,3},{3,2},{4,5},{5,4},{6,7},{7,6},{8,9},{9,8},{10,11... | collective-permute-start | bytes 786440 | tf_op jit(solution)/shard_map/ppermute | solution.py:20
  452.5 18.5 %collective-permute-start.12 = (bf16[64,2048]{1,0:T(8,128)(2,1)}, bf16[64,2048]{1,0:T(8,128)(2,1)}, u32[]{:S(2)}, u32[]{:S(2)}) collective-permute-start(bf16[64,2048]{1,0:T(8,128)(2,1)} %get-tuple-element.148), channel_id=1, source_target_pairs={{0,2},{1,3},{2,0},{3,1},{4,6},{5,7},{6,4},{7,5},{8,10},{9,11},{10,... | collective-permute-start | bytes 786440 | tf_op jit(solution)/shard_map/ppermute | solution.py:20
  459.3 11.8 collective-permute-start.18
  470.4 20.5 %collective-permute-start.11 = (bf16[64,2048]{1,0:T(8,128)(2,1)}, bf16[64,2048]{1,0:T(8,128)(2,1)}, u32[]{:S(2)}, u32[]{:S(2)}) collective-permute-start(bf16[64,2048]{1,0:T(8,128)(2,1)} %get-tuple-element.148), channel_id=1, source_target_pairs={{0,1},{1,0},{2,3},{3,2},{4,5},{5,4},{6,7},{7,6},{8,9},{9,8},{10,11... | collective-permute-start | bytes 786440 | tf_op jit(solution)/shard_map/ppermute | solution.py:20
  471.0 20.0 %collective-permute-start.13 = (bf16[64,2048]{1,0:T(8,128)(2,1)}, bf16[64,2048]{1,0:T(8,128)(2,1)}, u32[]{:S(2)}, u32[]{:S(2)}) collective-permute-start(bf16[64,2048]{1,0:T(8,128)(2,1)} %collective-permute-done.12), channel_id=1, source_target_pairs={{0,1},{1,0},{2,3},{3,2},{4,5},{5,4},{6,7},{7,6},{8,9},{9,8},{10,11... | collective-permute-start | bytes 786440 | tf_op jit(solution)/shard_map/ppermute | solution.py:20
  517.5 5.4 collective-permute-start.19
  522.8 2.9 collective-permute-start.14
  523.1 9.7 collective-permute-start.20
  525.8 12.3 %collective-permute-start.15 = (bf16[64,2048]{1,0:T(8,128)(2,1)S(1)}, bf16[64,2048]{1,0:T(8,128)(2,1)S(1)}, u32[]{:S(2)}, u32[]{:S(2)}) collective-permute-start(bf16[64,2048]{1,0:T(8,128)(2,1)S(1)} %fusion.141), channel_id=1, source_target_pairs={{0,2},{1,3},{2,0},{3,1},{4,6},{5,7},{6,4},{7,5},{8,10},{9,11},{10,... | collective-permute-start | bytes 786440 | tf_op jit(solution)/shard_map/ppermute | solution.py:20
  539.4 117.3 %collective-permute-start.21 = (bf16[128,2048]{1,0:T(8,128)(2,1)S(1)}, bf16[128,2048]{1,0:T(8,128)(2,1)S(1)}, u32[]{:S(2)}, u32[]{:S(2)}) collective-permute-start(bf16[128,2048]{1,0:T(8,128)(2,1)S(1)} %fusion.75), channel_id=1, source_target_pairs={{16,0},{17,1},{18,2},{19,3},{20,4},{21,5},{22,6},{23,7},{24,8},{25... | collective-permute-start | bytes 1572872 | tf_op jit(solution)/shard_map/ppermute | solution.py:16
  656.7 13.0 %collective-permute-start.23 = (bf16[128,2048]{1,0:T(8,128)(2,1)S(1)}, bf16[128,2048]{1,0:T(8,128)(2,1)S(1)}, u32[]{:S(2)}, u32[]{:S(2)}) collective-permute-start(bf16[128,2048]{1,0:T(8,128)(2,1)S(1)} %collective-permute-done.21), channel_id=1, source_target_pairs={{0,4},{4,0},{8,12},{12,8},{1,5},{5,1},{9,13},{13,9},{2,6},{6,2},{1... | collective-permute-start | bytes 1572872 | tf_op jit(solution)/shard_map/ppermute | solution.py:20
  657.8 13.5 %collective-permute-start.22 = (bf16[128,2048]{1,0:T(8,128)(2,1)S(1)}, bf16[128,2048]{1,0:T(8,128)(2,1)S(1)}, u32[]{:S(2)}, u32[]{:S(2)}) collective-permute-start(bf16[128,2048]{1,0:T(8,128)(2,1)S(1)} %collective-permute-done.21), channel_id=1, source_target_pairs={{0,2},{1,3},{2,0},{3,1},{4,6},{5,7},{6,4},{7,5},{8,10},{9,11},{10,... | collective-permute-start | bytes 1572872 | tf_op jit(solution)/shard_map/ppermute | solution.py:20
  669.7 6.6 collective-permute-start.24
  671.3 6.4 collective-permute-start.25
  677.9 5.4 collective-permute-start.27
  678.0 4.4 collective-permute-start.26
  713.2 5.3 collective-permute-start.28
  726.1 13.2 %collective-permute-start.29 = (bf16[64,2048]{1,0:T(8,128)(2,1)}, bf16[64,2048]{1,0:T(8,128)(2,1)}, u32[]{:S(2)}, u32[]{:S(2)}) collective-permute-start(bf16[64,2048]{1,0:T(8,128)(2,1)} %get-tuple-element.122), channel_id=1, source_target_pairs={{0,4},{4,0},{8,12},{12,8},{1,5},{5,1},{9,13},{13,9},{2,6},{6,2},{1... | collective-permute-start | bytes 786440 | tf_op jit(solution)/shard_map/ppermute | solution.py:20
  727.6 11.8 collective-permute-start.31
  742.1 13.8 %collective-permute-start.32 = (bf16[128,2048]{1,0:T(8,128)(2,1)S(1)}, bf16[128,2048]{1,0:T(8,128)(2,1)S(1)}, u32[]{:S(2)}, u32[]{:S(2)}) collective-permute-start(bf16[128,2048]{1,0:T(8,128)(2,1)S(1)} %pad_maximum_fusion.16), channel_id=1, source_target_pairs={{0,4},{4,0},{8,12},{12,8},{1,5},{5,1},{9,13},{13,9},{2,6},{6,2},{1... | collective-permute-start | bytes 1572872 | tf_op jit(solution)/shard_map/ppermute | solution.py:20
  744.1 13.5 %collective-permute-start.30 = (bf16[128,2048]{1,0:T(8,128)(2,1)S(1)}, bf16[128,2048]{1,0:T(8,128)(2,1)S(1)}, u32[]{:S(2)}, u32[]{:S(2)}) collective-permute-start(bf16[128,2048]{1,0:T(8,128)(2,1)S(1)} %pad_maximum_fusion.15), channel_id=1, source_target_pairs={{0,2},{1,3},{2,0},{3,1},{4,6},{5,7},{6,4},{7,5},{8,10},{9,11},{10,... | collective-permute-start | bytes 1572872 | tf_op jit(solution)/shard_map/ppermute | solution.py:20
  762.0 8.7 collective-permute-start.39
  769.6 8.3 collective-permute-start.38
  769.7 9.0 collective-permute-start.34
  770.6 8.1 collective-permute-start.40
  774.6 147.2 %collective-permute-start.54 = (bf16[1024,512]{0,1:T(8,128)(2,1)}, bf16[1024,512]{0,1:T(8,128)(2,1)}, u32[]{:S(2)}, u32[]{:S(2)}) collective-permute-start(bf16[1024,512]{0,1:T(8,128)(2,1)} %get-tuple-element.108), channel_id=1, source_target_pairs={{0,8},{4,12},{8,0},{12,4},{1,9},{5,13},{9,1},{13,5},{2,10},{6,14},... | collective-permute-start | bytes 3145736 | tf_op jit(solution)/shard_map/ppermute | solution.py:20
  775.8 65.8 %collective-permute-start.53 = (bf16[1024,512]{0,1:T(8,128)(2,1)}, bf16[1024,512]{0,1:T(8,128)(2,1)}, u32[]{:S(2)}, u32[]{:S(2)}) collective-permute-start(bf16[1024,512]{0,1:T(8,128)(2,1)} %get-tuple-element.109), channel_id=1, source_target_pairs={{0,12},{4,8},{8,4},{12,0},{1,13},{5,9},{9,5},{13,1},{2,14},{6,10},... | collective-permute-start | bytes 3145736 | tf_op jit(solution)/shard_map/ppermute | solution.py:20
  778.0 69.6 %collective-permute-start.52 = (bf16[1024,512]{0,1:T(8,128)(2,1)}, bf16[1024,512]{0,1:T(8,128)(2,1)}, u32[]{:S(2)}, u32[]{:S(2)}) collective-permute-start(bf16[1024,512]{0,1:T(8,128)(2,1)} %get-tuple-element.107), channel_id=1, source_target_pairs={{0,4},{4,0},{8,12},{12,8},{1,5},{5,1},{9,13},{13,9},{2,6},{6,2},{1... | collective-permute-start | bytes 3145736 | tf_op jit(solution)/shard_map/ppermute | solution.py:20
  778.8 12.5 %collective-permute-start.33 = (bf16[64,2048]{1,0:T(8,128)(2,1)}, bf16[64,2048]{1,0:T(8,128)(2,1)}, u32[]{:S(2)}, u32[]{:S(2)}) collective-permute-start(bf16[64,2048]{1,0:T(8,128)(2,1)} %get-tuple-element.146), channel_id=1, source_target_pairs={{0,1},{1,0},{2,3},{3,2},{4,5},{5,4},{6,7},{7,6},{8,9},{9,8},{10,11... | collective-permute-start | bytes 786440 | tf_op jit(solution)/shard_map/ppermute | solution.py:20
  779.5 11.8 collective-permute-start.35
  823.6 93.0 %collective-permute-start.43 = (bf16[512,2048]{0,1:T(8,128)(2,1)S(1)}, bf16[512,2048]{0,1:T(8,128)(2,1)S(1)}, u32[]{:S(2)}, u32[]{:S(2)}) collective-permute-start(bf16[512,2048]{0,1:T(8,128)(2,1)S(1)} %fusion.22), channel_id=1, source_target_pairs={{0,4},{1,5},{2,6},{3,7},{16,20},{17,21},{18,22},{19,23}} | collective-permute-start | bytes 6291464 | tf_op jit(solution)/shard_map/ppermute | solution.py:16
  840.3 96.3 %collective-permute-start.51 = (bf16[512,1024]{1,0:T(8,128)(2,1)}, bf16[512,1024]{1,0:T(8,128)(2,1)}, u32[]{:S(2)}, u32[]{:S(2)}) collective-permute-start(bf16[512,1024]{1,0:T(8,128)(2,1)} %get-tuple-element.111), channel_id=1, source_target_pairs={{0,8},{4,12},{8,0},{12,4},{1,9},{5,13},{9,1},{13,5},{2,10},{6,14},... | collective-permute-start | bytes 3145736 | tf_op jit(solution)/shard_map/ppermute | solution.py:20
  841.6 97.0 %collective-permute-start.50 = (bf16[512,1024]{1,0:T(8,128)(2,1)}, bf16[512,1024]{1,0:T(8,128)(2,1)}, u32[]{:S(2)}, u32[]{:S(2)}) collective-permute-start(bf16[512,1024]{1,0:T(8,128)(2,1)} %get-tuple-element.112), channel_id=1, source_target_pairs={{0,12},{4,8},{8,4},{12,0},{1,13},{5,9},{9,5},{13,1},{2,14},{6,10},... | collective-permute-start | bytes 3145736 | tf_op jit(solution)/shard_map/ppermute | solution.py:20
  847.6 111.0 %collective-permute-start.49 = (bf16[512,1024]{1,0:T(8,128)(2,1)}, bf16[512,1024]{1,0:T(8,128)(2,1)}, u32[]{:S(2)}, u32[]{:S(2)}) collective-permute-start(bf16[512,1024]{1,0:T(8,128)(2,1)} %get-tuple-element.110), channel_id=1, source_target_pairs={{0,4},{4,0},{8,12},{12,8},{1,5},{5,1},{9,13},{13,9},{2,6},{6,2},{1... | collective-permute-start | bytes 3145736 | tf_op jit(solution)/shard_map/ppermute | solution.py:20
  918.6 82.8 %collective-permute-start.44 = (bf16[512,2048]{0,1:T(8,128)(2,1)}, bf16[512,2048]{0,1:T(8,128)(2,1)}, u32[]{:S(2)}, u32[]{:S(2)}) collective-permute-start(bf16[512,2048]{0,1:T(8,128)(2,1)} %fusion.4), channel_id=1, source_target_pairs={{0,4},{4,8},{1,5},{5,9},{2,6},{6,10},{3,7},{7,11},{16,20},{20,24},... | collective-permute-start | bytes 6291464 | tf_op jit(solution)/shard_map/ppermute | solution.py:16
  960.5 40.9 %slice-start.2 = ((s8[6291456]{0:T(1024)(128)(4,1)}), s8[2097152]{0:T(1024)(128)(4,1)S(1)}, s32[]{:S(2)}) async-start(s8[6291456]{0:T(1024)(128)(4,1)} %bitcast.389), calls=%async_computation.3 | async-start | bytes 4194304
  963.3 38.1 %slice-start.3 = ((s8[6291456]{0:T(1024)(128)(4,1)}), s8[4194304]{0:T(1024)(128)(4,1)S(1)}, s32[]{:S(2)}) async-start(s8[6291456]{0:T(1024)(128)(4,1)} %bitcast.389), calls=%async_computation.4 | async-start | bytes 8388608
  963.3 43.6 %slice-start.4 = ((s8[6291456]{0:T(1024)(128)(4,1)}), s8[4194304]{0:T(1024)(128)(4,1)S(1)}, s32[]{:S(2)}) async-start(s8[6291456]{0:T(1024)(128)(4,1)} %bitcast.399), calls=%async_computation.5 | async-start | bytes 8388608
  969.4 37.5 %slice-start.5 = ((s8[6291456]{0:T(1024)(128)(4,1)}), s8[2097152]{0:T(1024)(128)(4,1)S(1)}, s32[]{:S(2)}) async-start(s8[6291456]{0:T(1024)(128)(4,1)} %bitcast.399), calls=%async_computation.6 | async-start | bytes 4194304
  969.4 37.5 %copy-start.48 = (bf16[4,128,256]{2,1,0:T(8,128)(2,1)S(1)}, bf16[4,128,256]{2,1,0:T(8,128)(2,1)}, u32[]{:S(2)}) copy-start(bf16[4,128,256]{2,1,0:T(8,128)(2,1)} %convolution_convert_fusion.6) | copy-start | bytes 786436
  969.4 37.6 %copy-start.49 = (bf16[4,128,256]{2,1,0:T(8,128)(2,1)S(1)}, bf16[4,128,256]{2,1,0:T(8,128)(2,1)}, u32[]{:S(2)}) copy-start(bf16[4,128,256]{2,1,0:T(8,128)(2,1)} %convolution_convert_fusion.7) | copy-start | bytes 786436
  1005.0 6.8 collective-permute-start.46
  1007.0 9.4 collective-permute-start.41
  1011.0 8.7 collective-permute-start.36
  1013.8 20.4 %collective-permute-start.47 = (bf16[512,2048]{0,1:T(8,128)(2,1)}, bf16[512,2048]{0,1:T(8,128)(2,1)}, u32[]{:S(2)}, u32[]{:S(2)}) collective-permute-start(bf16[512,2048]{0,1:T(8,128)(2,1)} %fusion.5), channel_id=1, source_target_pairs={{12,8},{8,4},{13,9},{9,5},{14,10},{10,6},{15,11},{11,7},{28,24},{2... | collective-permute-start | bytes 6291464 | tf_op jit(solution)/shard_map/ppermute | solution.py:16
  1018.9 9.2 collective-permute-start.42
  1021.0 18.0 %collective-permute-start.37 = (bf16[64,2048]{1,0:T(8,128)(2,1)S(1)}, bf16[64,2048]{1,0:T(8,128)(2,1)S(1)}, u32[]{:S(2)}, u32[]{:S(2)}) collective-permute-start(bf16[64,2048]{1,0:T(8,128)(2,1)S(1)} %fusion.131), channel_id=1, source_target_pairs={{0,2},{1,3},{2,0},{3,1},{4,6},{5,7},{6,4},{7,5},{8,10},{9,11},{10,... | collective-permute-start | bytes 786440 | tf_op jit(solution)/shard_map/ppermute | solution.py:20
  1029.2 179.3 %collective-permute-start.45 = (bf16[512,2048]{0,1:T(8,128)(2,1)}, bf16[512,2048]{0,1:T(8,128)(2,1)}, u32[]{:S(2)}, u32[]{:S(2)}) collective-permute-start(bf16[512,2048]{0,1:T(8,128)(2,1)} %get-tuple-element.85), channel_id=1, source_target_pairs={{0,4},{4,8},{8,12},{1,5},{5,9},{9,13},{2,6},{6,10},{10,14},{3,7},{... | collective-permute-start | bytes 6291464 | tf_op jit(solution)/shard_map/ppermute | solution.py:16
  1037.7 170.9 %collective-permute-start.48 = (bf16[512,2048]{0,1:T(8,128)(2,1)}, bf16[512,2048]{0,1:T(8,128)(2,1)}, u32[]{:S(2)}, u32[]{:S(2)}) collective-permute-start(bf16[512,2048]{0,1:T(8,128)(2,1)} %add_convert_fusion), channel_id=1, source_target_pairs={{12,8},{8,4},{4,0},{13,9},{9,5},{5,1},{14,10},{10,6},{6,2},{15,11}... | collective-permute-start | bytes 6291464 | tf_op jit(solution)/shard_map/ppermute | solution.py:16
  (72 other events, 471.9 us)
Sparse Core Ops, SparseCore 0:
  1041.2 161.8 all-reduce.5

commit v3 on v2

--- a/solution.py
+++ b/solution.py
@@ -10,111 +10,6 @@
 
 BF = jnp.bfloat16
 F32 = jnp.float32
-
-
-def hop(block, axis, pairs):
-    return lax.ppermute(block, axis, pairs)
-
-
-def swap(block, axis, distance):
-    return lax.ppermute(block, axis, [(i, i ^ distance) for i in range(lax.axis_size(axis))])
-
-
-def after(value, *others):
-    return lax.optimization_barrier((value,) + others)[0]
-
-
-def dslice(block, start, size, axis):
-    return lax.dynamic_slice_in_dim(block, start, size, axis)
-
-
-def layer_norm(hidden, gain, shift_vec):
-    centre = hidden - jnp.mean(hidden, axis=-1, keepdims=True)
-    spread = jnp.mean(centre * centre, axis=-1, keepdims=True)
-    return centre * lax.rsqrt(spread + 1e-05) * gain + shift_vec
-
-
-def layer_norm_back(hidden, gain, grad):
-    centre = hidden - jnp.mean(hidden, axis=-1, keepdims=True)
-    spread = jnp.mean(centre * centre, axis=-1, keepdims=True)
-    scale = lax.rsqrt(spread + 1e-05)
-    unit = centre * scale
-    scaled = grad * gain
-    inner = jnp.mean(scaled * unit, axis=-1, keepdims=True)
-    back = (scaled - jnp.mean(scaled, axis=-1, keepdims=True) - unit * inner) * scale
-    return back, jnp.sum(grad * unit, axis=0), jnp.sum(grad, axis=0)
-
-
-def spread_rows(rows):
-    other = swap(rows, "tensor", 2)
-    near = swap(rows, "tensor", 1)
-    far = swap(other, "tensor", 1)
-    return jnp.concatenate([rows, near, other, far], axis=0)
-
-
-def collect_rows(terms):
-    size = terms.shape[0] // 4
-    part = terms.reshape(4, size, -1)
-    got = swap(jnp.stack([part[1], part[3]]).astype(BF), "tensor", 1).astype(F32)
-    away = swap((part[2] + got[1]).astype(BF), "tensor", 2).astype(F32)
-    return part[0] + got[0] + away
-
-
-def spread_pair(rows):
-    size = rows.shape[0]
-    half = size // 2
-    plane = swap(rows, "dp", 1)
-    chip = swap(rows, "tensor", 2)
-    corner_a = swap(plane[:half], "tensor", 2)
-    corner_b = swap(chip[half:], "dp", 1)
-    near = swap(rows, "tensor", 1)
-    rest = jnp.concatenate([chip, plane, corner_a, corner_b], axis=0)
-    far = swap(rest, "tensor", 1)
-    return jnp.concatenate([rows, rest, near, far], axis=0)
-
-
-def collect_pair(terms):
-    size = terms.shape[0] // 8
-    half = size // 2
-    got = swap(terms[4 * size :].astype(BF), "tensor", 1).astype(F32)
-    total = terms[: 4 * size] + got
-    own, chip, plane, corner = (total[i * size : (i + 1) * size] for i in range(4))
-    one = swap(corner[:half].astype(BF), "tensor", 2).astype(F32)
-    two = swap(corner[half:].astype(BF), "dp", 1).astype(F32)
-    plane = jnp.concatenate([plane[:half] + one, plane[half:]], axis=0)
-    chip = jnp.concatenate([chip[:half], chip[half:] + two], axis=0)
-    return own + swap(chip.astype(BF), "tensor", 2).astype(F32) + swap(plane.astype(BF), "dp", 1).astype(F32)
-
-
-def scatter_line(full):
-    count = lax.axis_size("dp")
-    plane = lax.axis_index("dp")
-
-    def block(offset):
-        return dslice(full, lax.rem(plane + offset, count), 1, 0)[0]
-
-    own = block(0).astype(F32)
-    right = left = None
-    for step in range(count - 1):
-        to_right, to_left = block(count - 1 - step), block(step + 1)
-        if right is not None:
-            to_right = (to_right.astype(F32) + right.astype(F32)).astype(BF)
-            to_left = (to_left.astype(F32) + left.astype(F32)).astype(BF)
-        right = hop(to_right, "dp", [(i, i + 1) for i in range(step + 1)])
-        left = hop(to_left, "dp", [(i, i - 1) for i in range(count - 1, count - 2 - step, -1)])
-    return own + right.astype(F32) + left.astype(F32)
-
-
-def scatter_pair(full):
-    count = lax.axis_size("dp")
-    plane = lax.axis_index("dp")
-    sums = [dslice(full, plane, 1, 0)[0].astype(F32), None]
-    for distance in range(1, count):
-        piece = dslice(full, plane ^ distance, 1, 0)[0]
-        got = swap(piece, "dp", distance).astype(F32)
-        odd = distance & 1
-        sums[odd] = got if sums[odd] is None else sums[odd] + got
-    return sums
 
 
 MESH = pl.DeviceIdType.MESH
@@ -585,80 +480,606 @@
     )(x, vec, qvb, upb, prefix, slopes, wq, wo, wu, wd)
 
 
-def score_block(queries, keys, length, slopes, positions):
-    raw = jnp.einsum("qhe,khe->hqk", queries, keys, preferred_element_type=F32)
-    offsets = (positions[:, None] - positions[None, :]).astype(F32)
-    allowed = (positions[None, :] <= positions[:, None]) | (positions[None, :] < length)
-    scores = raw * queries.shape[2] ** (-0.5) - slopes[:, None, None] * offsets
-    return jnp.where(allowed, scores, -1e30)
-
-
-def attend_back(grad_mixed, kept, length, slopes, positions):
-    queries, keys, values, log_total = kept
-    seq_len, heads, size = queries.shape
-    grad_heads = grad_mixed.reshape(seq_len, heads, size)
-    scores = score_block(queries, keys, length, slopes, positions)
-    probs = jnp.exp(scores - log_total[..., None])
-    grad_probs = jnp.einsum("qhe,khe->hqk", grad_heads, values, preferred_element_type=F32)
-    inner = jnp.sum(probs * grad_probs, axis=-1, keepdims=True)
-    grad_raw = (probs * (grad_probs - inner) * size ** (-0.5)).astype(BF)
-    grad_q = jnp.einsum("hqk,khe->qhe", grad_raw, keys, preferred_element_type=F32).astype(BF)
-    grad_k = jnp.einsum("hqk,qhe->khe", grad_raw, queries, preferred_element_type=F32).astype(BF)
-    grad_v = jnp.einsum(
-        "hqk,qhe->khe", probs.astype(BF), grad_heads, preferred_element_type=F32
-    ).astype(BF)
-    return jnp.concatenate([g.reshape(seq_len, heads * size) for g in (grad_q, grad_k, grad_v)], axis=1)
-
-
-def backward(grad_out, grad_pair, kept, lengths, weights, gains, slopes, positions, planes):
-    hidden, normed, heads, mixed_all, middle, second, up, act = kept
-    w_qkv, w_out, w_up, w_down = weights
-    width = grad_out.shape[1]
-    part = width // planes
-    rows = hidden[0].shape[0]
-    grad_down_bias = jnp.sum(grad_out, axis=0)
-    blocks = grad_pair.reshape(-1, planes, part)
-    grad_act = jnp.einsum("tzd,zfd->tf", blocks, w_down, preferred_element_type=F32)
-    unused, pull = jax.vjp(lambda v: jax.nn.gelu(v, approximate=True), up)
-    grad_up = pull(grad_act)[0].astype(BF)
-    grad_second = jnp.einsum("tf,df->td", grad_up, w_up, preferred_element_type=F32)
-    grad_w_down = jnp.einsum("tf,tzd->zfd", act, blocks, preferred_element_type=F32).astype(BF)
-    grad_w_up = jnp.einsum("td,tf->df", second, grad_up, preferred_element_type=F32).astype(BF)
-    grad_up_bias = jnp.sum(grad_up.astype(F32), axis=0)
-    grad_second = collect_pair(grad_second)
-    back, gain_two, shift_two = layer_norm_back(jnp.concatenate(middle, axis=0), gains[1], grad_second)
-    grad_middle = grad_out + back
-    grad_out_bias = jnp.sum(grad_middle, axis=0)
-    grad_proj_all, grad_mid_all, grad_normed = [], [], []
-    for seq in range(len(hidden)):
-        full = spread_rows(grad_middle[seq * rows : (seq + 1) * rows].astype(BF))
-        mid = full.reshape(-1, planes, part)
-        grad_mixed = jnp.einsum("tzd,zfd->tf", mid, w_out, preferred_element_type=F32).astype(BF)
-        grad_proj = attend_back(grad_mixed, heads[seq], lengths[seq], slopes, positions)
-        term = jnp.einsum("tf,df->td", grad_proj, w_qkv, preferred_element_type=F32)
-        grad_normed.append(collect_rows(term))
-        grad_proj_all.append(grad_proj)
-        grad_mid_all.append(mid)
-    grad_proj = jnp.concatenate(grad_proj_all, axis=0)
-    grad_w_out = jnp.einsum(
-        "tf,tzd->zfd",
-        jnp.concatenate(mixed_all, axis=0),
-        jnp.concatenate(grad_mid_all, axis=0),
-        preferred_element_type=F32,
-    ).astype(BF)
-    grad_w_qkv = jnp.einsum(
-        "td,tf->df", jnp.concatenate(normed, axis=0), grad_proj, preferred_element_type=F32
-    ).astype(BF)
-    proj_sums = jnp.sum(grad_proj.astype(F32), axis=0)
-    back, gain_one, shift_one = layer_norm_back(
-        jnp.concatenate(hidden, axis=0), gains[0], jnp.concatenate(grad_normed, axis=0)
+def backward_kernel(
+    dims, top, vec, prefix, slopes, wq, wo, wu, wd, hid_in, mid_in, nb_in, qkv_in, mix_in, sec_in, up_in, act_in,
+    dh_out, gq_out, go_out, gu_out, gd_out, sums_out, proj_out, ups_out, ru, rd, rq, ro,
+    carry, grad, mid, hid, dmid, gp, gm, gu, gd, gq, go, part, own8, sc, rc, s8, r8,
+    s1, r1, sy, ry, sums, proj, ups, tmpq, tmpo,
+    load_sem, up_sem, out_sem, carry_s, carry_r, ag8_s, ag8_r, f8_s, f8_r, c8_s, c8_r, rs8_s, rs8_r,
+    ag_s, ag_r, rs_s, rs_r, ffn_s, ffn_r, att_s, att_r,
+):
+    n, seqs, heads, size, rows, deep, half = dims
+    R = seqs * rows
+    wide = heads * size
+    D = n * deep
+    sect, z, t = lax.axis_index("section"), lax.axis_index("dp"), lax.axis_index("tensor")
+    core = (sect, z, t ^ 1)
+    chip = (sect, z, t ^ 2)
+    plane = (sect, z ^ 1, t)
+    diag = (sect, z ^ 1, t ^ 2)
+    across = (1 - sect, z, t)
+    greet([(sect, z ^ k, t) for k in range(1, n)] + [core, chip, diag, across])
+    zl = z & 1
+    tile = 32
+    order = (0, 2, 1, 3)
+    targets = (None, chip, plane, diag)
+
+    def ag8(i):
+        return remote(gp.at[0], gp.at[i], ag8_s.at[i], ag8_r.at[i], targets[i])
+
+    def forward8(i):
+        return remote(gp.at[i], gp.at[4 + i], f8_s.at[i], f8_r.at[i], core)
+
+    def core8(i):
+        return remote(sc.at[i], rc.at[i], c8_s.at[i], c8_r.at[i], core)
+
+    def rs8(i):
+        return remote(s8.at[i - 1], r8.at[i - 1], rs8_s.at[i], rs8_r.at[i], targets[i])
+
+    def load(src, dst, i):
+        copy = pltpu.make_async_copy(src, dst, load_sem.at[i])
+        copy.start()
+        return copy
+
+    load_mid, load_hid = load(mid_in, mid, 0), load(hid_in, hid, 1)
+    sums[...] = jnp.zeros_like(sums)
+    proj[...] = jnp.zeros_like(proj)
+    ups[...] = jnp.zeros_like(ups)
+    over = remote(s1.at[0], carry, carry_s, carry_r, across)
+
+    def col_sum(row, value):
+        sums[row : row + 1, :] += jnp.sum(value, axis=0, keepdims=True)
+
+    def ffn(a, k):
+        i = a * (n - 1) + k - 1
+        return remote((gu, gd)[a].at[k], (ru, rd)[a].at[k - 1], ffn_s.at[i], ffn_r.at[i], (sect, z ^ k, t))
+
+    def feed(vu, vd, sec, act, dup, upb):
+        loads = [load(wu, vu, 2), load(wd, vd, 3), load(sec_in, sec, 4), load(act_in, act, 5)]
+
+        def up_load(number):
+            i, slot = order[number], number % 2
+            return [
+                pltpu.make_async_copy(up_in.at[i + 4 * b], upb.at[slot, b], up_sem.at[2 * slot + b])
+                for b in range(2)
+            ]
+
+        for number in range(2):
+            for copy in up_load(number):
+                copy.start()
+
+        @pl.when(sect == 1)
+        def _():
+            grad[...] = top[...]
+
+        @pl.when(sect == 0)
+        def _():
+            over.wait_recv()
+            grad[...] = carry[...]
+
+        gp[0] = grad[...]
+        for i in order[1:]:
+            ag8(i).start()
+        forward8(0).start()
+
+        def bias_body(j):
+            col_sum(5, grad[rows_of(j, tile), :].astype(F32))
+
+        tiles(R // tile, bias_body)
+        for copy in loads:
+            copy.wait()
+        tu = min(256, half)
+        td = min(256, D)
+
+        def group(number):
+            i, slot = order[number], number % 2
+            if i:
+                ag8(i).wait_recv()
+                forward8(i).start()
+            forward8(i).wait_recv()
+            for copy in up_load(number):
+                copy.wait()
+
+            def up_body(j):
+                cols = rows_of(j, tu)
+                got = None
+                for b in range(n):
+                    at = pl.ds(b * deep, deep)
+                    lhs = jnp.concatenate([gp[i, :, at], gp[4 + i, :, at]], axis=0)
+                    term = dot(lhs, vd[b, cols, :], NT)
+                    got = term if got is None else got + term
+                v = jnp.concatenate([upb[slot, 0, :, cols], upb[slot, 1, :, cols]], axis=0)
+                th = gelu_parts(v)
+                slope = 0.5 * (1.0 + th) + 0.5 * v * (1.0 - th * th) * np.float32(np.sqrt(2 / np.pi)) * (
+                    1.0 + np.float32(3 * 0.044715) * v * v
+                )
+                low = (got * slope).astype(BF)
+                dup[i, :, cols] = low[:R]
+                dup[4 + i, :, cols] = low[R:]
+                ups[0:1, cols] += jnp.sum(low.astype(F32), axis=0, keepdims=True)
+
+            tiles(half // tu, up_body)
+            if number + 2 < 4:
+                for copy in up_load(number + 2):
+                    copy.start()
+
+            def second_body(j):
+                cols = rows_of(j, td)
+                lhs = jnp.concatenate([dup[i], dup[4 + i]], axis=0)
+                got = dot(lhs, vu[cols, :], NT)
+                if i == 0:
+                    own8[:, cols] = got[:R]
+                else:
+                    part[slot, :, cols] = got[:R]
+                sc[i, :, cols] = got[R:].astype(BF)
+
+            tiles(D // td, second_body)
+            core8(i).start()
+
+        def reduce(number):
+            i, slot = order[number], number % 2
+            core8(i).wait_recv()
+            if i == 0:
+                return
+
+            def body(j):
+                sl = rows_of(j, tile)
+                s8[i - 1, sl, :] = (part[slot, sl, :] + rc[i, sl, :].astype(F32)).astype(BF)
+
+            tiles(R // tile, body)
+            rs8(i).start()
+
+        for number in range(4):
+            group(number)
+            if number:
+                reduce(number - 1)
+        reduce(3)
+
+        th_ = min(256, half)
+        for k in list(range(n - 1, 0, -1)) + [0]:
+            def down_body(j):
+                cols = rows_of(j, th_)
+                lhs = act[:, :, cols].reshape(8 * R, th_)
+                at = pl.ds(pl.multiple_of((z ^ k) * deep, deep), deep)
+                gd[k, cols, :] = dot(lhs, gp[:, :, at].reshape(8 * R, deep), TN).astype(BF)
+
+            tiles(half // th_, down_body)
+            dd = min(256, deep)
+
+            def up_body(j):
+                at = pl.ds(pl.multiple_of((z ^ k) * deep + j * dd, dd), dd)
+                lhs = sec[:, :, at].reshape(8 * R, dd)
+                gu[k, rows_of(j, dd), :] = dot(lhs, dup[...].reshape(8 * R, half), TN).astype(BF)
+
+            tiles(deep // dd, up_body)
+
+    pl.run_scoped(
+        feed,
+        pltpu.VMEM((D, half), BF), pltpu.VMEM((n, half, deep), BF), pltpu.VMEM((8, R, D), BF),
+        pltpu.VMEM((8, R, half), BF), pltpu.VMEM((8, R, half), BF), pltpu.VMEM((2, 2, R, half), F32),
     )
-    vectors = jnp.stack([gain_one, gain_two, shift_one, shift_two, grad_out_bias, grad_down_bias])
-    return (
-        grad_middle + back,
-        (grad_w_qkv, grad_w_out, grad_w_up, grad_w_down),
-        (vectors, proj_sums, grad_up_bias),
+    for i in order[1:]:
+        rs8(i).wait_recv()
+    for a in range(2):
+        for k in range(n - 1, 0, -1):
+            ffn(a, k).start()
+    load_mid.wait()
+    load_hid.wait()
+
+    def norm_back(value, gain, dy):
+        centre = value - jnp.mean(value, axis=-1, keepdims=True)
+        spread = jnp.mean(centre * centre, axis=-1, keepdims=True)
+        scale = lax.rsqrt(spread + 1e-05)
+        unit = centre * scale
+        scaled = dy * gain
+        inner = jnp.mean(scaled * unit, axis=-1, keepdims=True)
+        return (scaled - jnp.mean(scaled, axis=-1, keepdims=True) - unit * inner) * scale, unit
+
+    def mid_body(j):
+        sl = rows_of(j, tile)
+        dy = own8[sl, :] + rc[0, sl, :].astype(F32)
+        for i in (1, 2, 3):
+            dy = dy + r8[i - 1, sl, :].astype(F32)
+        back, unit = norm_back(mid[sl, :], vec[1:2, :], dy)
+        total = grad[sl, :].astype(F32) + back
+        dmid[sl, :] = total
+        gm[0, sl, :] = total.astype(BF)
+        col_sum(1, dy * unit)
+        col_sum(3, dy)
+        col_sum(4, total)
+
+    tiles(R // tile, mid_body)
+
+    def ag(i):
+        src, to = ((0, core), (0, chip), (2, core))[i]
+        dst = (1, 2, 3)[i]
+        return remote(gm.at[src], gm.at[dst], ag_s.at[i], ag_r.at[i], to)
+
+    ag(1).start()
+    ag(0).start()
+    to_core = remote(s1, r1, rs_s.at[0], rs_r.at[0], core)
+    to_chip = remote(sy, ry, rs_s.at[1], rs_r.at[1], chip)
+
+    def low_bit(k):
+        return k & -k
+
+    def att(k, c):
+        i = (k - 1) * 4 + c
+        src, dst = (gq.at[k, c], rq.at[k - 1, c]) if c < 3 else (go.at[k], ro.at[k - 1])
+        return remote(src, dst, att_s.at[i], att_r.at[i], (sect, z ^ low_bit(k), t))
+
+    send_order = sorted(range(1, n), key=lambda k: (low_bit(k), -k))
+
+    def attention(vq, vo, nb, qkv, mix, dmix, dqkv):
+        loads = [load(wo, vo, 2), load(qkv_in, qkv, 3), load(mix_in, mix, 4), load(nb_in, nb, 5), load(wq, vq, 6)]
+        ag(1).wait_recv()
+        ag(2).start()
+        for copy in loads:
+            copy.wait()
+        ag(0).wait_recv()
+
+        def mixed(b):
+            if b == 1:
+                ag(2).wait_recv()
+            tw = min(256, wide)
+
+            def body(j):
+                cols = rows_of(j, tw)
+                got = None
+                for p in range(n):
+                    at = pl.ds(p * deep, deep)
+                    lhs = jnp.concatenate([gm[2 * b, :, at], gm[2 * b + 1, :, at]], axis=0)
+                    term = dot(lhs, vo[p, cols, :], NT)
+                    got = term if got is None else got + term
+                low = got.astype(BF)
+                dmix[2 * b, :, cols] = low[:R]
+                dmix[2 * b + 1, :, cols] = low[R:]
+
+            tiles(wide // tw, body)
+
+        mixed(0)
+        mixed(1)
+
+        def head(i):
+            s, h = i // heads, lax.rem(i, heads)
+            pos = rows_of(s, rows)
+
+            def part_of(ref, c):
+                cols = pl.ds(pl.multiple_of(c * wide + h * size, size), size)
+                return jnp.concatenate([ref[j, pos, cols] for j in range(4)], axis=0)
+
+            q, k, v, dm = part_of(qkv, 0), part_of(qkv, 1), part_of(qkv, 2), part_of(dmix, 0)
+            scores = masked_scores(dot(q, k, NT), slopes[h], prefix[s], t, rows, size)
+            expon = jnp.exp(scores - jnp.max(scores, axis=-1, keepdims=True))
+            probs = expon / jnp.sum(expon, axis=-1, keepdims=True)
+            dp = dot(dm, v, NT)
+            inner = jnp.sum(probs * dp, axis=-1, keepdims=True)
+            raw = (probs * (dp - inner) * np.float32(size ** (-0.5))).astype(BF)
+            for c, got in enumerate((dot(raw, k), dot(raw, q, TN), dot(probs.astype(BF), dm, TN))):
+                low = got.astype(BF)
+                cols = pl.ds(pl.multiple_of(c * wide + h * size, size), size)
+                proj[0:1, cols] += jnp.sum(low.astype(F32), axis=0, keepdims=True)
+                for j in range(4):
+                    dqkv[j, pos, cols] = low[j * rows : (j + 1) * rows]
+
+        tiles(seqs * heads, head)
+
+        def normed(blocks, put):
+            td = min(256, D)
+
+            def body(j):
+                cols = rows_of(j, td)
+                got = None
+                for c in range(3):
+                    lhs = jnp.concatenate([dqkv[b, :, c * wide : (c + 1) * wide] for b in blocks], axis=0)
+                    term = dot(lhs, vq[c, cols, :], NT)
+                    got = term if got is None else got + term
+                put(cols, got)
+
+            tiles(D // td, body)
+
+        def put_send(cols, got):
+            s1[0, :, cols] = got[:R].astype(BF)
+            s1[1, :, cols] = got[R:].astype(BF)
+
+        def put_part(cols, got):
+            part[0, :, cols] = got[:R]
+            part[1, :, cols] = got[R:]
+
+        normed((3, 1), put_send)
+        to_core.start()
+        normed((2, 0), put_part)
+        to_core.wait_recv()
+
+        def add_chip(i):
+            sl = rows_of(i, tile)
+            sy[sl, :] = (part[0, sl, :] + r1[0, sl, :].astype(F32)).astype(BF)
+
+        tiles(R // tile, add_chip)
+        to_chip.start()
+        for k in send_order + [0]:
+            tw = min(256, wide)
+            at = pl.ds(pl.multiple_of((z ^ k) * deep, deep), deep)
+
+            def out_body(j):
+                cols = rows_of(j, tw)
+                lhs = mix[:, :, cols].reshape(4 * R, tw)
+                go[k, cols, :] = dot(lhs, gm[:, :, at].reshape(4 * R, deep), TN).astype(BF)
+
+            tiles(wide // tw, out_body)
+            for c in range(3):
+                def body(j):
+                    cols = rows_of(j, tw)
+                    rhs = dqkv[:, :, pl.ds(pl.multiple_of(c * wide + j * tw, tw), tw)].reshape(4 * R, tw)
+                    gq[k, c, :, cols] = dot(nb[:, :, at].reshape(4 * R, deep), rhs, TN).astype(BF)
+
+                tiles(wide // tw, body)
+            if k and low_bit(k) == 1:
+                for c in range(4):
+                    att(k, c).start()
+
+    pl.run_scoped(
+        attention,
+        pltpu.VMEM((3, D, wide), BF), pltpu.VMEM((n, wide, deep), BF), pltpu.VMEM((4, R, D), BF),
+        pltpu.VMEM((4, R, 3 * wide), BF), pltpu.VMEM((4, R, wide), BF), pltpu.VMEM((4, R, wide), BF),
+        pltpu.VMEM((4, R, 3 * wide), BF),
     )
+    to_chip.wait_recv()
+    to_core.wait_send()
+
+    def low_body(j):
+        sl = rows_of(j, tile)
+        dy = part[1, sl, :] + r1[1, sl, :].astype(F32) + ry[sl, :].astype(F32)
+        back, unit = norm_back(hid[sl, :].astype(F32), vec[0:1, :], dy)
+        total = dmid[sl, :] + back
+        dmid[sl, :] = total
+        s1[0, sl, :] = total.astype(BF)
+        col_sum(0, dy * unit)
+        col_sum(2, dy)
+
+    tiles(R // tile, low_body)
+
+    @pl.when(sect == 1)
+    def _():
+        over.start()
+
+    outs = []
+
+    def put(src, dst):
+        copy = pltpu.make_async_copy(src, dst, out_sem.at[len(outs)])
+        copy.start()
+        outs.append(copy)
+
+    put(dmid, dh_out)
+    put(sums, sums_out)
+    put(proj, proj_out)
+    put(ups, ups_out)
+
+    for k in send_order:
+        if low_bit(k) == 1:
+            continue
+        for child in send_order:
+            if child ^ low_bit(child) != k:
+                continue
+            for c in range(4):
+                att(child, c).wait_recv()
+                src = rq.at[child - 1, c] if c < 3 else ro.at[child - 1]
+                dst = tmpq if c < 3 else tmpo
+                copy = pltpu.make_async_copy(src, dst, load_sem.at[7])
+                copy.start()
+                copy.wait()
+                if c < 3:
+                    gq[k, c] = (gq[k, c].astype(F32) + tmpq[...].astype(F32)).astype(BF)
+                else:
+                    go[k] = (go[k].astype(F32) + tmpo[...].astype(F32)).astype(BF)
+                if child == [j for j in send_order if j ^ low_bit(j) == k][-1]:
+                    att(k, c).start()
+
+    def final_feed(bu, bd, fu, fd):
+        for a in range(2):
+            for k in range(n - 1, 0, -1):
+                ffn(a, k).wait_recv()
+        loads = [load(ru, bu, 2), load(rd, bd, 3)]
+        for copy in loads:
+            copy.wait()
+        step = min(64, deep)
+
+        def up_body(j):
+            sl = rows_of(j, step)
+            same = gu[0, sl, :].astype(F32)
+            other = bu[0, sl, :].astype(F32)
+            for k in range(2, n):
+                if k % 2 == 0:
+                    same = same + bu[k - 1, sl, :].astype(F32)
+                else:
+                    other = other + bu[k - 1, sl, :].astype(F32)
+            fu[0, sl, :] = same
+            fu[1, sl, :] = other
+
+        tiles(deep // step, up_body)
+
+        def down_body(j):
+            sl = rows_of(j, step)
+            same = gd[0, sl, :].astype(F32)
+            other = bd[0, sl, :].astype(F32)
+            for k in range(2, n):
+                if k % 2 == 0:
+                    same = same + bd[k - 1, sl, :].astype(F32)
+                else:
+                    other = other + bd[k - 1, sl, :].astype(F32)
+            fd[0, sl, :] = same
+            fd[1, sl, :] = other
+
+        tiles(half // step, down_body)
+        copies = []
+        for b in range(2):
+            at = pl.ds(pl.multiple_of((zl ^ b) * half, half), half)
+            copies.append(pltpu.make_async_copy(fu.at[b], gu_out.at[:, at], load_sem.at[2 + 2 * b]))
+            copies.append(pltpu.make_async_copy(fd.at[b], gd_out.at[at, :], load_sem.at[3 + 2 * b]))
+        for copy in copies:
+            copy.start()
+        for copy in copies:
+            copy.wait()
+
+    pl.run_scoped(
+        final_feed,
+        pltpu.VMEM((n - 1, deep, half), BF), pltpu.VMEM((n - 1, half, deep), BF),
+        pltpu.VMEM((2, deep, half), F32), pltpu.VMEM((2, half, deep), F32),
+    )
+
+    def final_attention(bq, bo, fq, fo):
+        last = [k for k in send_order if k == low_bit(k)]
+        for k in last:
+            for c in range(4):
+                att(k, c).wait_recv()
+        loads = [load(rq, bq, 2), load(ro, bo, 3)]
+        for copy in loads:
+            copy.wait()
+        step = min(64, deep)
+
+        def q_body(j):
+            sl = rows_of(j, step)
+            for c in range(3):
+                total = gq[0, c, sl, :].astype(F32)
+                for k in last:
+                    total = total + bq[k - 1, c, sl, :].astype(F32)
+                fq[c, sl, :] = total
+
+        tiles(deep // step, q_body)
+
+        def o_body(j):
+            sl = rows_of(j, step)
+            total = go[0, sl, :].astype(F32)
+            for k in last:
+                total = total + bo[k - 1, sl, :].astype(F32)
+            fo[sl, :] = total
+
+        tiles(wide // step, o_body)
+        copies = [
+            pltpu.make_async_copy(fq, gq_out, load_sem.at[2]),
+            pltpu.make_async_copy(fo, go_out, load_sem.at[3]),
+        ]
+        for copy in copies:
+            copy.start()
+        for copy in copies:
+            copy.wait()
+
+    pl.run_scoped(
+        final_attention,
+        pltpu.VMEM((n - 1, 3, deep, wide), BF), pltpu.VMEM((n - 1, wide, deep), BF),
+        pltpu.VMEM((3, deep, wide), F32), pltpu.VMEM((wide, deep), F32),
+    )
+
+    for i in range(4):
+        if i:
+            ag8(i).wait_send()
+            rs8(i).wait_send()
+        forward8(i).wait_send()
+        core8(i).wait_send()
+    for i in range(3):
+        ag(i).wait_send()
+    to_chip.wait_send()
+    for a in range(2):
+        for k in range(1, n):
+            ffn(a, k).wait_send()
+    for k in range(1, n):
+        for c in range(4):
+            att(k, c).wait_send()
+
+    @pl.when(sect == 1)
+    def _():
+        over.wait_send()
+
+    for copy in outs:
+        copy.wait()
+
+
+def run_backward(dims, top, vec, prefix, slopes, weights, kept):
+    n, seqs, heads, size, rows, deep, half = dims
+    R, wide, D = seqs * rows, heads * size, n * deep
+    V = lambda shape, dtype: pltpu.VMEM(shape, dtype)
+    S = lambda *shape: jax.ShapeDtypeStruct(shape[:-1], shape[-1])
+    any_ = pl.BlockSpec(memory_space=pl.ANY)
+    vm = pl.BlockSpec(memory_space=pltpu.VMEM)
+    sm = pl.BlockSpec(memory_space=pltpu.SMEM)
+    dma = lambda k: pltpu.SemaphoreType.DMA((k,))
+    one = pltpu.SemaphoreType.DMA(())
+    outs = (
+        S(R, D, F32), S(3, deep, wide, F32), S(wide, deep, F32), S(deep, 2 * half, F32), S(2 * half, deep, F32),
+        S(8, D, F32), S(1, 3 * wide, F32), S(1, half, F32),
+        S(n - 1, deep, half, BF), S(n - 1, half, deep, BF), S(n - 1, 3, deep, wide, BF), S(n - 1, wide, deep, BF),
+    )
+    scratch = [
+        V((R, D), BF), V((R, D), BF), V((R, D), F32), V((R, D), BF), V((R, D), F32),
+        V((8, R, D), BF), V((4, R, D), BF),
+        V((n, deep, half), BF), V((n, half, deep), BF), V((n, 3, deep, wide), BF), V((n, wide, deep), BF),
+        V((2, R, D), F32), V((R, D), F32), V((4, R, D), BF), V((4, R, D), BF), V((3, R, D), BF), V((3, R, D), BF),
+        V((2, R, D), BF), V((2, R, D), BF), V((R, D), BF), V((R, D), BF),
+        V((8, D), F32), V((1, 3 * wide), F32), V((1, half), F32), V((deep, wide), BF), V((wide, deep), BF),
+        dma(8), dma(4), dma(4), one, one,
+        dma(4), dma(4), dma(4), dma(4), dma(4), dma(4), dma(4), dma(4),
+        dma(3), dma(3), dma(2), dma(2), dma(2 * (n - 1)), dma(2 * (n - 1)), dma(4 * (n - 1)), dma(4 * (n - 1)),
+    ]
+    return pl.pallas_call(
+        functools.partial(backward_kernel, dims),
+        out_shape=outs,
+        in_specs=[vm, vm, sm, sm] + [any_] * 12,
+        out_specs=(any_,) * len(outs),
+        scratch_shapes=scratch,
+        compiler_params=pltpu.CompilerParams(
+            collective_id=1, has_side_effects=True, vmem_limit_bytes=62 * 1024 * 1024
+        ),
+    )(top, vec, prefix, slopes, *weights, *kept)
+
+
+def small_kernel(spread, peers, src, out, got, send_sem, recv_sem):
+    sect, z, t = lax.axis_index("section"), lax.axis_index("dp"), lax.axis_index("tensor")
+    n, m = peers
+    count = n * m
+    me = z * m + t
+
+    def peer(k):
+        other = me ^ k
+        return other, (sect, other // m, lax.rem(other, m))
+
+    greet([peer(k)[1] for k in range(1, count)])
+    copies = []
+    for k in range(1, count):
+        other, device = peer(k)
+        block = src if spread else src.at[other]
+        copies.append(remote(block, got.at[k], send_sem.at[k], recv_sem.at[k], device))
+        copies[-1].start()
+    if spread:
+        out[me] = src[...]
+    else:
+        total = src[me]
+    for k in range(1, count):
+        copies[k - 1].wait_recv()
+        if spread:
+            out[me ^ k] = got[k]
+        else:
+            total = total + got[k]
+    if not spread:
+        out[...] = total
+    for copy in copies:
+        copy.wait_send()
+
+
+def small_exchange(value, spread, peers, collective_id):
+    count = peers[0] * peers[1]
+    block = value.shape if spread else value.shape[1:]
+    return pl.pallas_call(
+        functools.partial(small_kernel, spread, peers),
+        out_shape=jax.ShapeDtypeStruct((count,) + block if spread else block, F32),
+        in_specs=[pl.BlockSpec(memory_space=pltpu.VMEM)],
+        out_specs=pl.BlockSpec(memory_space=pltpu.VMEM),
+        scratch_shapes=[
+            pltpu.VMEM((count,) + block, F32),
+            pltpu.SemaphoreType.DMA((count,)),
+            pltpu.SemaphoreType.DMA((count,)),
+        ],
+        compiler_params=pltpu.CompilerParams(collective_id=collective_id, has_side_effects=True),
+    )(value)
 
 
 def on_device(activations, ln_gains, biases, w_qkv, qv_bias, w_out, w_up, up_bias, w_down, prefix):
@@ -678,75 +1099,36 @@
     own = activations[0]
 
     flat = jnp.concatenate([v.reshape(-1) for v in (ln_gains, biases, qv_bias, up_bias)])
-    everyone = lax.all_gather(flat, ("dp", "tensor"), axis=0)
+    peers = (planes, tensors)
+    everyone = small_exchange(flat.astype(F32).reshape(-1, 128), True, peers, 2).reshape(planes * tensors, -1)
     lane = width // (planes * tensors)
     cut = 6 * lane
-    features = everyone[:, :cut].reshape(-1, 6, lane).swapaxes(0, 1).reshape(6, width).astype(F32)
-    gains, shifts = features[:2], features[2:]
+    features = everyone[:, :cut].reshape(-1, 6, lane).swapaxes(0, 1).reshape(6, width)
     mine = everyone.reshape(planes, tensors, -1)
     mine = lax.dynamic_index_in_dim(mine, place, 1, keepdims=False)[:, cut:]
     qv_full = mine[:, : 2 * heads * size_part].reshape(planes, 2, heads, size_part)
     qv_full = qv_full.transpose(1, 2, 0, 3).reshape(2, heads, size)
     up_full = mine[:, 2 * heads * size_part :].reshape(planes, up_bias.shape[1], up_bias.shape[2])
-    up_full = up_full.transpose(1, 0, 2).reshape(units).astype(F32)
+    up_full = up_full.transpose(1, 0, 2).reshape(units)
     up_own = jnp.where(odd, up_full[half:], up_full[:half])
 
     head_ids = place * heads + jnp.arange(heads)
     slopes = jnp.exp2(-8.0 * (head_ids.astype(F32) + 1.0) / (heads * tensors))
-    positions = jnp.concatenate([(place ^ j) * rows + jnp.arange(rows) for j in range(tensors)])
 
     dims = (planes, seqs, heads, size, rows, deep, half)
     vec = jnp.concatenate([features, jnp.zeros((2, width), F32)], axis=0)
-    flat_qv = qv_full.astype(F32).reshape(2, wide)
+    flat_qv = qv_full.reshape(2, wide)
     qvb = jnp.stack([flat_qv[0], jnp.zeros_like(flat_qv[0]), flat_qv[1]])
     got = run_forward(
         dims, own.reshape(seqs * rows, width), vec, qvb, up_own[None], prefix, slopes,
         w_qkv[0].transpose(1, 0, 2), w_out[0], w_up[0], w_down[0],
     )
-    output, wq, wo, wu, wd, hid, mid, nb, qkv, mix, sec, up, act = got
-    R = seqs * rows
-    def per_seq(a):
-        a = a.reshape(4, seqs, rows, -1)
-        return [a[:, s].reshape(4 * rows, -1) for s in range(seqs)]
-    heads_kept = []
-    for s, v in enumerate(per_seq(qkv)):
-        q, k, w = (v[:, c * wide : (c + 1) * wide].reshape(4 * rows, heads, size) for c in range(3))
-        sc = score_block(q, k, prefix[s], slopes, positions)
-        heads_kept.append((q, k, w, jax.nn.logsumexp(sc, axis=-1)))
-    hid = hid.astype(F32)
-    kept = (
-        [hid[s * rows : (s + 1) * rows] for s in range(seqs)], per_seq(nb), heads_kept, per_seq(mix),
-        [mid[s * rows : (s + 1) * rows] for s in range(seqs)], sec.reshape(8 * R, width),
-        up.reshape(8 * R, half), act.reshape(8 * R, half),
-    )
-    full_q = wq.transpose(1, 0, 2).reshape(planes * deep, 3 * wide)
-    weights = (full_q, wo, wu, wd)
-    back_common = (gains, slopes, positions, planes)
-    grad_top = own.reshape(R, width)
-    grad_mid, grads_top, sums_top = backward(
-        grad_top.astype(F32), spread_pair(grad_top), kept, prefix, weights, *back_common
-    )
-    returned = hop(grad_mid.astype(BF), "section", [(1, 0)])
-    grad_low, grads_low, sums_low = backward(
-        returned.astype(F32), spread_pair(returned), kept, prefix, weights, *back_common
-    )
-
-    def scatter(grads):
-        g_qkv, g_out, g_up, g_down = grads
-        down = scatter_pair(g_down)
-        up = scatter_pair(g_up.reshape(planes, deep, half))
-        line = jnp.concatenate(
-            [g_qkv.reshape(planes, deep, 3 * wide), g_out.reshape(planes, deep, wide)], axis=2
-        )
-        line = scatter_line(line)
-        return line, up, down
-
-    line, up, down = scatter(jax.tree.map(lambda a, b: jnp.where(is_first, a, b), grads_low, grads_top))
-    vectors, proj_sums, up_sums = jax.tree.map(lambda a, b: jnp.where(is_first, a, b), sums_low, sums_top)
-    up_grad = jnp.where(odd, jnp.concatenate([up[1], up[0]], axis=1), jnp.concatenate(up, axis=1))
-    down_grad = jnp.where(odd, jnp.concatenate([down[1], down[0]], axis=0), jnp.concatenate(down, axis=0))
-
-    vec = vectors.reshape(6, planes * tensors, lane).swapaxes(0, 1).reshape(planes * tensors, cut)
+    output, weights, kept = got[0], got[1:5], got[5:]
+    back = run_backward(dims, own.reshape(seqs * rows, width), vec, prefix, slopes, weights, kept)
+    grad_low, grad_q, grad_o, grad_u, grad_d, vectors, proj_sums, up_sums = back[:8]
+    proj_sums, up_sums = proj_sums[0], up_sums[0]
+
+    vec = vectors[:6].reshape(6, planes * tensors, lane).swapaxes(0, 1).reshape(planes * tensors, cut)
     qv_sums = jnp.stack([proj_sums[:wide], proj_sums[2 * wide :]]).reshape(2, heads, planes, size_part)
     qv_sums = qv_sums.transpose(2, 0, 1, 3).reshape(planes, -1)
     zero = jnp.zeros_like(up_sums)
@@ -755,7 +1137,8 @@
     own_part = jnp.concatenate([qv_sums, up_sums], axis=1)[:, None, :]
     own_part = jnp.where((jnp.arange(tensors) == place)[None, :, None], own_part, 0.0)
     message = jnp.concatenate([vec, own_part.reshape(planes * tensors, -1)], axis=1)
-    small = lax.psum_scatter(message, ("dp", "tensor"), scatter_dimension=0, tiled=False)
+    message = message.reshape(planes * tensors, -1, 128)
+    small = small_exchange(message, False, peers, 3).reshape(-1)
     mid = cut + 2 * heads * size_part
 
     ends = jnp.where(is_first, grad_low, output).reshape(seqs, rows, width)
@@ -763,12 +1146,12 @@
         ends[None],
         small[: 2 * lane].reshape(1, 2, lane),
         small[2 * lane : cut].reshape(1, 4, lane),
-        line[:, : 3 * wide].reshape(1, deep, 3, wide),
+        grad_q.transpose(1, 0, 2)[None],
         small[cut:mid].reshape(1, 2, heads, size_part),
-        line[:, 3 * wide :].reshape(1, wide, deep),
-        up_grad[None],
+        grad_o[None],
+        grad_u[None],
         small[mid:].reshape(1, up_bias.shape[1], up_bias.shape[2]),
-        down_grad[None],
+        grad_d[None],
     )
 
 

time: 1240 us -> 950 us (0.77); the launches traced: 1230 us -> 949 us
  Pallas kernels: 341 us -> 922 us
  waiting for transfers between devices: 400 us -> 0 us
  matrix products: 140 us -> 0 us
  starting transfers between devices: 127 us -> 0 us
  local copies, waits for them, and re-layouts: 108 us -> 20.2 us
  other arithmetic: 69.6 us -> 6.52 us
  blocking collectives: 24.7 us -> 0 us
  between operations: 16.2 us -> 0.83 us
    pallas_call x0 -> x3, Pallas kernels: none -> 580 us  [the longest x1 556 us: run_backward(): pl.pallas_call(functools.partial(backward_kernel, dims), out_shape=outs,...]
    ppermute x55 -> x0, waiting for transfers between devices: 241 us -> none  [the longest x7 148 us: hop(): return lax.ppermute(block, axis, pairs)]
    unnamed x2 -> x0, waiting for transfers between devices: 159 us -> none
    dot_general x38 -> x0, matrix products: 140 us -> none  [the longest x2 20.5 us: backward(): jnp.einsum('tzd,zfd->tf', blocks, w_down, preferred_element_type=F32)]
    ppermute x55 -> x0, starting transfers between devices: 127 us -> none  [the longest x48 109 us: swap(): lax.ppermute(block, axis, [(i, i ^ distance) for i in range(lax.axis_size...]
    reshape x12 -> x3, local copies, waits for them, and re-layouts: 27.8 us -> 0.17 us  [the longest x1 0.09 us: on_device(): mine[:, :2 * heads * size_part].reshape(planes, 2, heads, size_part)]
    slice x29 -> x3, local copies, waits for them, and re-layouts: 27 us -> 0.01 us  [the longest x1 0.01 us: on_device(): everyone[:, :cut].reshape(-1, 6, lane).swapaxes(0, 1).reshape(6, width)]
    all_gather x1 -> x0, blocking collectives: 24.7 us -> none  [on_device(): everyone = lax.all_gather(flat, ('dp', 'tensor'), axis=0)]
  transfers between devices with their start and end apart: 56 -> 0, of which waited for: 22 -> 0; matrix products, arithmetic and copies ran while one was open for 17% -> 0% of each run, Pallas kernels for 28% -> 0%
where the time goes in v3:
time: 950 us; the launch traced here: 949 us
  Pallas kernels  922 us (97%)
  local copies, waits for them, and re-layouts  20.2 us (2%)
    pallas_call x1, Pallas kernels, run_backward(): pl.pallas_call(functools.partial(backward_kernel, dims), out_shape=outs,...  556 us
    pallas_call x1, Pallas kernels, run_forward(): pl.pallas_call(functools.partial(forward_kernel, dims), out_shape=outs, i...  341 us
    pallas_call x2, Pallas kernels, small_exchange(): pl.pallas_call(functools.partial(small_kernel, spread, peers), out_shape=...  23.9 us

profile of v3, /device:TPU:0, one launch (start us, length us, event | category | flops | bytes accessed | tf_op | source)
XLA Modules:
  0.0 949.1 jit_solution(17110374552236613407)
XLA Ops:
  0.7 0.5 multiply_exponential_fusion.slopes
  1.2 0.1 broadcast_in_dim.44
  1.3 0.8 reshape.134
  2.1 0.1 pad.10.clone
  2.1 0.8 reshape.135
  2.9 1.3 fusion.src
  4.2 11.0 %shard_map.169 = f32[16,12,128]{2,1,0:T(8,128)} custom-call(f32[12,128]{1,0:T(8,128)} %fusion.src), custom_call_target="tpu_custom_call" | custom-call | tf_op jit(solution)/shard_map/pallas_call | solution.py:1071
  15.2 0.9 copy.34
  16.1 0.6 concatenate.21.vec
  16.8 0.9 reshape_reshape.4
  17.8 0.1 reshape.139
  17.9 0.1 slice.62
  18.0 0.1 slice.64
  18.1 0.7 pad_maximum_fusion.2.qvb
  18.7 0.1 reshape.140
  18.8 0.7 select_n.56.upb
  19.5 341.2 %shard_map.170 = (f32[128,2048]{1,0:T(8,128)}, bf16[3,2048,512]{2,1,0:T(8,128)(2,1)}, bf16[4,512,512]{2,1,0:T(8,128)(2,1)}, bf16[2048,1024]{1,0:T(8,128)(2,1)}, ...) custom-call(bf16[128,2048]{1,0:T(8,128)(2,1)} %bitcast.49, ...), custom_call_target="tpu_custom_call" | custom-call | tf_op jit(solution)/shard_map/pallas_call | solution.py:471
  360.7 556.5 %shard_map.171 = (f32[128,2048]{1,0:T(8,128)}, f32[3,512,512]{2,1,0:T(8,128)}, f32[512,512]{1,0:T(8,128)}, f32[512,2048]{1,0:T(8,128)}, f32[2048,512]{1,0:T(8,12...) custom-call(bf16[128,2048]{1,0:T(8,128)(2,1)} %bitcast.50, ...), custom_call_target="tpu_custom_call" | custom-call | tf_op jit(solution)/shard_map/pallas_call | solution.py:1023
  917.2 0.0 copy-start.4
  917.2 0.0 copy-start.2
  917.2 2.5 broadcast_select_fusion
  919.7 0.7 slice_reduce_fusion.1
  920.4 0.1 stack.13
  920.5 0.8 pad_select_fusion
  921.3 0.1 stack.14
  921.4 0.1 reshape.142
  921.5 0.1 reshape.143
  921.5 0.1 reshape.144
  921.7 0.1 broadcast_select_fusion.1
  921.8 0.0 copy-done.4
  921.8 0.7 pad_maximum_fusion.src
  922.5 12.9 %shard_map.172 = f32[12,128]{1,0:T(8,128)} custom-call(f32[16,12,128]{2,1,0:T(8,128)} %pad_maximum_fusion.src), custom_call_target="tpu_custom_call" | custom-call | tf_op jit(solution)/shard_map/pallas_call | solution.py:1071
  935.4 1.3 fusion.3
  936.8 1.3 fusion.2
  938.0 0.7 reshape.147
  938.7 0.7 reshape.148
  939.4 0.0 copy-done.2
  939.4 0.0 copy-start.3
  939.4 0.0 copy-start.1
  939.4 1.7 copy.40
  941.0 0.3 copy-done.3
  941.3 1.0 copy.41
  942.3 1.1 copy-done.1
  943.4 0.0 copy-start
  943.4 2.1 copy.42
  945.5 1.6 copy-done
  947.1 2.0 copy.43
  (21 shorter events, 0.2 us)
Async XLA Ops:
  917.2 4.6 copy-start.4
  917.2 22.2 %copy-start.2 = (f32[3,512,512]{2,1,0:T(8,128)S(1)}, f32[3,512,512]{2,1,0:T(8,128)}, u32[]{:S(2)}) copy-start(f32[3,512,512]{2,1,0:T(8,128)} %get-tuple-element.47) | copy-start | bytes 9437188
  939.4 2.0 copy-start.3
  939.4 4.0 copy-start.1
  943.4 3.7 copy-start

commit v4 on v3

--- a/solution.py
+++ b/solution.py
@@ -13,6 +13,9 @@
 
 
 MESH = pl.DeviceIdType.MESH
+RELAYED = ((3,), ())
+GRADS_RELAYED = ((), (3, 2))
+ATT_RELAYED = (0, 1, 2)
 NT = (((1,), (1,)), ((), ()))
 TN = (((0,), (0,)), ((), ()))
 
@@ -74,13 +77,18 @@
     return jnp.where(open_, scores, -1e30)
 
 
+def relayed(layer):
+    return [k for k in RELAYED[layer]]
+
+
 def forward_kernel(
     dims, x_in, vec, qvb, upb, prefix, slopes, wq_in, wo_in, wu_in, wd_in,
-    out, wq, wo, wu, wd, x_out, mid_out, nb_out, qkv_out, mix_out, sec_out, up_out, act_out,
+    out, wq, wo, wu, wd, x_out, mid_out, nb_out, qkv_out, mix_out, sec_out, up_out, act_out, top_out, lent,
     carry, carry_send, hid, mid, nb, qkv, mix, sec, up, act, outv,
     vq, vo, vu, vd, s1, r1, part, sy, ry, part8, sc, rc, s8, r8,
     line_s, line_r, pair_s, pair_r, own_sem, load_sem, keep_sem, carry_s, carry_r,
     ag_s, ag_r, rs_s, rs_r, ag8_s, ag8_r, f8_s, f8_r, c8_s, c8_r, rs8_s, rs8_r,
+    top_s, top_r, near_s, near_r, lent_s, lent_r, direct_s,
 ):
     n, seqs, heads, size, rows, deep, half = dims
     R = seqs * rows
@@ -93,7 +101,24 @@
     plane = (sect, z ^ 1, t)
     diag = (sect, z ^ 1, t ^ 2)
     across = (1 - sect, z, t)
-    greet([(sect, z ^ k, t) for k in range(1, n)] + [core, chip, diag, across])
+    greet([(s, z ^ k, t) for k in range(1, n) for s in (sect, 1 - sect)] + [core, chip, diag, across])
+
+    def lend(b):
+        at = pl.ds(pl.multiple_of(((z & 1) ^ b) * half, half), half)
+        return remote(wd_in.at[at], lent.at[at], lent_s.at[b], lent_r.at[b], across)
+
+    def on_layer(layer, body):
+        pl.when(sect == layer)(body)
+
+    def lends(layer):
+        return [b for b in range(2) if any(k & 1 == b for k in relayed(layer))]
+
+    for layer in range(2):
+        def body():
+            for b in lends(layer):
+                lend(b).start()
+
+        on_layer(layer, body)
 
     zl = z & 1
     mine = [
@@ -129,13 +154,13 @@
 
     def pair(a, k):
         h = (z ^ k) & 1
-        to = (sect, z ^ k, t)
+        to = (sect if a == 0 else 1 - sect, z ^ k, t)
         i = a * (n - 1) + k - 1
         if a == 0:
             src = wu_in.at[:, pl.ds(pl.multiple_of(h * half, half), half)]
             dst = wu.at[pl.ds(pl.multiple_of(z * deep, deep), deep)]
         else:
-            src = wd_in.at[pl.ds(pl.multiple_of(h * half, half), half)]
+            src = lent.at[pl.ds(pl.multiple_of(h * half, half), half)]
             dst = wd.at[z]
         return remote(src, dst, pair_s.at[i], pair_r.at[i], to)
 
@@ -184,6 +209,30 @@
         ag(1).wait_recv()
         ag(2).start()
 
+    def direct(k):
+        i = n - 1 + k - 1
+        src = wd_in.at[pl.ds(pl.multiple_of(((z ^ k) & 1) * half, half), half)]
+        return remote(src, wd.at[z], direct_s.at[k - 1], pair_r.at[i], (sect, z ^ k, t))
+
+    def relay(layer):
+        for b in lends(layer):
+            lend(b).wait_recv()
+        for k in relayed(layer):
+            pair(1, k).start()
+
+    def top(i):
+        return remote(x_in, top_out.at[i], top_s.at[i], top_r.at[i], (core, chip, plane, diag)[i])
+
+    def top_near(i):
+        return remote(top_out.at[i], top_out.at[4 + i], near_s.at[i], near_r.at[i], core)
+
+    top_own = pltpu.make_async_copy(x_in, top_out.at[0], own_sem.at[4])
+    top_land = [remote(x_in, top_out.at[4], top_s.at[0], top_r.at[0], core)]
+
+    @pl.when(sect == 1)
+    def _():
+        relay(0)
+
     for step in range(1, n):
         for a in range(2):
             for side in range(2):
@@ -201,9 +250,16 @@
                         make().start()
 
         if step == n - 2 or n == 2:
-            for a in range(2):
-                for k in range(n - 1, 0, -1):
-                    pair(a, k).start()
+            for k in range(n - 1, 0, -1):
+                pair(0, k).start()
+
+            for layer in range(2):
+                def body():
+                    for k in range(n - 1, 0, -1):
+                        if k not in relayed(layer):
+                            direct(k).start()
+
+                on_layer(layer, body)
 
     for copy in mine:
         copy.wait()
@@ -214,6 +270,10 @@
 
     @pl.when(sect == 1)
     def _():
+        top_own.start()
+        for i in (1, 2, 3):
+            top(i).start()
+        top_land[0].start()
         remote(carry_send, carry, carry_s, carry_r, across).wait_recv()
         hid[...] = carry[...]
         first_norm()
@@ -335,6 +395,7 @@
     for a in range(2):
         for k in range(n - 1, 0, -1):
             pair_recv(a, k).wait_recv()
+
     load_u = pltpu.make_async_copy(wu, vu, load_sem.at[2])
     load_d = pltpu.make_async_copy(wd, vd, load_sem.at[3])
     load_u.start()
@@ -410,6 +471,7 @@
     @pl.when(sect == 0)
     def _():
         over.start()
+        relay(1)
 
     keep(outv, out)
 
@@ -422,9 +484,8 @@
                 def _():
                     make().wait_send()
 
-    for a in range(2):
-        for k in range(n - 1, 0, -1):
-            pair(a, k).wait_send()
+    for k in range(n - 1, 0, -1):
+        pair(0, k).wait_send()
     for i in range(3):
         ag(i).wait_send()
     to_core.wait_send()
@@ -436,9 +497,35 @@
         forward8(i).wait_send()
         core8(i).wait_send()
 
+    for layer in range(2):
+        def body():
+            for b in lends(layer):
+                lend(b).wait_send()
+            for k in range(1, n):
+                if k not in relayed(layer):
+                    direct(k).wait_send()
+            for k in relayed(1 - layer):
+                pair(1, k).wait_send()
+
+        on_layer(layer, body)
+
     @pl.when(sect == 0)
     def _():
         over.wait_send()
+
+    @pl.when(sect == 1)
+    def _():
+        for i in (1, 2, 3):
+            top(i).wait_recv()
+            top_near(i).start()
+        top_land[0].wait_recv()
+        for i in (1, 2, 3):
+            top_near(i).wait_recv()
+        top_own.wait()
+        top_land[0].wait_send()
+        for i in (1, 2, 3):
+            top(i).wait_send()
+            top_near(i).wait_send()
 
     for copy in keeps:
         copy.wait()
@@ -456,7 +543,7 @@
     outs = (
         S(R, D, F32), S(3, D, wide, BF), S(n, wide, deep, BF), S(D, half, BF), S(n, half, deep, BF),
         S(R, D, BF), S(R, D, F32), S(4, R, D, BF), S(4, R, 3 * wide, BF), S(4, R, wide, BF),
-        S(8, R, D, BF), S(8, R, half, F32), S(8, R, half, BF),
+        S(8, R, D, BF), S(8, R, half, F32), S(8, R, half, BF), S(8, R, D, BF), S(2 * half, deep, BF),
     )
     scratch = [
         V((R, D), BF), V((R, D), BF), V((R, D), BF), V((R, D), F32), V((4, R, D), BF), V((4, R, 3 * wide), BF),
@@ -464,9 +551,10 @@
         V((3, D, wide), BF), V((n, wide, deep), BF), V((D, half), BF), V((n, half, deep), BF),
         V((2, R, D), BF), V((2, R, D), BF), V((2, R, D), F32), V((R, D), BF), V((R, D), BF),
         V((4, R, D), F32), V((4, R, D), BF), V((4, R, D), BF), V((4, R, D), BF), V((4, R, D), BF),
-        dma(4 * (n - 1)), dma(4 * (n - 1)), dma(2 * (n - 1)), dma(2 * (n - 1)), dma(4), dma(4), dma(9),
+        dma(4 * (n - 1)), dma(4 * (n - 1)), dma(2 * (n - 1)), dma(2 * (n - 1)), dma(5), dma(4), dma(9),
         pltpu.SemaphoreType.DMA(()), pltpu.SemaphoreType.DMA(()),
         dma(3), dma(3), dma(2), dma(2), dma(4), dma(4), dma(4), dma(4), dma(4), dma(4), dma(4), dma(4),
+        dma(4), dma(4), dma(4), dma(4), dma(2), dma(2), dma(n - 1),
     ]
     return pl.pallas_call(
         functools.partial(forward_kernel, dims),
@@ -481,12 +569,12 @@
 
 
 def backward_kernel(
-    dims, top, vec, prefix, slopes, wq, wo, wu, wd, hid_in, mid_in, nb_in, qkv_in, mix_in, sec_in, up_in, act_in,
-    dh_out, gq_out, go_out, gu_out, gd_out, sums_out, proj_out, ups_out, ru, rd, rq, ro,
+    dims, top, vec, prefix, slopes, wq, wo, wu, wd, hid_in, mid_in, nb_in, qkv_in, mix_in, sec_in, up_in, act_in, top_in,
+    dh_out, gq_out, go_out, gu_out, gd_out, sums_out, proj_out, ups_out, ru, rd, rq, ro, lent, lentq,
     carry, grad, mid, hid, dmid, gp, gm, gu, gd, gq, go, part, own8, sc, rc, s8, r8,
     s1, r1, sy, ry, sums, proj, ups, tmpq, tmpo,
     load_sem, up_sem, out_sem, carry_s, carry_r, ag8_s, ag8_r, f8_s, f8_r, c8_s, c8_r, rs8_s, rs8_r,
-    ag_s, ag_r, rs_s, rs_r, ffn_s, ffn_r, att_s, att_r,
+    ag_s, ag_r, rs_s, rs_r, ffn_s, ffn_r, att_s, att_r, lent_s, lent_r, lentq_s, lentq_r, over_s,
 ):
     n, seqs, heads, size, rows, deep, half = dims
     R = seqs * rows
@@ -498,7 +586,7 @@
     plane = (sect, z ^ 1, t)
     diag = (sect, z ^ 1, t ^ 2)
     across = (1 - sect, z, t)
-    greet([(sect, z ^ k, t) for k in range(1, n)] + [core, chip, diag, across])
+    greet([(s, z ^ k, t) for k in range(1, n) for s in (sect, 1 - sect)] + [core, chip, diag, across])
     zl = z & 1
     tile = 32
     order = (0, 2, 1, 3)
@@ -532,7 +620,20 @@
 
     def ffn(a, k):
         i = a * (n - 1) + k - 1
-        return remote((gu, gd)[a].at[k], (ru, rd)[a].at[k - 1], ffn_s.at[i], ffn_r.at[i], (sect, z ^ k, t))
+        to = (sect if a == 0 else 1 - sect, z ^ k, t)
+        src = gu.at[k] if a == 0 else lent.at[k - 1]
+        return remote(src, (ru, rd)[a].at[k - 1], ffn_s.at[i], ffn_r.at[i], to)
+
+    def direct(k):
+        return remote(gd.at[k], rd.at[k - 1], lent_s.at[k - 1], ffn_r.at[n - 1 + k - 1], (sect, z ^ k, t))
+
+    def lend(k):
+        return remote(gd.at[k], lent.at[k - 1], lent_s.at[k - 1], lent_r.at[k - 1], across)
+
+    def relay(layer):
+        for k in GRADS_RELAYED[layer]:
+            lend(k).wait_recv()
+            ffn(1, k).start()
 
     def feed(vu, vd, sec, act, dup, upb):
         loads = [load(wu, vu, 2), load(wd, vd, 3), load(sec_in, sec, 4), load(act_in, act, 5)]
@@ -548,19 +649,23 @@
             for copy in up_load(number):
                 copy.start()
 
+        load_top = pltpu.make_async_copy(top_in, gp, load_sem.at[6])
+
         @pl.when(sect == 1)
         def _():
+            load_top.start()
             grad[...] = top[...]
+            load_top.wait()
 
         @pl.when(sect == 0)
         def _():
+            relay(1)
             over.wait_recv()
             grad[...] = carry[...]
-
-        gp[0] = grad[...]
-        for i in order[1:]:
-            ag8(i).start()
-        forward8(0).start()
+            gp[0] = grad[...]
+            for i in order[1:]:
+                ag8(i).start()
+            forward8(0).start()
 
         def bias_body(j):
             col_sum(5, grad[rows_of(j, tile), :].astype(F32))
@@ -573,10 +678,14 @@
 
         def group(number):
             i, slot = order[number], number % 2
-            if i:
-                ag8(i).wait_recv()
-                forward8(i).start()
-            forward8(i).wait_recv()
+
+            @pl.when(sect == 0)
+            def _():
+                if i:
+                    ag8(i).wait_recv()
+                    forward8(i).start()
+                forward8(i).wait_recv()
+
             for copy in up_load(number):
                 copy.wait()
 
@@ -660,9 +769,13 @@
     )
     for i in order[1:]:
         rs8(i).wait_recv()
-    for a in range(2):
-        for k in range(n - 1, 0, -1):
-            ffn(a, k).start()
+    for layer in range(2):
+        @pl.when(sect == layer)
+        def _():
+            for k in range(n - 1, 0, -1):
+                (lend if k in GRADS_RELAYED[layer] else direct)(k).start()
+                ffn(0, k).start()
+
     load_mid.wait()
     load_hid.wait()
 
@@ -708,6 +821,33 @@
         src, dst = (gq.at[k, c], rq.at[k - 1, c]) if c < 3 else (go.at[k], ro.at[k - 1])
         return remote(src, dst, att_s.at[i], att_r.at[i], (sect, z ^ low_bit(k), t))
 
+    def att_lend(k, c):
+        i = (k - 1) * 4 + c
+        return remote(gq.at[k, c], lentq.at[k - 1, c], lentq_s.at[i], lentq_r.at[i], across)
+
+    def att_relay(k, c):
+        i = (k - 1) * 4 + c
+        to = (1 - sect, z ^ low_bit(k), t)
+        return remote(lentq.at[k - 1, c], rq.at[k - 1, c], over_s.at[i], att_r.at[i], to)
+
+    def att_start(k, c):
+        if c not in ATT_RELAYED:
+            att(k, c).start()
+            return
+
+        @pl.when(sect == 0)
+        def _():
+            att_lend(k, c).start()
+
+        @pl.when(sect == 1)
+        def _():
+            att(k, c).start()
+
+    def at_once(k):
+        return k > 1 and low_bit(k) == 1
+
+    att_order = [k for k in range(n - 1, 1, -1) if k & 1]
+    att_order += sorted((k for k in range(2, n, 2)), key=lambda k: (low_bit(k), -k)) + [1]
     send_order = sorted(range(1, n), key=lambda k: (low_bit(k), -k))
 
     def attention(vq, vo, nb, qkv, mix, dmix, dqkv):
@@ -739,6 +879,18 @@
 
         mixed(0)
         mixed(1)
+        tw = min(256, wide)
+        for k in send_order + [0]:
+            at = pl.ds(pl.multiple_of((z ^ k) * deep, deep), deep)
+
+            def out_body(j):
+                cols = rows_of(j, tw)
+                lhs = mix[:, :, cols].reshape(4 * R, tw)
+                go[k, cols, :] = dot(lhs, gm[:, :, at].reshape(4 * R, deep), TN).astype(BF)
+
+            tiles(wide // tw, out_body)
+            if at_once(k):
+                att_start(k, 3)
 
         def head(i):
             s, h = i // heads, lax.rem(i, heads)
@@ -786,37 +938,41 @@
             part[0, :, cols] = got[:R]
             part[1, :, cols] = got[R:]
 
-        normed((3, 1), put_send)
-        to_core.start()
-        normed((2, 0), put_part)
-        to_core.wait_recv()
-
-        def add_chip(i):
-            sl = rows_of(i, tile)
-            sy[sl, :] = (part[0, sl, :] + r1[0, sl, :].astype(F32)).astype(BF)
-
-        tiles(R // tile, add_chip)
-        to_chip.start()
-        for k in send_order + [0]:
-            tw = min(256, wide)
-            at = pl.ds(pl.multiple_of((z ^ k) * deep, deep), deep)
-
-            def out_body(j):
-                cols = rows_of(j, tw)
-                lhs = mix[:, :, cols].reshape(4 * R, tw)
-                go[k, cols, :] = dot(lhs, gm[:, :, at].reshape(4 * R, deep), TN).astype(BF)
-
-            tiles(wide // tw, out_body)
-            for c in range(3):
-                def body(j):
-                    cols = rows_of(j, tw)
-                    rhs = dqkv[:, :, pl.ds(pl.multiple_of(c * wide + j * tw, tw), tw)].reshape(4 * R, tw)
-                    gq[k, c, :, cols] = dot(nb[:, :, at].reshape(4 * R, deep), rhs, TN).astype(BF)
-
-                tiles(wide // tw, body)
-            if k and low_bit(k) == 1:
-                for c in range(4):
-                    att(k, c).start()
+        def normed_all():
+            normed((3, 1), put_send)
+            to_core.start()
+            normed((2, 0), put_part)
+            to_core.wait_recv()
+
+            def add_chip(i):
+                sl = rows_of(i, tile)
+                sy[sl, :] = (part[0, sl, :] + r1[0, sl, :].astype(F32)).astype(BF)
+
+            tiles(R // tile, add_chip)
+            to_chip.start()
+
+        def grads_q():
+            for k in send_order + [0]:
+                at = pl.ds(pl.multiple_of((z ^ k) * deep, deep), deep)
+                for c in range(3):
+                    def body(j):
+                        cols = rows_of(j, tw)
+                        rhs = dqkv[:, :, pl.ds(pl.multiple_of(c * wide + j * tw, tw), tw)].reshape(4 * R, tw)
+                        gq[k, c, :, cols] = dot(nb[:, :, at].reshape(4 * R, deep), rhs, TN).astype(BF)
+
+                    tiles(wide // tw, body)
+                    if at_once(k):
+                        att_start(k, c)
+
+        @pl.when(sect == 0)
+        def _():
+            grads_q()
+            normed_all()
+
+        @pl.when(sect == 1)
+        def _():
+            normed_all()
+            grads_q()
 
     pl.run_scoped(
         attention,
@@ -873,7 +1029,18 @@
                 else:
                     go[k] = (go[k].astype(F32) + tmpo[...].astype(F32)).astype(BF)
                 if child == [j for j in send_order if j ^ low_bit(j) == k][-1]:
-                    att(k, c).start()
+                    att_start(k, c)
+
+    for c in range(4):
+        att_start(1, c)
+
+    @pl.when(sect == 1)
+    def _():
+        relay(0)
+        for k in att_order:
+            for c in ATT_RELAYED:
+                att_lend(k, c).wait_recv()
+                att_relay(k, c).start()
 
     def final_feed(bu, bd, fu, fd):
         for a in range(2):
@@ -971,20 +1138,42 @@
     )
 
     for i in range(4):
+        @pl.when(sect == 0)
+        def _():
+            if i:
+                ag8(i).wait_send()
+            forward8(i).wait_send()
+
         if i:
-            ag8(i).wait_send()
             rs8(i).wait_send()
-        forward8(i).wait_send()
         core8(i).wait_send()
     for i in range(3):
         ag(i).wait_send()
     to_chip.wait_send()
-    for a in range(2):
-        for k in range(1, n):
-            ffn(a, k).wait_send()
+    for layer in range(2):
+        @pl.when(sect == layer)
+        def _():
+            for k in range(1, n):
+                ffn(0, k).wait_send()
+                (lend if k in GRADS_RELAYED[layer] else direct)(k).wait_send()
+            for k in GRADS_RELAYED[1 - layer]:
+                ffn(1, k).wait_send()
+
     for k in range(1, n):
         for c in range(4):
-            att(k, c).wait_send()
+            if c not in ATT_RELAYED:
+                att(k, c).wait_send()
+                continue
+
+            @pl.when(sect == 0)
+            def _():
+                att_lend(k, c).wait_send()
+
+            @pl.when(sect == 1)
+            def _():
+                att(k, c).wait_send()
+                att_relay(k, c).wait_send()
+
 
     @pl.when(sect == 1)
     def _():
@@ -1008,6 +1197,7 @@
         S(R, D, F32), S(3, deep, wide, F32), S(wide, deep, F32), S(deep, 2 * half, F32), S(2 * half, deep, F32),
         S(8, D, F32), S(1, 3 * wide, F32), S(1, half, F32),
         S(n - 1, deep, half, BF), S(n - 1, half, deep, BF), S(n - 1, 3, deep, wide, BF), S(n - 1, wide, deep, BF),
+        S(n - 1, half, deep, BF), S(n - 1, 3, deep, wide, BF),
     )
     scratch = [
         V((R, D), BF), V((R, D), BF), V((R, D), F32), V((R, D), BF), V((R, D), F32),
@@ -1018,12 +1208,13 @@
         V((8, D), F32), V((1, 3 * wide), F32), V((1, half), F32), V((deep, wide), BF), V((wide, deep), BF),
         dma(8), dma(4), dma(4), one, one,
         dma(4), dma(4), dma(4), dma(4), dma(4), dma(4), dma(4), dma(4),
-        dma(3), dma(3), dma(2), dma(2), dma(2 * (n - 1)), dma(2 * (n - 1)), dma(4 * (n - 1)), dma(4 * (n - 1)),
+        dma(3), dma(3), dma(2), dma(2), dma(2 * (n - 1)), dma(2 * (n - 1)), dma(4 * (n - 1)), dma(4 * (n - 1)), dma(n - 1), dma(n - 1),
+        dma(4 * (n - 1)), dma(4 * (n - 1)), dma(4 * (n - 1)),
     ]
     return pl.pallas_call(
         functools.partial(backward_kernel, dims),
         out_shape=outs,
-        in_specs=[vm, vm, sm, sm] + [any_] * 12,
+        in_specs=[vm, vm, sm, sm] + [any_] * 13,
         out_specs=(any_,) * len(outs),
         scratch_shapes=scratch,
         compiler_params=pltpu.CompilerParams(
@@ -1123,7 +1314,7 @@
         dims, own.reshape(seqs * rows, width), vec, qvb, up_own[None], prefix, slopes,
         w_qkv[0].transpose(1, 0, 2), w_out[0], w_up[0], w_down[0],
     )
-    output, weights, kept = got[0], got[1:5], got[5:]
+    output, weights, kept = got[0], got[1:5], got[5:14]
     back = run_backward(dims, own.reshape(seqs * rows, width), vec, prefix, slopes, weights, kept)
     grad_low, grad_q, grad_o, grad_u, grad_d, vectors, proj_sums, up_sums = back[:8]
     proj_sums, up_sums = proj_sums[0], up_sums[0]

time: 950 us -> 892 us (0.939)
  Pallas kernels: 922 us -> 864 us
    pallas_call x1, Pallas kernels: 556 us -> 524 us  [run_backward(): pl.pallas_call(functools.partial(backward_kernel, dims), out_shape=outs,...]
    pallas_call x1, Pallas kernels: 341 us -> 320 us  [run_forward(): pl.pallas_call(functools.partial(forward_kernel, dims), out_shape=outs, i...]
where the time goes in v4:
time: 892 us; the launch traced here: 891 us
  Pallas kernels  864 us (97%)
  local copies, waits for them, and re-layouts  20.2 us (2%)
    pallas_call x1, Pallas kernels, run_backward(): pl.pallas_call(functools.partial(backward_kernel, dims), out_shape=outs,...  524 us
    pallas_call x1, Pallas kernels, run_forward(): pl.pallas_call(functools.partial(forward_kernel, dims), out_shape=outs, i...  320 us
    pallas_call x2, Pallas kernels, small_exchange(): pl.pallas_call(functools.partial(small_kernel, spread, peers), out_shape=...  20 us

profile of v4, /device:TPU:0, one launch (start us, length us, event | category | flops | bytes accessed | tf_op | source)
XLA Modules:
  0.0 891.1 jit_solution(8800851005860273504)
XLA Ops:
  0.7 0.5 multiply_exponential_fusion.slopes
  1.2 0.1 broadcast_in_dim.44
  1.3 0.8 reshape.134
  2.1 0.1 pad.10.clone
  2.1 0.8 reshape.135
  2.9 1.3 fusion.src
  4.2 11.0 %shard_map.169 = f32[16,12,128]{2,1,0:T(8,128)} custom-call(f32[12,128]{1,0:T(8,128)} %fusion.src), custom_call_target="tpu_custom_call" | custom-call | tf_op jit(solution)/shard_map/pallas_call | solution.py:1262
  15.2 0.9 copy.34
  16.1 0.6 concatenate.21.vec
  16.8 0.9 reshape_reshape.4
  17.8 0.1 reshape.139
  17.9 0.1 slice.62
  18.0 0.1 slice.64
  18.1 0.7 pad_maximum_fusion.2.qvb
  18.7 0.1 reshape.140
  18.8 0.7 select_n.56.upb
  19.5 319.8 %shard_map.170 = (f32[128,2048]{1,0:T(8,128)}, bf16[3,2048,512]{2,1,0:T(8,128)(2,1)}, bf16[4,512,512]{2,1,0:T(8,128)(2,1)}, bf16[2048,1024]{1,0:T(8,128)(2,1)}, ...) custom-call(bf16[128,2048]{1,0:T(8,128)(2,1)} %bitcast.49, ...), custom_call_target="tpu_custom_call" | custom-call | tf_op jit(solution)/shard_map/pallas_call | solution.py:559
  339.3 523.7 %shard_map.171 = (f32[128,2048]{1,0:T(8,128)}, f32[3,512,512]{2,1,0:T(8,128)}, f32[512,512]{1,0:T(8,128)}, f32[512,2048]{1,0:T(8,128)}, f32[2048,512]{1,0:T(8,12...) custom-call(bf16[128,2048]{1,0:T(8,128)(2,1)} %bitcast.50, ...), custom_call_target="tpu_custom_call" | custom-call | tf_op jit(solution)/shard_map/pallas_call | solution.py:1214
  863.1 0.0 copy-start.4
  863.1 0.0 copy-start.2
  863.1 2.5 broadcast_select_fusion
  865.6 0.7 slice_reduce_fusion.1
  866.3 0.1 stack.13
  866.4 0.8 pad_select_fusion
  867.1 0.1 stack.14
  867.2 0.1 reshape.142
  867.3 0.1 reshape.143
  867.4 0.1 reshape.144
  867.6 0.1 broadcast_select_fusion.1
  867.7 0.0 copy-done.4
  867.7 0.7 pad_maximum_fusion.src
  868.4 9.1 %shard_map.172 = f32[12,128]{1,0:T(8,128)} custom-call(f32[16,12,128]{2,1,0:T(8,128)} %pad_maximum_fusion.src), custom_call_target="tpu_custom_call" | custom-call | tf_op jit(solution)/shard_map/pallas_call | solution.py:1262
  877.4 1.3 fusion.3
  878.7 1.3 fusion.2
  880.0 0.7 reshape.147
  880.7 0.7 reshape.148
  881.4 0.0 copy-done.2
  881.4 0.0 copy-start.3
  881.4 0.0 copy-start.1
  881.4 1.7 copy.40
  883.0 0.3 copy-done.3
  883.3 1.0 copy.41
  884.3 1.1 copy-done.1
  885.4 0.0 copy-start
  885.4 2.1 copy.42
  887.5 1.6 copy-done
  889.1 2.0 copy.43
  (21 shorter events, 0.2 us)
Async XLA Ops:
  863.1 4.6 copy-start.4
  863.1 18.3 %copy-start.2 = (f32[3,512,512]{2,1,0:T(8,128)S(1)}, f32[3,512,512]{2,1,0:T(8,128)}, u32[]{:S(2)}) copy-start(f32[3,512,512]{2,1,0:T(8,128)} %get-tuple-element.49) | copy-start | bytes 9437188
  881.4 2.0 copy-start.3
  881.4 4.0 copy-start.1
  885.4 3.7 copy-start

commit v5 on v4

--- a/solution.py
+++ b/solution.py
@@ -81,14 +81,24 @@
     return [k for k in RELAYED[layer]]
 
 
+def peers_of(n):
+    sect, z, t = lax.axis_index("section"), lax.axis_index("dp"), lax.axis_index("tensor")
+    return [(sect, z ^ (k // 4), t ^ (k % 4)) for k in range(1, 4 * n)]
+
+
+def note_copy(n, k, src, dst, send_sem, recv_sem):
+    return remote(src, dst.at[k], send_sem.at[k], recv_sem.at[k], peers_of(n)[k - 1])
+
+
 def forward_kernel(
-    dims, x_in, vec, qvb, upb, prefix, slopes, wq_in, wo_in, wu_in, wd_in,
-    out, wq, wo, wu, wd, x_out, mid_out, nb_out, qkv_out, mix_out, sec_out, up_out, act_out, top_out, lent,
+    dims, x_in, note, prefix, slopes, wq_in, wo_in, wu_in, wd_in,
+    out, wq, wo, wu, wd, x_out, mid_out, nb_out, qkv_out, mix_out, sec_out, up_out, act_out, top_out, lent, vec_out,
+    notes, panel, vec, qvb, upb, note_s, note_r,
     carry, carry_send, hid, mid, nb, qkv, mix, sec, up, act, outv,
     vq, vo, vu, vd, s1, r1, part, sy, ry, part8, sc, rc, s8, r8,
     line_s, line_r, pair_s, pair_r, own_sem, load_sem, keep_sem, carry_s, carry_r,
     ag_s, ag_r, rs_s, rs_r, ag8_s, ag8_r, f8_s, f8_r, c8_s, c8_r, rs8_s, rs8_r,
-    top_s, top_r, near_s, near_r, lent_s, lent_r, direct_s,
+    top_s, top_r, near_s, near_r, lent_s, lent_r, direct_s, cor_s, cor_r,
 ):
     n, seqs, heads, size, rows, deep, half = dims
     R = seqs * rows
@@ -101,7 +111,10 @@
     plane = (sect, z ^ 1, t)
     diag = (sect, z ^ 1, t ^ 2)
     across = (1 - sect, z, t)
-    greet([(s, z ^ k, t) for k in range(1, n) for s in (sect, 1 - sect)] + [core, chip, diag, across])
+    greet(peers_of(n) + [(1 - sect, z ^ k, t) for k in range(n)])
+    share = [note_copy(n, k, note, notes, note_s, note_r) for k in range(1, 4 * n)]
+    for copy in share:
+        copy.start()
 
     def lend(b):
         at = pl.ds(pl.multiple_of(((z & 1) ^ b) * half, half), half)
@@ -185,6 +198,31 @@
     for copy in mine:
         copy.start()
 
+    def vectors():
+        for copy in share:
+            copy.wait_recv()
+        notes[0] = note[...]
+        panel[...] = jnp.zeros_like(panel)
+        me = z * 4 + t
+        lane = D // (4 * n)
+        for k in range(4 * n):
+            panel[((me ^ k) * lane) // 128] += notes[k, 0:8, :]
+        for j in range(D // 128):
+            vec[:, j * 128 : (j + 1) * 128] = panel[j]
+        low = notes[0, 8:32, :]
+        for k in range(4, 4 * n, 4):
+            low = low + notes[k, 8:32, :]
+        qvb[...] = jnp.zeros_like(qvb)
+        for h in range(heads):
+            for c in range(2):
+                qvb[2 * c : 2 * c + 1, h * size : (h + 1) * size] = low[c * heads + h : c * heads + h + 1, :]
+        count = half // 128
+        first = low[2 * heads : 2 * heads + count]
+        later = low[2 * heads + count : 2 * heads + 2 * count]
+        units = jnp.where(zl == 1, later, first)
+        for j in range(count):
+            upb[0:1, j * 128 : (j + 1) * 128] = units[j : j + 1, :]
+
     tile = 32
 
     def first_norm():
@@ -199,6 +237,8 @@
         src, to = ((0, core), (0, chip), (2, core))[i]
         dst = (1, 2, 3)[i]
         return remote(nb.at[src], nb.at[dst], ag_s.at[i], ag_r.at[i], to)
+
+    vectors()
 
     @pl.when(sect == 0)
     def _():
@@ -295,6 +335,7 @@
 
     keep(hid, x_out)
     keep(nb, nb_out)
+    keep(vec, vec_out)
 
     tn = min(256, wide)
     for c in range(3):
@@ -378,6 +419,10 @@
     def ag8(i):
         return remote(sec.at[0], sec.at[i], ag8_s.at[i], ag8_r.at[i], targets[i])
 
+    def corner8(i):
+        at = pl.ds(i * (R // 2), R // 2)
+        return remote(sec.at[2 - i, at], sec.at[3, at], cor_s.at[i], cor_r.at[i], (chip, plane)[i])
+
     def forward8(i):
         return remote(sec.at[i], sec.at[4 + i], f8_s.at[i], f8_r.at[i], core)
 
@@ -388,7 +433,7 @@
         return remote(s8.at[i], r8.at[i], rs8_s.at[i], rs8_r.at[i], targets[i])
 
     order = (0, 2, 1, 3)
-    for i in order[1:]:
+    for i in order[1:3]:
         ag8(i).start()
     forward8(0).start()
 
@@ -406,9 +451,15 @@
     tu = min(256, half)
 
     def group(i):
-        if i:
-            ag8(i).wait_recv()
-            forward8(i).start()
+        if i == order[1]:
+            for k, side in ((2, 0), (1, 1)):
+                ag8(k).wait_recv()
+                corner8(side).start()
+                forward8(k).start()
+        if i == 3:
+            corner8(0).wait_recv()
+            corner8(1).wait_recv()
+            forward8(3).start()
         forward8(i).wait_recv()
 
         def up_body(j):
@@ -475,6 +526,8 @@
 
     keep(outv, out)
 
+    for copy in share:
+        copy.wait_send()
     for step in range(1, n):
         for a in range(2):
             for side in range(2):
@@ -491,8 +544,10 @@
     to_core.wait_send()
     to_chip.wait_send()
     for i in range(4):
+        if i in (1, 2):
+            ag8(i).wait_send()
+            corner8(i - 1).wait_send()
         if i:
-            ag8(i).wait_send()
             rs8(i).wait_send()
         forward8(i).wait_send()
         core8(i).wait_send()
@@ -531,7 +586,7 @@
         copy.wait()
 
 
-def run_forward(dims, x, vec, qvb, upb, prefix, slopes, wq, wo, wu, wd):
+def run_forward(dims, x, note, prefix, slopes, wq, wo, wu, wd):
     n, seqs, heads, size, rows, deep, half = dims
     R, wide, D = seqs * rows, heads * size, n * deep
     V = lambda shape, dtype: pltpu.VMEM(shape, dtype)
@@ -543,38 +598,40 @@
     outs = (
         S(R, D, F32), S(3, D, wide, BF), S(n, wide, deep, BF), S(D, half, BF), S(n, half, deep, BF),
         S(R, D, BF), S(R, D, F32), S(4, R, D, BF), S(4, R, 3 * wide, BF), S(4, R, wide, BF),
-        S(8, R, D, BF), S(8, R, half, F32), S(8, R, half, BF), S(8, R, D, BF), S(2 * half, deep, BF),
+        S(8, R, D, BF), S(8, R, half, F32), S(8, R, half, BF), S(8, R, D, BF), S(2 * half, deep, BF), S(8, D, F32),
     )
     scratch = [
+        V((4 * n, 32, 128), F32), V((D // 128, 8, 128), F32), V((8, D), F32), V((4, wide), F32), V((1, half), F32),
+        dma(4 * n), dma(4 * n),
         V((R, D), BF), V((R, D), BF), V((R, D), BF), V((R, D), F32), V((4, R, D), BF), V((4, R, 3 * wide), BF),
         V((4, R, wide), BF), V((8, R, D), BF), V((8, R, half), F32), V((8, R, half), BF), V((R, D), F32),
         V((3, D, wide), BF), V((n, wide, deep), BF), V((D, half), BF), V((n, half, deep), BF),
         V((2, R, D), BF), V((2, R, D), BF), V((2, R, D), F32), V((R, D), BF), V((R, D), BF),
         V((4, R, D), F32), V((4, R, D), BF), V((4, R, D), BF), V((4, R, D), BF), V((4, R, D), BF),
-        dma(4 * (n - 1)), dma(4 * (n - 1)), dma(2 * (n - 1)), dma(2 * (n - 1)), dma(5), dma(4), dma(9),
+        dma(4 * (n - 1)), dma(4 * (n - 1)), dma(2 * (n - 1)), dma(2 * (n - 1)), dma(5), dma(4), dma(10),
         pltpu.SemaphoreType.DMA(()), pltpu.SemaphoreType.DMA(()),
         dma(3), dma(3), dma(2), dma(2), dma(4), dma(4), dma(4), dma(4), dma(4), dma(4), dma(4), dma(4),
-        dma(4), dma(4), dma(4), dma(4), dma(2), dma(2), dma(n - 1),
+        dma(4), dma(4), dma(4), dma(4), dma(2), dma(2), dma(n - 1), dma(2), dma(2),
     ]
     return pl.pallas_call(
         functools.partial(forward_kernel, dims),
         out_shape=outs,
-        in_specs=[vm, vm, vm, vm, sm, sm, any_, any_, any_, any_],
+        in_specs=[vm, vm, sm, sm, any_, any_, any_, any_],
         out_specs=(any_,) * len(outs),
         scratch_shapes=scratch,
         compiler_params=pltpu.CompilerParams(
             collective_id=0, has_side_effects=True, vmem_limit_bytes=60 * 1024 * 1024
         ),
-    )(x, vec, qvb, upb, prefix, slopes, wq, wo, wu, wd)
+    )(x, note, prefix, slopes, wq, wo, wu, wd)
 
 
 def backward_kernel(
     dims, top, vec, prefix, slopes, wq, wo, wu, wd, hid_in, mid_in, nb_in, qkv_in, mix_in, sec_in, up_in, act_in, top_in,
-    dh_out, gq_out, go_out, gu_out, gd_out, sums_out, proj_out, ups_out, ru, rd, rq, ro, lent, lentq,
+    dh_out, gq_out, go_out, gu_out, gd_out, sums_out, low_out, ru, rd, rq, ro, lent, lentq,
     carry, grad, mid, hid, dmid, gp, gm, gu, gd, gq, go, part, own8, sc, rc, s8, r8,
-    s1, r1, sy, ry, sums, proj, ups, tmpq, tmpo,
+    s1, r1, sy, ry, sums, proj, ups, tmpq, tmpo, panel, low, notes, lows, sums_v, low_v, note_s, note_r, low_s, low_r,
     load_sem, up_sem, out_sem, carry_s, carry_r, ag8_s, ag8_r, f8_s, f8_r, c8_s, c8_r, rs8_s, rs8_r,
-    ag_s, ag_r, rs_s, rs_r, ffn_s, ffn_r, att_s, att_r, lent_s, lent_r, lentq_s, lentq_r, over_s,
+    ag_s, ag_r, rs_s, rs_r, ffn_s, ffn_r, att_s, att_r, lent_s, lent_r, lentq_s, lentq_r, over_s, cor_s, cor_r,
 ):
     n, seqs, heads, size, rows, deep, half = dims
     R = seqs * rows
@@ -586,7 +643,7 @@
     plane = (sect, z ^ 1, t)
     diag = (sect, z ^ 1, t ^ 2)
     across = (1 - sect, z, t)
-    greet([(s, z ^ k, t) for k in range(1, n) for s in (sect, 1 - sect)] + [core, chip, diag, across])
+    greet(peers_of(n) + [(1 - sect, z ^ k, t) for k in range(n)])
     zl = z & 1
     tile = 32
     order = (0, 2, 1, 3)
@@ -594,6 +651,10 @@
 
     def ag8(i):
         return remote(gp.at[0], gp.at[i], ag8_s.at[i], ag8_r.at[i], targets[i])
+
+    def corner8(i):
+        at = pl.ds(i * (R // 2), R // 2)
+        return remote(gp.at[2 - i, at], gp.at[3, at], cor_s.at[i], cor_r.at[i], (chip, plane)[i])
 
     def forward8(i):
         return remote(gp.at[i], gp.at[4 + i], f8_s.at[i], f8_r.at[i], core)
@@ -636,20 +697,23 @@
             ffn(1, k).start()
 
     def feed(vu, vd, sec, act, dup, upb):
-        loads = [load(wu, vu, 2), load(wd, vd, 3), load(sec_in, sec, 4), load(act_in, act, 5)]
-
-        def up_load(number):
-            i, slot = order[number], number % 2
+        loads = [load(wd, vd, 3), load(wu, vu, 2), load(sec_in, sec, 4), load(act_in, act, 5)]
+
+        def up_load(number, turn):
+            i, slot = turn[number], number % 2
             return [
                 pltpu.make_async_copy(up_in.at[i + 4 * b], upb.at[slot, b], up_sem.at[2 * slot + b])
                 for b in range(2)
             ]
 
-        for number in range(2):
-            for copy in up_load(number):
-                copy.start()
-
         load_top = pltpu.make_async_copy(top_in, gp, load_sem.at[6])
+        for layer in range(2):
+            @pl.when(sect == layer)
+            def _():
+                for number in range(2):
+                    for copy in up_load(number, order[:: 1 - 2 * layer]):
+                        copy.start()
+
 
         @pl.when(sect == 1)
         def _():
@@ -663,7 +727,7 @@
             over.wait_recv()
             grad[...] = carry[...]
             gp[0] = grad[...]
-            for i in order[1:]:
+            for i in order[1:3]:
                 ag8(i).start()
             forward8(0).start()
 
@@ -676,17 +740,20 @@
         tu = min(256, half)
         td = min(256, D)
 
-        def group(number):
-            i, slot = order[number], number % 2
-
-            @pl.when(sect == 0)
-            def _():
-                if i:
-                    ag8(i).wait_recv()
-                    forward8(i).start()
+        def group(number, turn, arriving):
+            i, slot = turn[number], number % 2
+            if arriving:
+                if number == 1:
+                    for k, side in ((2, 0), (1, 1)):
+                        ag8(k).wait_recv()
+                        corner8(side).start()
+                        forward8(k).start()
+                if i == 3:
+                    corner8(0).wait_recv()
+                    corner8(1).wait_recv()
+                    forward8(3).start()
                 forward8(i).wait_recv()
-
-            for copy in up_load(number):
+            for copy in up_load(number, turn):
                 copy.wait()
 
             def up_body(j):
@@ -709,7 +776,7 @@
 
             tiles(half // tu, up_body)
             if number + 2 < 4:
-                for copy in up_load(number + 2):
+                for copy in up_load(number + 2, turn):
                     copy.start()
 
             def second_body(j):
@@ -725,8 +792,8 @@
             tiles(D // td, second_body)
             core8(i).start()
 
-        def reduce(number):
-            i, slot = order[number], number % 2
+        def reduce(number, turn):
+            i, slot = turn[number], number % 2
             core8(i).wait_recv()
             if i == 0:
                 return
@@ -738,11 +805,20 @@
             tiles(R // tile, body)
             rs8(i).start()
 
-        for number in range(4):
-            group(number)
-            if number:
-                reduce(number - 1)
-        reduce(3)
+        def every(turn, arriving):
+            for number in range(4):
+                group(number, turn, arriving)
+                if number:
+                    reduce(number - 1, turn)
+            reduce(3, turn)
+
+        @pl.when(sect == 0)
+        def _():
+            every(order, True)
+
+        @pl.when(sect == 1)
+        def _():
+            every(order[::-1], False)
 
         th_ = min(256, half)
         for k in list(range(n - 1, 0, -1)) + [0]:
@@ -1007,9 +1083,30 @@
         outs.append(copy)
 
     put(dmid, dh_out)
-    put(sums, sums_out)
-    put(proj, proj_out)
-    put(ups, ups_out)
+
+    lane = D // (4 * n)
+    for j in range(D // 128):
+        panel[j] = sums[:, j * 128 : (j + 1) * 128]
+    for h in range(heads):
+        for c in range(2):
+            at = 2 * c * wide + h * size
+            low[c * heads + h : c * heads + h + 1, :] = proj[0:1, at : at + size]
+    count = half // 128
+    for j in range(count):
+        row = ups[0:1, j * 128 : (j + 1) * 128]
+        at = 2 * heads + j
+        low[at : at + 1, :] = jnp.where(zl == 0, row, 0.0)
+        low[at + count : at + count + 1, :] = jnp.where(zl == 1, row, 0.0)
+    me = z * 4 + t
+    share = []
+    for k in range(1, 4 * n):
+        to = peers_of(n)[k - 1]
+        share.append(
+            remote(panel.at[((me ^ k) * lane) // 128], notes.at[k], note_s.at[k], note_r.at[k], to))
+        if k % 4 == 0:
+            share.append(remote(low, lows.at[k // 4], low_s.at[k // 4], low_r.at[k // 4], to))
+    for copy in share:
+        copy.start()
 
     for k in send_order:
         if low_bit(k) == 1:
@@ -1042,6 +1139,19 @@
                 att_lend(k, c).wait_recv()
                 att_relay(k, c).start()
 
+    for copy in share:
+        copy.wait_recv()
+    total = panel[(me * lane) // 128]
+    for k in range(1, 4 * n):
+        total = total + notes[k]
+    sums_v[...] = total
+    total = low[...]
+    for k in range(1, n):
+        total = total + lows[k]
+    low_v[...] = total
+    put(sums_v, sums_out)
+    put(low_v, low_out)
+
     def final_feed(bu, bd, fu, fd):
         for a in range(2):
             for k in range(n - 1, 0, -1):
@@ -1140,8 +1250,9 @@
     for i in range(4):
         @pl.when(sect == 0)
         def _():
-            if i:
+            if i in (1, 2):
                 ag8(i).wait_send()
+                corner8(i - 1).wait_send()
             forward8(i).wait_send()
 
         if i:
@@ -1179,6 +1290,8 @@
     def _():
         over.wait_send()
 
+    for copy in share:
+        copy.wait_send()
     for copy in outs:
         copy.wait()
 
@@ -1195,7 +1308,7 @@
     one = pltpu.SemaphoreType.DMA(())
     outs = (
         S(R, D, F32), S(3, deep, wide, F32), S(wide, deep, F32), S(deep, 2 * half, F32), S(2 * half, deep, F32),
-        S(8, D, F32), S(1, 3 * wide, F32), S(1, half, F32),
+        S(8, 128, F32), S(24, 128, F32),
         S(n - 1, deep, half, BF), S(n - 1, half, deep, BF), S(n - 1, 3, deep, wide, BF), S(n - 1, wide, deep, BF),
         S(n - 1, half, deep, BF), S(n - 1, 3, deep, wide, BF),
     )
@@ -1206,10 +1319,12 @@
         V((2, R, D), F32), V((R, D), F32), V((4, R, D), BF), V((4, R, D), BF), V((3, R, D), BF), V((3, R, D), BF),
         V((2, R, D), BF), V((2, R, D), BF), V((R, D), BF), V((R, D), BF),
         V((8, D), F32), V((1, 3 * wide), F32), V((1, half), F32), V((deep, wide), BF), V((wide, deep), BF),
+        V((D // 128, 8, 128), F32), V((24, 128), F32), V((4 * n, 8, 128), F32), V((n, 24, 128), F32),
+        V((8, 128), F32), V((24, 128), F32), dma(4 * n), dma(4 * n), dma(n), dma(n),
         dma(8), dma(4), dma(4), one, one,
         dma(4), dma(4), dma(4), dma(4), dma(4), dma(4), dma(4), dma(4),
         dma(3), dma(3), dma(2), dma(2), dma(2 * (n - 1)), dma(2 * (n - 1)), dma(4 * (n - 1)), dma(4 * (n - 1)), dma(n - 1), dma(n - 1),
-        dma(4 * (n - 1)), dma(4 * (n - 1)), dma(4 * (n - 1)),
+        dma(4 * (n - 1)), dma(4 * (n - 1)), dma(4 * (n - 1)), dma(2), dma(2),
     ]
     return pl.pallas_call(
         functools.partial(backward_kernel, dims),
@@ -1223,125 +1338,53 @@
     )(top, vec, prefix, slopes, *weights, *kept)
 
 
-def small_kernel(spread, peers, src, out, got, send_sem, recv_sem):
-    sect, z, t = lax.axis_index("section"), lax.axis_index("dp"), lax.axis_index("tensor")
-    n, m = peers
-    count = n * m
-    me = z * m + t
-
-    def peer(k):
-        other = me ^ k
-        return other, (sect, other // m, lax.rem(other, m))
-
-    greet([peer(k)[1] for k in range(1, count)])
-    copies = []
-    for k in range(1, count):
-        other, device = peer(k)
-        block = src if spread else src.at[other]
-        copies.append(remote(block, got.at[k], send_sem.at[k], recv_sem.at[k], device))
-        copies[-1].start()
-    if spread:
-        out[me] = src[...]
-    else:
-        total = src[me]
-    for k in range(1, count):
-        copies[k - 1].wait_recv()
-        if spread:
-            out[me ^ k] = got[k]
-        else:
-            total = total + got[k]
-    if not spread:
-        out[...] = total
-    for copy in copies:
-        copy.wait_send()
-
-
-def small_exchange(value, spread, peers, collective_id):
-    count = peers[0] * peers[1]
-    block = value.shape if spread else value.shape[1:]
-    return pl.pallas_call(
-        functools.partial(small_kernel, spread, peers),
-        out_shape=jax.ShapeDtypeStruct((count,) + block if spread else block, F32),
-        in_specs=[pl.BlockSpec(memory_space=pltpu.VMEM)],
-        out_specs=pl.BlockSpec(memory_space=pltpu.VMEM),
-        scratch_shapes=[
-            pltpu.VMEM((count,) + block, F32),
-            pltpu.SemaphoreType.DMA((count,)),
-            pltpu.SemaphoreType.DMA((count,)),
-        ],
-        compiler_params=pltpu.CompilerParams(collective_id=collective_id, has_side_effects=True),
-    )(value)
-
-
 def on_device(activations, ln_gains, biases, w_qkv, qv_bias, w_out, w_up, up_bias, w_down, prefix):
     is_first = lax.axis_index("section") == 0
     plane = lax.axis_index("dp")
     place = lax.axis_index("tensor")
     planes = lax.axis_size("dp")
     tensors = lax.axis_size("tensor")
-    odd = plane % 2 == 1
     seqs, rows, width = activations.shape[1:]
-    heads, size_part = qv_bias.shape[2:]
-    size = size_part * planes
-    wide = heads * size
+    heads, part = qv_bias.shape[2:]
+    size = part * planes
     deep = w_qkv.shape[1]
     units = w_up.shape[2]
-    half = units // 2
-    own = activations[0]
-
-    flat = jnp.concatenate([v.reshape(-1) for v in (ln_gains, biases, qv_bias, up_bias)])
-    peers = (planes, tensors)
-    everyone = small_exchange(flat.astype(F32).reshape(-1, 128), True, peers, 2).reshape(planes * tensors, -1)
     lane = width // (planes * tensors)
-    cut = 6 * lane
-    features = everyone[:, :cut].reshape(-1, 6, lane).swapaxes(0, 1).reshape(6, width)
-    mine = everyone.reshape(planes, tensors, -1)
-    mine = lax.dynamic_index_in_dim(mine, place, 1, keepdims=False)[:, cut:]
-    qv_full = mine[:, : 2 * heads * size_part].reshape(planes, 2, heads, size_part)
-    qv_full = qv_full.transpose(1, 2, 0, 3).reshape(2, heads, size)
-    up_full = mine[:, 2 * heads * size_part :].reshape(planes, up_bias.shape[1], up_bias.shape[2])
-    up_full = up_full.transpose(1, 0, 2).reshape(units)
-    up_own = jnp.where(odd, up_full[half:], up_full[:half])
-
+    own = activations[0].reshape(seqs * rows, width)
+    spot = (plane * tensors + place) * lane % 128
+
+    def placed(block, start):
+        length = block.shape[1]
+        wide_block = jnp.tile(block.astype(F32), (1, 128 // length))
+        lanes = jnp.arange(128)
+        return jnp.where((lanes >= start) & (lanes < start + length), wide_block, 0.0)
+
+    features = placed(jnp.concatenate([ln_gains[0], biases[0]]), spot)
+    note = jnp.concatenate([
+        features, jnp.zeros((2, 128), F32), placed(qv_bias[0].reshape(2 * heads, part), plane * part),
+        placed(up_bias[0], plane * part),
+    ])
     head_ids = place * heads + jnp.arange(heads)
     slopes = jnp.exp2(-8.0 * (head_ids.astype(F32) + 1.0) / (heads * tensors))
-
-    dims = (planes, seqs, heads, size, rows, deep, half)
-    vec = jnp.concatenate([features, jnp.zeros((2, width), F32)], axis=0)
-    flat_qv = qv_full.reshape(2, wide)
-    qvb = jnp.stack([flat_qv[0], jnp.zeros_like(flat_qv[0]), flat_qv[1]])
+    dims = (planes, seqs, heads, size, rows, deep, units // 2)
     got = run_forward(
-        dims, own.reshape(seqs * rows, width), vec, qvb, up_own[None], prefix, slopes,
-        w_qkv[0].transpose(1, 0, 2), w_out[0], w_up[0], w_down[0],
+        dims, own, note, prefix, slopes, w_qkv[0].transpose(1, 0, 2), w_out[0], w_up[0], w_down[0]
     )
-    output, weights, kept = got[0], got[1:5], got[5:14]
-    back = run_backward(dims, own.reshape(seqs * rows, width), vec, prefix, slopes, weights, kept)
-    grad_low, grad_q, grad_o, grad_u, grad_d, vectors, proj_sums, up_sums = back[:8]
-    proj_sums, up_sums = proj_sums[0], up_sums[0]
-
-    vec = vectors[:6].reshape(6, planes * tensors, lane).swapaxes(0, 1).reshape(planes * tensors, cut)
-    qv_sums = jnp.stack([proj_sums[:wide], proj_sums[2 * wide :]]).reshape(2, heads, planes, size_part)
-    qv_sums = qv_sums.transpose(2, 0, 1, 3).reshape(planes, -1)
-    zero = jnp.zeros_like(up_sums)
-    up_sums = jnp.where(odd, jnp.concatenate([zero, up_sums]), jnp.concatenate([up_sums, zero]))
-    up_sums = up_sums.reshape(up_bias.shape[1], planes, up_bias.shape[2]).transpose(1, 0, 2).reshape(planes, -1)
-    own_part = jnp.concatenate([qv_sums, up_sums], axis=1)[:, None, :]
-    own_part = jnp.where((jnp.arange(tensors) == place)[None, :, None], own_part, 0.0)
-    message = jnp.concatenate([vec, own_part.reshape(planes * tensors, -1)], axis=1)
-    message = message.reshape(planes * tensors, -1, 128)
-    small = small_exchange(message, False, peers, 3).reshape(-1)
-    mid = cut + 2 * heads * size_part
-
+    output, weights, kept, vec = got[0], got[1:5], got[5:14], got[15]
+    back = run_backward(dims, own, vec, prefix, slopes, weights, kept)
+    grad_low, grad_q, grad_o, grad_u, grad_d, sums, low = back[:7]
+    sums = lax.dynamic_slice_in_dim(sums, spot, lane, 1)
+    low = lax.dynamic_slice_in_dim(low, plane * part, part, 1)
     ends = jnp.where(is_first, grad_low, output).reshape(seqs, rows, width)
     return (
         ends[None],
-        small[: 2 * lane].reshape(1, 2, lane),
-        small[2 * lane : cut].reshape(1, 4, lane),
+        sums[None, 0:2],
+        sums[None, 2:6],
         grad_q.transpose(1, 0, 2)[None],
-        small[cut:mid].reshape(1, 2, heads, size_part),
+        low[: 2 * heads].reshape(1, 2, heads, part),
         grad_o[None],
         grad_u[None],
-        small[mid:].reshape(1, up_bias.shape[1], up_bias.shape[2]),
+        low[2 * heads :][None],
         grad_d[None],
     )
 

time: 892 us -> 860 us (0.964)
  Pallas kernels: 864 us -> 841 us
    pallas_call x2 -> x0, Pallas kernels: 20 us -> none  [small_exchange(): pl.pallas_call(functools.partial(small_kernel, spread, peers), out_shape=...]
where the time goes in v5:
time: 860 us
  Pallas kernels  841 us (98%)
  local copies, waits for them, and re-layouts  13.2 us (2%)
    pallas_call x1, Pallas kernels, run_backward(): pl.pallas_call(functools.partial(backward_kernel, dims), out_shape=outs,...  517 us
    pallas_call x1, Pallas kernels, run_forward(): pl.pallas_call(functools.partial(forward_kernel, dims), out_shape=outs, i...  324 us

profile of v5, /device:TPU:0, one launch (start us, length us, event | category | flops | bytes accessed | tf_op | source)
XLA Modules:
  0.0 859.9 jit_solution(9149616739050797307)
XLA Ops:
  0.7 0.7 convert_select_fusion
  1.4 0.7 bitcast_convert_fusion
  2.1 0.1 tile.21
  2.2 0.7 tile.8
  2.9 0.1 tile.9
  2.9 0.1 pad.1.clone
  3.0 0.7 pad_maximum_fusion.note
  3.7 0.5 multiply_exponential_fusion.slopes
  4.2 323.7 %shard_map.169 = (f32[128,2048]{1,0:T(8,128)}, bf16[3,2048,512]{2,1,0:T(8,128)(2,1)}, bf16[4,512,512]{2,1,0:T(8,128)(2,1)}, bf16[2048,1024]{1,0:T(8,128)(2,1)}, ...) custom-call(bf16[128,2048]{1,0:T(8,128)(2,1)} %bitcast.31, ...), custom_call_target="tpu_custom_call" | custom-call | tf_op jit(solution)/shard_map/pallas_call | solution.py:616
  327.9 517.2 %shard_map.170 = (f32[128,2048]{1,0:T(8,128)}, f32[3,512,512]{2,1,0:T(8,128)}, f32[512,512]{1,0:T(8,128)}, f32[512,2048]{1,0:T(8,128)}, f32[2048,512]{1,0:T(8,12...) custom-call(bf16[128,2048]{1,0:T(8,128)(2,1)} %bitcast.32, ...), custom_call_target="tpu_custom_call" | custom-call | tf_op jit(solution)/shard_map/pallas_call | solution.py:1329
  845.2 0.0 copy-start.4
  845.2 0.0 copy-start.5
  845.2 0.0 copy-start.2
  845.2 2.5 broadcast_select_fusion
  847.7 0.0 copy-done.4
  847.7 0.7 dynamic-slice_bitcast_fusion
  848.4 0.7 constant_dynamic-slice_fusion
  849.0 0.0 copy-done.5
  849.0 0.6 slice_bitcast_fusion
  849.6 0.6 slice_bitcast_fusion.1
  850.2 0.0 copy-done.2
  850.2 0.0 copy-start.3
  850.2 0.0 copy-start.1
  850.2 1.7 copy.23
  851.9 0.3 copy-done.3
  852.2 1.0 copy.24
  853.1 1.1 copy-done.1
  854.2 0.0 copy-start
  854.2 2.1 copy.25
  856.4 1.6 copy-done
  857.9 2.0 copy.26
  (6 shorter events, 0.0 us)
Async XLA Ops:
  845.2 2.5 copy-start.4
  845.2 3.9 copy-start.5
  845.2 5.0 copy-start.2
  850.2 2.0 copy-start.3
  850.2 4.0 copy-start.1
  854.2 3.7 copy-start

commit v6 on v5

--- a/solution.py
+++ b/solution.py
@@ -13,9 +13,10 @@
 
 
 MESH = pl.DeviceIdType.MESH
+EARLY = True
 RELAYED = ((3,), ())
 GRADS_RELAYED = ((), (3, 2))
-ATT_RELAYED = (0, 1, 2)
+ATT_RELAYED = (0, 1)
 NT = (((1,), (1,)), ((), ()))
 TN = (((0,), (0,)), ((), ()))
 
@@ -47,6 +48,10 @@
         return carry
 
     lax.fori_loop(0, count, step, 0)
+
+
+def half_tiles(count, part, body):
+    tiles(count // 2, lambda i: body(i + part * (count // 2)))
 
 
 def rows_of(i, size):
@@ -225,29 +230,42 @@
 
     tile = 32
 
-    def first_norm():
+    def part_of_rows(h, size=R):
+        return pl.ds(h * (size // 2), size // 2)
+
+    def first_norm(h):
         def body(i):
             sl = rows_of(i, tile)
             v = hid[sl, :].astype(F32)
             nb[0, sl, :] = norm_rows(v, vec[0:1, :], vec[2:3, :]).astype(BF)
 
-        tiles(R // tile, body)
-
-    def ag(i):
+        half_tiles(R // tile, h, body)
+        ag(1, h).start()
+        ag(0, h).start()
+
+    def ag(i, h):
         src, to = ((0, core), (0, chip), (2, core))[i]
         dst = (1, 2, 3)[i]
-        return remote(nb.at[src], nb.at[dst], ag_s.at[i], ag_r.at[i], to)
+        at = part_of_rows(h)
+        return remote(nb.at[src, at], nb.at[dst, at], ag_s.at[2 * i + h], ag_r.at[2 * i + h], to)
+
+    def over(h):
+        at = part_of_rows(h)
+        return remote(carry_send.at[at], carry.at[at], carry_s.at[h], carry_r.at[h], across)
+
+    def pass_on():
+        for h in range(2):
+            ag(1, h).wait_recv()
+            ag(2, h).start()
 
     vectors()
 
     @pl.when(sect == 0)
     def _():
         hid[...] = x_in[...]
-        first_norm()
-        ag(1).start()
-        ag(0).start()
-        ag(1).wait_recv()
-        ag(2).start()
+        first_norm(0)
+        first_norm(1)
+        pass_on()
 
     def direct(k):
         i = n - 1 + k - 1
@@ -293,13 +311,13 @@
             for k in range(n - 1, 0, -1):
                 pair(0, k).start()
 
-            for layer in range(2):
-                def body():
-                    for k in range(n - 1, 0, -1):
-                        if k not in relayed(layer):
-                            direct(k).start()
-
-                on_layer(layer, body)
+    for layer in range(2):
+        def body():
+            for k in range(n - 1, 0, -1):
+                if k not in relayed(layer):
+                    direct(k).start()
+
+        on_layer(layer, body)
 
     for copy in mine:
         copy.wait()
@@ -314,18 +332,15 @@
         for i in (1, 2, 3):
             top(i).start()
         top_land[0].start()
-        remote(carry_send, carry, carry_s, carry_r, across).wait_recv()
-        hid[...] = carry[...]
-        first_norm()
-        ag(1).start()
-        ag(0).start()
-        ag(1).wait_recv()
-        ag(2).start()
-
-    ag(0).wait_recv()
-    ag(2).wait_recv()
+        for h in range(2):
+            over(h).wait_recv()
+            hid[part_of_rows(h), :] = carry[part_of_rows(h), :]
+            first_norm(h)
+
     load_q.wait()
     load_o.wait()
+    ag(0, 0).wait_recv()
+    ag(0, 1).wait_recv()
     keeps = []
 
     def keep(src, dst):
@@ -334,22 +349,32 @@
         keeps.append(copy)
 
     keep(hid, x_out)
+    keep(vec, vec_out)
+
+    tn = min(256, wide)
+
+    def project_in(b):
+        for c in range(3):
+            def body(j):
+                cols = rows_of(j, tn)
+                lhs = jnp.concatenate([nb[2 * b], nb[2 * b + 1]], axis=0)
+                got = dot(lhs, vq[c, :, cols]) + qvb[c : c + 1, cols]
+                got = got.astype(BF)
+                qkv[2 * b, :, pl.ds(pl.multiple_of(c * wide + j * tn, tn), tn)] = got[:R]
+                qkv[2 * b + 1, :, pl.ds(pl.multiple_of(c * wide + j * tn, tn), tn)] = got[R:]
+
+            tiles(wide // tn, body)
+
+    project_in(0)
+
+    @pl.when(sect == 1)
+    def _():
+        pass_on()
+
+    ag(2, 0).wait_recv()
+    ag(2, 1).wait_recv()
+    project_in(1)
     keep(nb, nb_out)
-    keep(vec, vec_out)
-
-    tn = min(256, wide)
-    for c in range(3):
-        def body(i):
-            j = lax.rem(i, wide // tn)
-            b = i // (wide // tn)
-            cols = rows_of(j, tn)
-            lhs = jnp.concatenate([nb[2 * b], nb[2 * b + 1]], axis=0)
-            got = dot(lhs, vq[c, :, cols]) + qvb[c : c + 1, cols]
-            got = got.astype(BF)
-            qkv[2 * b, :, pl.ds(pl.multiple_of(c * wide + j * tn, tn), tn)] = got[:R]
-            qkv[2 * b + 1, :, pl.ds(pl.multiple_of(c * wide + j * tn, tn), tn)] = got[R:]
-
-        tiles(2 * (wide // tn), body)
     keep(qkv, qkv_out)
 
     def head(i):
@@ -411,13 +436,12 @@
         mid[sl, :] = v
         sec[0, sl, :] = norm_rows(v, vec[1:2, :], vec[3:4, :]).astype(BF)
 
-    tiles(R // tile, middle_body)
-    keep(mid, mid_out)
 
     targets = (None, chip, plane, diag)
 
-    def ag8(i):
-        return remote(sec.at[0], sec.at[i], ag8_s.at[i], ag8_r.at[i], targets[i])
+    def ag8(i, h):
+        at = part_of_rows(h)
+        return remote(sec.at[0, at], sec.at[i, at], ag8_s.at[2 * i + h], ag8_r.at[2 * i + h], targets[i])
 
     def corner8(i):
         at = pl.ds(i * (R // 2), R // 2)
@@ -433,35 +457,39 @@
         return remote(s8.at[i], r8.at[i], rs8_s.at[i], rs8_r.at[i], targets[i])
 
     order = (0, 2, 1, 3)
-    for i in order[1:3]:
-        ag8(i).start()
+    for h in range(2):
+        half_tiles(R // tile, h, middle_body)
+        for i in order[1:3]:
+            ag8(i, h).start()
     forward8(0).start()
-
-    for a in range(2):
+    keep(mid, mid_out)
+
+    def arrive():
+        ag8(2, 0).wait_recv()
+        corner8(0).start()
+        ag8(2, 1).wait_recv()
+        forward8(2).start()
+        ag8(1, 0).wait_recv()
+        ag8(1, 1).wait_recv()
+        corner8(1).start()
+        forward8(1).start()
+
+    def arrive_corner():
+        corner8(0).wait_recv()
+        corner8(1).wait_recv()
+        forward8(3).start()
+
+    load_u = pltpu.make_async_copy(wu, vu, load_sem.at[2])
+    load_d = pltpu.make_async_copy(wd, vd, load_sem.at[3])
+
+    def weights_in(a):
         for k in range(n - 1, 0, -1):
             pair_recv(a, k).wait_recv()
-
-    load_u = pltpu.make_async_copy(wu, vu, load_sem.at[2])
-    load_d = pltpu.make_async_copy(wd, vd, load_sem.at[3])
-    load_u.start()
-    load_d.start()
-    load_u.wait()
-    load_d.wait()
+        (load_u, load_d)[a].start()
 
     tu = min(256, half)
 
-    def group(i):
-        if i == order[1]:
-            for k, side in ((2, 0), (1, 1)):
-                ag8(k).wait_recv()
-                corner8(side).start()
-                forward8(k).start()
-        if i == 3:
-            corner8(0).wait_recv()
-            corner8(1).wait_recv()
-            forward8(3).start()
-        forward8(i).wait_recv()
-
+    def up_part(i):
         def up_body(j):
             cols = rows_of(j, tu)
             lhs = jnp.concatenate([sec[i], sec[4 + i]], axis=0)
@@ -474,6 +502,7 @@
 
         tiles(half // tu, up_body)
 
+    def down_part(i):
         def down_body(j):
             cols = rows_of(j, deep)
             lhs = jnp.concatenate([act[i], act[4 + i]], axis=0)
@@ -496,11 +525,41 @@
         tiles(R // tile, body)
         rs8(i).start()
 
-    for number, i in enumerate(order):
-        group(i)
-        if number:
-            reduce(order[number - 1])
-    reduce(order[-1])
+    @pl.when(sect == 0)
+    def _():
+        arrive()
+        arrive_corner()
+        weights_in(0)
+        weights_in(1)
+        for i in range(4):
+            forward8(i).wait_recv()
+        load_u.wait()
+        load_d.wait()
+        for number, i in enumerate(order[::-1]):
+            up_part(i)
+            down_part(i)
+            if number:
+                reduce(order[4 - number])
+        reduce(order[0])
+
+    @pl.when(sect == 1)
+    def _():
+        weights_in(0)
+        weights_in(1)
+        load_u.wait()
+        load_d.wait()
+        for number, i in enumerate(order):
+            if number == 1:
+                arrive()
+            if number == 3:
+                arrive_corner()
+            forward8(i).wait_recv()
+            up_part(i)
+            down_part(i)
+            if number:
+                reduce(order[number - 1])
+        reduce(order[3])
+
     keep(sec, sec_out)
     keep(up, up_out)
     keep(act, act_out)
@@ -516,12 +575,15 @@
         outv[sl, :] = v
         carry_send[sl, :] = v.astype(BF)
 
-    tiles(R // tile, out_body)
-    over = remote(carry_send, carry, carry_s, carry_r, across)
+    for h in range(2):
+        half_tiles(R // tile, h, out_body)
+
+        @pl.when(sect == 0)
+        def _():
+            over(h).start()
 
     @pl.when(sect == 0)
     def _():
-        over.start()
         relay(1)
 
     keep(outv, out)
@@ -539,13 +601,14 @@
 
     for k in range(n - 1, 0, -1):
         pair(0, k).wait_send()
-    for i in range(3):
-        ag(i).wait_send()
+    for i in range(6):
+        ag(i // 2, i % 2).wait_send()
     to_core.wait_send()
     to_chip.wait_send()
     for i in range(4):
         if i in (1, 2):
-            ag8(i).wait_send()
+            ag8(i, 0).wait_send()
+            ag8(i, 1).wait_send()
             corner8(i - 1).wait_send()
         if i:
             rs8(i).wait_send()
@@ -566,7 +629,8 @@
 
     @pl.when(sect == 0)
     def _():
-        over.wait_send()
+        over(0).wait_send()
+        over(1).wait_send()
 
     @pl.when(sect == 1)
     def _():
@@ -609,8 +673,8 @@
         V((2, R, D), BF), V((2, R, D), BF), V((2, R, D), F32), V((R, D), BF), V((R, D), BF),
         V((4, R, D), F32), V((4, R, D), BF), V((4, R, D), BF), V((4, R, D), BF), V((4, R, D), BF),
         dma(4 * (n - 1)), dma(4 * (n - 1)), dma(2 * (n - 1)), dma(2 * (n - 1)), dma(5), dma(4), dma(10),
-        pltpu.SemaphoreType.DMA(()), pltpu.SemaphoreType.DMA(()),
-        dma(3), dma(3), dma(2), dma(2), dma(4), dma(4), dma(4), dma(4), dma(4), dma(4), dma(4), dma(4),
+        dma(2), dma(2),
+        dma(6), dma(6), dma(2), dma(2), dma(8), dma(8), dma(4), dma(4), dma(4), dma(4), dma(4), dma(4),
         dma(4), dma(4), dma(4), dma(4), dma(2), dma(2), dma(n - 1), dma(2), dma(2),
     ]
     return pl.pallas_call(
@@ -649,8 +713,12 @@
     order = (0, 2, 1, 3)
     targets = (None, chip, plane, diag)
 
-    def ag8(i):
-        return remote(gp.at[0], gp.at[i], ag8_s.at[i], ag8_r.at[i], targets[i])
+    def part_of_rows(h):
+        return pl.ds(h * (R // 2), R // 2)
+
+    def ag8(i, h):
+        at = part_of_rows(h)
+        return remote(gp.at[0, at], gp.at[i, at], ag8_s.at[2 * i + h], ag8_r.at[2 * i + h], targets[i])
 
     def corner8(i):
         at = pl.ds(i * (R // 2), R // 2)
@@ -674,7 +742,10 @@
     sums[...] = jnp.zeros_like(sums)
     proj[...] = jnp.zeros_like(proj)
     ups[...] = jnp.zeros_like(ups)
-    over = remote(s1.at[0], carry, carry_s, carry_r, across)
+
+    def over(h):
+        at = part_of_rows(h)
+        return remote(s1.at[0, at], carry.at[at], carry_s.at[h], carry_r.at[h], across)
 
     def col_sum(row, value):
         sums[row : row + 1, :] += jnp.sum(value, axis=0, keepdims=True)
@@ -690,6 +761,10 @@
 
     def lend(k):
         return remote(gd.at[k], lent.at[k - 1], lent_s.at[k - 1], lent_r.at[k - 1], across)
+
+    def ffn_start(layer, k):
+        (lend if k in GRADS_RELAYED[layer] else direct)(k).start()
+        ffn(0, k).start()
 
     def relay(layer):
         for k in GRADS_RELAYED[layer]:
@@ -724,11 +799,13 @@
         @pl.when(sect == 0)
         def _():
             relay(1)
-            over.wait_recv()
-            grad[...] = carry[...]
-            gp[0] = grad[...]
-            for i in order[1:3]:
-                ag8(i).start()
+            for h in range(2):
+                over(h).wait_recv()
+                value = carry[part_of_rows(h), :]
+                grad[part_of_rows(h), :] = value
+                gp[0, part_of_rows(h), :] = value
+                for i in order[1:3]:
+                    ag8(i, h).start()
             forward8(0).start()
 
         def bias_body(j):
@@ -744,10 +821,14 @@
             i, slot = turn[number], number % 2
             if arriving:
                 if number == 1:
-                    for k, side in ((2, 0), (1, 1)):
-                        ag8(k).wait_recv()
-                        corner8(side).start()
-                        forward8(k).start()
+                    ag8(2, 0).wait_recv()
+                    corner8(0).start()
+                    ag8(2, 1).wait_recv()
+                    forward8(2).start()
+                    ag8(1, 0).wait_recv()
+                    ag8(1, 1).wait_recv()
+                    corner8(1).start()
+                    forward8(1).start()
                 if i == 3:
                     corner8(0).wait_recv()
                     corner8(1).wait_recv()
@@ -837,6 +918,10 @@
                 gu[k, rows_of(j, dd), :] = dot(lhs, dup[...].reshape(8 * R, half), TN).astype(BF)
 
             tiles(deep // dd, up_body)
+            if EARLY and k:
+                @pl.when(sect == 0)
+                def _():
+                    ffn_start(0, k)
 
     pl.run_scoped(
         feed,
@@ -845,12 +930,11 @@
     )
     for i in order[1:]:
         rs8(i).wait_recv()
-    for layer in range(2):
+    for layer in range(1 if EARLY else 0, 2):
         @pl.when(sect == layer)
         def _():
             for k in range(n - 1, 0, -1):
-                (lend if k in GRADS_RELAYED[layer] else direct)(k).start()
-                ffn(0, k).start()
+                ffn_start(layer, k)
 
     load_mid.wait()
     load_hid.wait()
@@ -877,15 +961,16 @@
         col_sum(3, dy)
         col_sum(4, total)
 
-    tiles(R // tile, mid_body)
-
-    def ag(i):
+    def ag(i, h):
         src, to = ((0, core), (0, chip), (2, core))[i]
         dst = (1, 2, 3)[i]
-        return remote(gm.at[src], gm.at[dst], ag_s.at[i], ag_r.at[i], to)
-
-    ag(1).start()
-    ag(0).start()
+        at = part_of_rows(h)
+        return remote(gm.at[src, at], gm.at[dst, at], ag_s.at[2 * i + h], ag_r.at[2 * i + h], to)
+
+    for h in range(2):
+        half_tiles(R // tile, h, mid_body)
+        ag(1, h).start()
+        ag(0, h).start()
     to_core = remote(s1, r1, rs_s.at[0], rs_r.at[0], core)
     to_chip = remote(sy, ry, rs_s.at[1], rs_r.at[1], chip)
 
@@ -928,15 +1013,19 @@
 
     def attention(vq, vo, nb, qkv, mix, dmix, dqkv):
         loads = [load(wo, vo, 2), load(qkv_in, qkv, 3), load(mix_in, mix, 4), load(nb_in, nb, 5), load(wq, vq, 6)]
-        ag(1).wait_recv()
-        ag(2).start()
-        for copy in loads:
-            copy.wait()
-        ag(0).wait_recv()
+        loads[0].wait()
+        ag(0, 0).wait_recv()
+        ag(0, 1).wait_recv()
 
         def mixed(b):
             if b == 1:
-                ag(2).wait_recv()
+                for h in range(2):
+                    ag(1, h).wait_recv()
+                    ag(2, h).start()
+                for copy in loads[1:]:
+                    copy.wait()
+                ag(2, 0).wait_recv()
+                ag(2, 1).wait_recv()
             tw = min(256, wide)
 
             def body(j):
@@ -1069,11 +1158,12 @@
         col_sum(0, dy * unit)
         col_sum(2, dy)
 
-    tiles(R // tile, low_body)
-
-    @pl.when(sect == 1)
-    def _():
-        over.start()
+    for h in range(2):
+        half_tiles(R // tile, h, low_body)
+
+        @pl.when(sect == 1)
+        def _():
+            over(h).start()
 
     outs = []
 
@@ -1251,15 +1341,16 @@
         @pl.when(sect == 0)
         def _():
             if i in (1, 2):
-                ag8(i).wait_send()
+                ag8(i, 0).wait_send()
+                ag8(i, 1).wait_send()
                 corner8(i - 1).wait_send()
             forward8(i).wait_send()
 
         if i:
             rs8(i).wait_send()
         core8(i).wait_send()
-    for i in range(3):
-        ag(i).wait_send()
+    for i in range(6):
+        ag(i // 2, i % 2).wait_send()
     to_chip.wait_send()
     for layer in range(2):
         @pl.when(sect == layer)
@@ -1288,7 +1379,8 @@
 
     @pl.when(sect == 1)
     def _():
-        over.wait_send()
+        over(0).wait_send()
+        over(1).wait_send()
 
     for copy in share:
         copy.wait_send()
@@ -1305,7 +1397,6 @@
     vm = pl.BlockSpec(memory_space=pltpu.VMEM)
     sm = pl.BlockSpec(memory_space=pltpu.SMEM)
     dma = lambda k: pltpu.SemaphoreType.DMA((k,))
-    one = pltpu.SemaphoreType.DMA(())
     outs = (
         S(R, D, F32), S(3, deep, wide, F32), S(wide, deep, F32), S(deep, 2 * half, F32), S(2 * half, deep, F32),
         S(8, 128, F32), S(24, 128, F32),
@@ -1321,9 +1412,9 @@
         V((8, D), F32), V((1, 3 * wide), F32), V((1, half), F32), V((deep, wide), BF), V((wide, deep), BF),
         V((D // 128, 8, 128), F32), V((24, 128), F32), V((4 * n, 8, 128), F32), V((n, 24, 128), F32),
         V((8, 128), F32), V((24, 128), F32), dma(4 * n), dma(4 * n), dma(n), dma(n),
-        dma(8), dma(4), dma(4), one, one,
-        dma(4), dma(4), dma(4), dma(4), dma(4), dma(4), dma(4), dma(4),
-        dma(3), dma(3), dma(2), dma(2), dma(2 * (n - 1)), dma(2 * (n - 1)), dma(4 * (n - 1)), dma(4 * (n - 1)), dma(n - 1), dma(n - 1),
+        dma(8), dma(4), dma(4), dma(2), dma(2),
+        dma(8), dma(8), dma(4), dma(4), dma(4), dma(4), dma(4), dma(4),
+        dma(6), dma(6), dma(2), dma(2), dma(2 * (n - 1)), dma(2 * (n - 1)), dma(4 * (n - 1)), dma(4 * (n - 1)), dma(n - 1), dma(n - 1),
         dma(4 * (n - 1)), dma(4 * (n - 1)), dma(4 * (n - 1)), dma(2), dma(2),
     ]
     return pl.pallas_call(

time: 860 us -> 845 us (0.983)
  Pallas kernels: 841 us -> 825 us
    pallas_call x1, Pallas kernels: 517 us -> 499 us  [run_backward(): pl.pallas_call(functools.partial(backward_kernel, dims), out_shape=outs,...]
where the time goes in v6:
time: 845 us; the launch traced here: 844 us
  Pallas kernels  825 us (98%)
  local copies, waits for them, and re-layouts  13.2 us (2%)
    pallas_call x1, Pallas kernels, run_backward(): pl.pallas_call(functools.partial(backward_kernel, dims), out_shape=outs,...  499 us
    pallas_call x1, Pallas kernels, run_forward(): pl.pallas_call(functools.partial(forward_kernel, dims), out_shape=outs, i...  326 us

profile of v6, /device:TPU:0, one launch (start us, length us, event | category | flops | bytes accessed | tf_op | source)
XLA Modules:
  0.0 844.3 jit_solution(3488687443744542769)
XLA Ops:
  0.7 0.7 convert_select_fusion
  1.4 0.7 bitcast_convert_fusion
  2.1 0.1 tile.21
  2.2 0.7 tile.8
  2.9 0.1 tile.9
  2.9 0.1 pad.1.clone
  3.0 0.7 pad_maximum_fusion.note
  3.7 0.5 multiply_exponential_fusion.slopes
  4.2 326.3 %shard_map.169 = (f32[128,2048]{1,0:T(8,128)}, bf16[3,2048,512]{2,1,0:T(8,128)(2,1)}, bf16[4,512,512]{2,1,0:T(8,128)(2,1)}, bf16[2048,1024]{1,0:T(8,128)(2,1)}, ...) custom-call(bf16[128,2048]{1,0:T(8,128)(2,1)} %bitcast.31, ...), custom_call_target="tpu_custom_call" | custom-call | tf_op jit(solution)/shard_map/pallas_call | solution.py:680
  330.5 499.0 %shard_map.170 = (f32[128,2048]{1,0:T(8,128)}, f32[3,512,512]{2,1,0:T(8,128)}, f32[512,512]{1,0:T(8,128)}, f32[512,2048]{1,0:T(8,128)}, f32[2048,512]{1,0:T(8,12...) custom-call(bf16[128,2048]{1,0:T(8,128)(2,1)} %bitcast.32, ...), custom_call_target="tpu_custom_call" | custom-call | tf_op jit(solution)/shard_map/pallas_call | solution.py:1420
  829.5 0.0 copy-start.4
  829.5 0.0 copy-start.5
  829.6 0.0 copy-start.2
  829.6 2.5 broadcast_select_fusion
  832.1 0.0 copy-done.4
  832.1 0.7 dynamic-slice_bitcast_fusion
  832.7 0.7 constant_dynamic-slice_fusion
  833.4 0.0 copy-done.5
  833.4 0.6 slice_bitcast_fusion
  834.0 0.6 slice_bitcast_fusion.1
  834.5 0.0 copy-done.2
  834.5 0.0 copy-start.3
  834.6 0.0 copy-start.1
  834.6 1.7 copy.23
  836.2 0.3 copy-done.3
  836.5 1.0 copy.24
  837.5 1.1 copy-done.1
  838.6 0.0 copy-start
  838.6 2.1 copy.25
  840.7 1.6 copy-done
  842.3 2.0 copy.26
  (6 shorter events, 0.0 us)
Async XLA Ops:
  829.5 2.5 copy-start.4
  829.5 3.9 copy-start.5
  829.6 5.0 copy-start.2
  834.5 2.0 copy-start.3
  834.6 4.0 copy-start.1
  838.6 3.7 copy-start

commit v7 on v6

--- a/solution.py
+++ b/solution.py
@@ -16,7 +16,7 @@
 EARLY = True
 RELAYED = ((3,), ())
 GRADS_RELAYED = ((), (3, 2))
-ATT_RELAYED = (0, 1)
+ATT_RELAYED = (0, 1, 2)
 NT = (((1,), (1,)), ((), ()))
 TN = (((0,), (0,)), ((), ()))
 
@@ -378,33 +378,37 @@
     keep(qkv, qkv_out)
 
     def head(i):
-        s, h = i // heads, lax.rem(i, heads)
+        s = i // (heads // 2)
+        both = [2 * lax.rem(i, heads // 2) + b for b in range(2)]
         pos = rows_of(s, rows)
 
-        def part_of(c):
+        def part_of(c, h):
             cols = pl.ds(pl.multiple_of(c * wide + h * size, size), size)
             return jnp.concatenate([qkv[j, pos, cols] for j in range(4)], axis=0)
 
-        raw = dot(part_of(0), part_of(1), NT)
-        scores = masked_scores(raw, slopes[h], prefix[s], t, rows, size)
-        expon = jnp.exp(scores - jnp.max(scores, axis=-1, keepdims=True))
-        probs = (expon / jnp.sum(expon, axis=-1, keepdims=True)).astype(BF)
-        got = dot(probs, part_of(2)).astype(BF)
-        for j in range(4):
-            mix[j, pos, rows_of(h, size)] = got[j * rows : (j + 1) * rows]
-
-    tiles(seqs * heads, head)
+        raw = [dot(part_of(0, h), part_of(1, h), NT) for h in both]
+        scores = [masked_scores(raw[b], slopes[both[b]], prefix[s], t, rows, size) for b in range(2)]
+        expon = [jnp.exp(v - jnp.max(v, axis=-1, keepdims=True)) for v in scores]
+        probs = [(v / jnp.sum(v, axis=-1, keepdims=True)).astype(BF) for v in expon]
+        got = [dot(probs[b], part_of(2, both[b])).astype(BF) for b in range(2)]
+        for b in range(2):
+            for j in range(4):
+                mix[j, pos, rows_of(both[b], size)] = got[b][j * rows : (j + 1) * rows]
+
+    tiles(seqs * heads // 2, head)
     keep(mix, mix_out)
 
-    def project(pair_of, put):
-        lhs_blocks = pair_of
+    def columns(c):
+        return pl.ds(c * (D // 2), D // 2)
+
+    def project(lhs_blocks, put, c):
 
         def body(i):
             lhs = jnp.concatenate([mix[lhs_blocks[0]], mix[lhs_blocks[1]]], axis=0)
             got = dot(lhs, vo[i])
             put(rows_of(i, deep), got)
 
-        tiles(n, body)
+        half_tiles(n, c, body)
 
     def put_send(cols, got):
         s1[0, :, cols] = got[:R].astype(BF)
@@ -414,20 +418,35 @@
         part[0, :, cols] = got[:R]
         part[1, :, cols] = got[R:]
 
-    to_core = remote(s1, r1, rs_s.at[0], rs_r.at[0], core)
-    to_chip = remote(sy, ry, rs_s.at[1], rs_r.at[1], chip)
-    project((3, 1), put_send)
-    to_core.start()
-    project((2, 0), put_part)
-    to_core.wait_recv()
-
-    def add_chip(i):
-        sl = rows_of(i, tile)
-        sy[sl, :] = (part[0, sl, :] + r1[0, sl, :].astype(F32)).astype(BF)
-
-    tiles(R // tile, add_chip)
-    to_chip.start()
-    to_chip.wait_recv()
+    def to_core(c):
+        at = columns(c)
+        return remote(s1.at[:, :, at], r1.at[:, :, at], rs_s.at[c], rs_r.at[c], core)
+
+    def to_chip(c):
+        at = columns(c)
+        return remote(sy.at[:, at], ry.at[:, at], rs_s.at[2 + c], rs_r.at[2 + c], chip)
+
+    def add_chip(c):
+        to_core(c).wait_recv()
+
+        def body(i):
+            sl = rows_of(i, tile)
+            at = columns(c)
+            sy[sl, at] = (part[0, sl, at] + r1[0, sl, at].astype(F32)).astype(BF)
+
+        tiles(R // tile, body)
+        to_chip(c).start()
+
+    project((3, 1), put_send, 0)
+    to_core(0).start()
+    project((2, 0), put_part, 0)
+    project((3, 1), put_send, 1)
+    to_core(1).start()
+    add_chip(0)
+    project((2, 0), put_part, 1)
+    add_chip(1)
+    to_chip(0).wait_recv()
+    to_chip(1).wait_recv()
 
     def middle_body(i):
         sl = rows_of(i, tile)
@@ -603,8 +622,9 @@
         pair(0, k).wait_send()
     for i in range(6):
         ag(i // 2, i % 2).wait_send()
-    to_core.wait_send()
-    to_chip.wait_send()
+    for c in range(2):
+        to_core(c).wait_send()
+        to_chip(c).wait_send()
     for i in range(4):
         if i in (1, 2):
             ag8(i, 0).wait_send()
@@ -674,7 +694,7 @@
         V((4, R, D), F32), V((4, R, D), BF), V((4, R, D), BF), V((4, R, D), BF), V((4, R, D), BF),
         dma(4 * (n - 1)), dma(4 * (n - 1)), dma(2 * (n - 1)), dma(2 * (n - 1)), dma(5), dma(4), dma(10),
         dma(2), dma(2),
-        dma(6), dma(6), dma(2), dma(2), dma(8), dma(8), dma(4), dma(4), dma(4), dma(4), dma(4), dma(4),
+        dma(6), dma(6), dma(4), dma(4), dma(8), dma(8), dma(4), dma(4), dma(4), dma(4), dma(4), dma(4),
         dma(4), dma(4), dma(4), dma(4), dma(2), dma(2), dma(n - 1), dma(2), dma(2),
     ]
     return pl.pallas_call(
@@ -772,7 +792,12 @@
             ffn(1, k).start()
 
     def feed(vu, vd, sec, act, dup, upb):
-        loads = [load(wd, vd, 3), load(wu, vu, 2), load(sec_in, sec, 4), load(act_in, act, 5)]
+        load_d = pltpu.make_async_copy(wd, vd, load_sem.at[3])
+        load_u = pltpu.make_async_copy(wu, vu, load_sem.at[2])
+        later = [
+            pltpu.make_async_copy(sec_in, sec, load_sem.at[4]),
+            pltpu.make_async_copy(act_in, act, load_sem.at[5]),
+        ]
 
         def up_load(number, turn):
             i, slot = turn[number], number % 2
@@ -789,15 +814,18 @@
                     for copy in up_load(number, order[:: 1 - 2 * layer]):
                         copy.start()
 
+        load_d.start()
 
         @pl.when(sect == 1)
         def _():
             load_top.start()
+            load_u.start()
             grad[...] = top[...]
             load_top.wait()
 
         @pl.when(sect == 0)
         def _():
+            load_u.start()
             relay(1)
             for h in range(2):
                 over(h).wait_recv()
@@ -812,8 +840,7 @@
             col_sum(5, grad[rows_of(j, tile), :].astype(F32))
 
         tiles(R // tile, bias_body)
-        for copy in loads:
-            copy.wait()
+        load_d.wait()
         tu = min(256, half)
         td = min(256, D)
 
@@ -860,6 +887,11 @@
                 for copy in up_load(number + 2, turn):
                     copy.start()
 
+            if number == 0:
+                load_u.wait()
+                for copy in later:
+                    copy.start()
+
             def second_body(j):
                 cols = rows_of(j, td)
                 lhs = jnp.concatenate([dup[i], dup[4 + i]], axis=0)
@@ -900,6 +932,9 @@
         @pl.when(sect == 1)
         def _():
             every(order[::-1], False)
+
+        for copy in later:
+            copy.wait()
 
         th_ = min(256, half)
         for k in list(range(n - 1, 0, -1)) + [0]:
@@ -971,8 +1006,28 @@
         half_tiles(R // tile, h, mid_body)
         ag(1, h).start()
         ag(0, h).start()
-    to_core = remote(s1, r1, rs_s.at[0], rs_r.at[0], core)
-    to_chip = remote(sy, ry, rs_s.at[1], rs_r.at[1], chip)
+    def columns(c):
+        return pl.ds(c * (D // 2), D // 2)
+
+    def to_core(c):
+        at = columns(c)
+        return remote(s1.at[:, :, at], r1.at[:, :, at], rs_s.at[c], rs_r.at[c], core)
+
+    def to_chip(c):
+        at = columns(c)
+        return remote(sy.at[:, at], ry.at[:, at], rs_s.at[2 + c], rs_r.at[2 + c], chip)
+
+    def add_chip(c):
+        to_core(c).wait_recv()
+
+        def body(i):
+            sl = rows_of(i, tile)
+            at = columns(c)
+            sy[sl, at] = (part[0, sl, at] + r1[0, sl, at].astype(F32)).astype(BF)
+
+        tiles(R // tile, body)
+        to_chip(c).start()
+
 
     def low_bit(k):
         return k & -k
@@ -1058,30 +1113,35 @@
                 att_start(k, 3)
 
         def head(i):
-            s, h = i // heads, lax.rem(i, heads)
+            s = i // (heads // 2)
             pos = rows_of(s, rows)
 
-            def part_of(ref, c):
+            def part_of(ref, c, h):
                 cols = pl.ds(pl.multiple_of(c * wide + h * size, size), size)
                 return jnp.concatenate([ref[j, pos, cols] for j in range(4)], axis=0)
 
-            q, k, v, dm = part_of(qkv, 0), part_of(qkv, 1), part_of(qkv, 2), part_of(dmix, 0)
-            scores = masked_scores(dot(q, k, NT), slopes[h], prefix[s], t, rows, size)
-            expon = jnp.exp(scores - jnp.max(scores, axis=-1, keepdims=True))
-            probs = expon / jnp.sum(expon, axis=-1, keepdims=True)
-            dp = dot(dm, v, NT)
-            inner = jnp.sum(probs * dp, axis=-1, keepdims=True)
-            raw = (probs * (dp - inner) * np.float32(size ** (-0.5))).astype(BF)
-            for c, got in enumerate((dot(raw, k), dot(raw, q, TN), dot(probs.astype(BF), dm, TN))):
-                low = got.astype(BF)
-                cols = pl.ds(pl.multiple_of(c * wide + h * size, size), size)
-                proj[0:1, cols] += jnp.sum(low.astype(F32), axis=0, keepdims=True)
-                for j in range(4):
-                    dqkv[j, pos, cols] = low[j * rows : (j + 1) * rows]
-
-        tiles(seqs * heads, head)
-
-        def normed(blocks, put):
+            def one(h):
+                q, k, v, dm = part_of(qkv, 0, h), part_of(qkv, 1, h), part_of(qkv, 2, h), part_of(dmix, 0, h)
+                scores = masked_scores(dot(q, k, NT), slopes[h], prefix[s], t, rows, size)
+                dp = dot(dm, v, NT)
+                expon = jnp.exp(scores - jnp.max(scores, axis=-1, keepdims=True))
+                probs = expon / jnp.sum(expon, axis=-1, keepdims=True)
+                inner = jnp.sum(probs * dp, axis=-1, keepdims=True)
+                raw = (probs * (dp - inner) * np.float32(size ** (-0.5))).astype(BF)
+                return [g.astype(BF) for g in (dot(raw, k), dot(raw, q, TN), dot(probs.astype(BF), dm, TN))]
+
+            both = [2 * lax.rem(i, heads // 2) + b for b in range(2)]
+            results = [one(h) for h in both]
+            for h, result in zip(both, results):
+                for c, low in enumerate(result):
+                    cols = pl.ds(pl.multiple_of(c * wide + h * size, size), size)
+                    proj[0:1, cols] += jnp.sum(low.astype(F32), axis=0, keepdims=True)
+                    for j in range(4):
+                        dqkv[j, pos, cols] = low[j * rows : (j + 1) * rows]
+
+        tiles(seqs * heads // 2, head)
+
+        def normed(blocks, put, c_half):
             td = min(256, D)
 
             def body(j):
@@ -1093,7 +1153,7 @@
                     got = term if got is None else got + term
                 put(cols, got)
 
-            tiles(D // td, body)
+            half_tiles(D // td, c_half, body)
 
         def put_send(cols, got):
             s1[0, :, cols] = got[:R].astype(BF)
@@ -1104,17 +1164,14 @@
             part[1, :, cols] = got[R:]
 
         def normed_all():
-            normed((3, 1), put_send)
-            to_core.start()
-            normed((2, 0), put_part)
-            to_core.wait_recv()
-
-            def add_chip(i):
-                sl = rows_of(i, tile)
-                sy[sl, :] = (part[0, sl, :] + r1[0, sl, :].astype(F32)).astype(BF)
-
-            tiles(R // tile, add_chip)
-            to_chip.start()
+            normed((3, 1), put_send, 0)
+            to_core(0).start()
+            normed((2, 0), put_part, 0)
+            normed((3, 1), put_send, 1)
+            to_core(1).start()
+            add_chip(0)
+            normed((2, 0), put_part, 1)
+            add_chip(1)
 
         def grads_q():
             for k in send_order + [0]:
@@ -1145,8 +1202,9 @@
         pltpu.VMEM((4, R, 3 * wide), BF), pltpu.VMEM((4, R, wide), BF), pltpu.VMEM((4, R, wide), BF),
         pltpu.VMEM((4, R, 3 * wide), BF),
     )
-    to_chip.wait_recv()
-    to_core.wait_send()
+    for c in range(2):
+        to_chip(c).wait_recv()
+        to_core(c).wait_send()
 
     def low_body(j):
         sl = rows_of(j, tile)
@@ -1243,49 +1301,34 @@
     put(low_v, low_out)
 
     def final_feed(bu, bd, fu, fd):
-        for a in range(2):
-            for k in range(n - 1, 0, -1):
+        stores = []
+        turn = [1] + list(range(n - 1, 1, -1))
+        for k in turn:
+            for a in (1, 0):
+                own, got, buf, total = ((gu, ru, bu, fu), (gd, rd, bd, fd))[a]
                 ffn(a, k).wait_recv()
-        loads = [load(ru, bu, 2), load(rd, bd, 3)]
-        for copy in loads:
-            copy.wait()
-        step = min(64, deep)
-
-        def up_body(j):
-            sl = rows_of(j, step)
-            same = gu[0, sl, :].astype(F32)
-            other = bu[0, sl, :].astype(F32)
-            for k in range(2, n):
-                if k % 2 == 0:
-                    same = same + bu[k - 1, sl, :].astype(F32)
-                else:
-                    other = other + bu[k - 1, sl, :].astype(F32)
-            fu[0, sl, :] = same
-            fu[1, sl, :] = other
-
-        tiles(deep // step, up_body)
-
-        def down_body(j):
-            sl = rows_of(j, step)
-            same = gd[0, sl, :].astype(F32)
-            other = bd[0, sl, :].astype(F32)
-            for k in range(2, n):
-                if k % 2 == 0:
-                    same = same + bd[k - 1, sl, :].astype(F32)
-                else:
-                    other = other + bd[k - 1, sl, :].astype(F32)
-            fd[0, sl, :] = same
-            fd[1, sl, :] = other
-
-        tiles(half // step, down_body)
-        copies = []
-        for b in range(2):
-            at = pl.ds(pl.multiple_of((zl ^ b) * half, half), half)
-            copies.append(pltpu.make_async_copy(fu.at[b], gu_out.at[:, at], load_sem.at[2 + 2 * b]))
-            copies.append(pltpu.make_async_copy(fd.at[b], gd_out.at[at, :], load_sem.at[3 + 2 * b]))
-        for copy in copies:
-            copy.start()
-        for copy in copies:
+                copy = load(got.at[k - 1], buf.at[k - 1], 2 + a)
+                copy.wait()
+                b = k & 1
+                same = [other for other in turn if other & 1 == b]
+                step = min(64, deep)
+
+                def body(j):
+                    sl = rows_of(j, step)
+                    value = buf[k - 1, sl, :].astype(F32)
+                    if k != same[0]:
+                        value = value + total[b, sl, :]
+                    elif b == 0:
+                        value = value + own[0, sl, :].astype(F32)
+                    total[b, sl, :] = value
+
+                tiles(total.shape[1] // step, body)
+                if k == same[-1]:
+                    at = pl.ds(pl.multiple_of((zl ^ b) * half, half), half)
+                    dst = gu_out.at[:, at] if a == 0 else gd_out.at[at, :]
+                    stores.append(pltpu.make_async_copy(total.at[b], dst, load_sem.at[4 + 2 * a + b]))
+                    stores[-1].start()
+        for copy in stores:
             copy.wait()
 
     pl.run_scoped(
@@ -1295,40 +1338,31 @@
     )
 
     def final_attention(bq, bo, fq, fo):
-        last = [k for k in send_order if k == low_bit(k)]
+        last = [k for k in range(1, n) if k == low_bit(k)]
+        stores = []
         for k in last:
-            for c in range(4):
+            for c in (3, 0, 1, 2):
                 att(k, c).wait_recv()
-        loads = [load(rq, bq, 2), load(ro, bo, 3)]
-        for copy in loads:
-            copy.wait()
-        step = min(64, deep)
-
-        def q_body(j):
-            sl = rows_of(j, step)
-            for c in range(3):
-                total = gq[0, c, sl, :].astype(F32)
-                for k in last:
-                    total = total + bq[k - 1, c, sl, :].astype(F32)
-                fq[c, sl, :] = total
-
-        tiles(deep // step, q_body)
-
-        def o_body(j):
-            sl = rows_of(j, step)
-            total = go[0, sl, :].astype(F32)
-            for k in last:
-                total = total + bo[k - 1, sl, :].astype(F32)
-            fo[sl, :] = total
-
-        tiles(wide // step, o_body)
-        copies = [
-            pltpu.make_async_copy(fq, gq_out, load_sem.at[2]),
-            pltpu.make_async_copy(fo, go_out, load_sem.at[3]),
-        ]
-        for copy in copies:
-            copy.start()
-        for copy in copies:
+                src, buf = (rq.at[k - 1, c], bq.at[k - 1, c]) if c < 3 else (ro.at[k - 1], bo.at[k - 1])
+                copy = load(src, buf, 2)
+                copy.wait()
+                step = min(64, deep)
+
+                def body(j):
+                    sl = rows_of(j, step)
+                    if c < 3:
+                        first = gq[0, c, sl, :].astype(F32) if k == 1 else fq[c, sl, :]
+                        fq[c, sl, :] = first + bq[k - 1, c, sl, :].astype(F32)
+                    else:
+                        first = go[0, sl, :].astype(F32) if k == 1 else fo[sl, :]
+                        fo[sl, :] = first + bo[k - 1, sl, :].astype(F32)
+
+                tiles((deep if c < 3 else wide) // step, body)
+                if k == last[-1]:
+                    src, dst = (fq.at[c], gq_out.at[c]) if c < 3 else (fo, go_out)
+                    stores.append(pltpu.make_async_copy(src, dst, load_sem.at[4 + c]))
+                    stores[-1].start()
+        for copy in stores:
             copy.wait()
 
     pl.run_scoped(
@@ -1351,7 +1385,8 @@
         core8(i).wait_send()
     for i in range(6):
         ag(i // 2, i % 2).wait_send()
-    to_chip.wait_send()
+    to_chip(0).wait_send()
+    to_chip(1).wait_send()
     for layer in range(2):
         @pl.when(sect == layer)
         def _():
@@ -1414,7 +1449,7 @@
         V((8, 128), F32), V((24, 128), F32), dma(4 * n), dma(4 * n), dma(n), dma(n),
         dma(8), dma(4), dma(4), dma(2), dma(2),
         dma(8), dma(8), dma(4), dma(4), dma(4), dma(4), dma(4), dma(4),
-        dma(6), dma(6), dma(2), dma(2), dma(2 * (n - 1)), dma(2 * (n - 1)), dma(4 * (n - 1)), dma(4 * (n - 1)), dma(n - 1), dma(n - 1),
+        dma(6), dma(6), dma(4), dma(4), dma(2 * (n - 1)), dma(2 * (n - 1)), dma(4 * (n - 1)), dma(4 * (n - 1)), dma(n - 1), dma(n - 1),
         dma(4 * (n - 1)), dma(4 * (n - 1)), dma(4 * (n - 1)), dma(2), dma(2),
     ]
     return pl.pallas_call(

time: 845 us -> 841 us (level)
  no operation moved by 1% of the time
where the time goes in v7:
time: 841 us; the launch traced here: 839 us
  Pallas kernels  820 us (98%)
  local copies, waits for them, and re-layouts  13.2 us (2%)
    pallas_call x1, Pallas kernels, run_backward(): pl.pallas_call(functools.partial(backward_kernel, dims), out_shape=outs,...  493 us
    pallas_call x1, Pallas kernels, run_forward(): pl.pallas_call(functools.partial(forward_kernel, dims), out_shape=outs, i...  326 us

profile of v7, /device:TPU:0, one launch (start us, length us, event | category | flops | bytes accessed | tf_op | source)
XLA Modules:
  0.0 838.7 jit_solution(1310430275591287980)
XLA Ops:
  0.7 0.7 convert_select_fusion
  1.4 0.7 bitcast_convert_fusion
  2.1 0.1 tile.21
  2.2 0.7 tile.8
  2.9 0.1 tile.9
  2.9 0.1 pad.1.clone
  3.0 0.7 pad_maximum_fusion.note
  3.7 0.5 multiply_exponential_fusion.slopes
  4.2 326.4 %shard_map.169 = (f32[128,2048]{1,0:T(8,128)}, bf16[3,2048,512]{2,1,0:T(8,128)(2,1)}, bf16[4,512,512]{2,1,0:T(8,128)(2,1)}, bf16[2048,1024]{1,0:T(8,128)(2,1)}, ...) custom-call(bf16[128,2048]{1,0:T(8,128)(2,1)} %bitcast.31, ...), custom_call_target="tpu_custom_call" | custom-call | tf_op jit(solution)/shard_map/pallas_call | solution.py:700
  330.6 493.3 %shard_map.170 = (f32[128,2048]{1,0:T(8,128)}, f32[3,512,512]{2,1,0:T(8,128)}, f32[512,512]{1,0:T(8,128)}, f32[512,2048]{1,0:T(8,128)}, f32[2048,512]{1,0:T(8,12...) custom-call(bf16[128,2048]{1,0:T(8,128)(2,1)} %bitcast.32, ...), custom_call_target="tpu_custom_call" | custom-call | tf_op jit(solution)/shard_map/pallas_call | solution.py:1455
  823.9 0.0 copy-start.4
  823.9 0.0 copy-start.5
  823.9 0.0 copy-start.2
  824.0 2.5 broadcast_select_fusion
  826.4 0.0 copy-done.4
  826.4 0.7 dynamic-slice_bitcast_fusion
  827.1 0.7 constant_dynamic-slice_fusion
  827.8 0.0 copy-done.5
  827.8 0.6 slice_bitcast_fusion
  828.4 0.6 slice_bitcast_fusion.1
  828.9 0.0 copy-done.2
  828.9 0.0 copy-start.3
  828.9 0.0 copy-start.1
  828.9 1.7 copy.23
  830.6 0.3 copy-done.3
  830.9 1.0 copy.24
  831.9 1.1 copy-done.1
  833.0 0.0 copy-start
  833.0 2.1 copy.25
  835.1 1.6 copy-done
  836.7 2.0 copy.26
  (6 shorter events, 0.0 us)
Async XLA Ops:
  823.9 2.5 copy-start.4
  823.9 3.9 copy-start.5
  823.9 5.0 copy-start.2
  828.9 2.0 copy-start.3
  828.9 4.0 copy-start.1
  833.0 3.7 copy-start

commit v8 on v7

--- a/solution.py
+++ b/solution.py
@@ -15,8 +15,8 @@
 MESH = pl.DeviceIdType.MESH
 EARLY = True
 RELAYED = ((3,), ())
-GRADS_RELAYED = ((), (3, 2))
-ATT_RELAYED = (0, 1, 2)
+GRADS_RELAYED = ((3,), (3, 2,1))
+ATT_RELAYED = (0, 1)
 NT = (((1,), (1,)), ((), ()))
 TN = (((0,), (0,)), ((), ()))
 
@@ -783,7 +783,10 @@
         return remote(gd.at[k], lent.at[k - 1], lent_s.at[k - 1], lent_r.at[k - 1], across)
 
     def ffn_start(layer, k):
-        (lend if k in GRADS_RELAYED[layer] else direct)(k).start()
+        if k not in GRADS_RELAYED[layer]:
+            direct(k).start()
+        elif layer == 0:
+            lend(k).start()
         ffn(0, k).start()
 
     def relay(layer):
@@ -794,10 +797,19 @@
     def feed(vu, vd, sec, act, dup, upb):
         load_d = pltpu.make_async_copy(wd, vd, load_sem.at[3])
         load_u = pltpu.make_async_copy(wu, vu, load_sem.at[2])
-        later = [
-            pltpu.make_async_copy(sec_in, sec, load_sem.at[4]),
-            pltpu.make_async_copy(act_in, act, load_sem.at[5]),
-        ]
+        load_a = pltpu.make_async_copy(act_in, act, load_sem.at[5])
+        load_s = pltpu.make_async_copy(sec_in, sec, load_sem.at[4])
+        th_ = min(256, half)
+
+        def down_grad(k):
+            def body(j):
+                cols = rows_of(j, th_)
+                lhs = act[:, :, cols].reshape(8 * R, th_)
+                at = pl.ds(pl.multiple_of((z ^ k) * deep, deep), deep)
+                gd[k, cols, :] = dot(lhs, gp[:, :, at].reshape(8 * R, deep), TN).astype(BF)
+
+            tiles(half // th_, body)
+
 
         def up_load(number, turn):
             i, slot = turn[number], number % 2
@@ -819,13 +831,19 @@
         @pl.when(sect == 1)
         def _():
             load_top.start()
+            load_a.start()
             load_u.start()
             grad[...] = top[...]
             load_top.wait()
+            load_a.wait()
+            for k in GRADS_RELAYED[1]:
+                down_grad(k)
+                lend(k).start()
 
         @pl.when(sect == 0)
         def _():
             load_u.start()
+            load_a.start()
             relay(1)
             for h in range(2):
                 over(h).wait_recv()
@@ -889,8 +907,7 @@
 
             if number == 0:
                 load_u.wait()
-                for copy in later:
-                    copy.start()
+                load_s.start()
 
             def second_body(j):
                 cols = rows_of(j, td)
@@ -933,18 +950,17 @@
         def _():
             every(order[::-1], False)
 
-        for copy in later:
-            copy.wait()
-
-        th_ = min(256, half)
+        load_s.wait()
+
+        @pl.when(sect == 0)
+        def _():
+            load_a.wait()
+
         for k in list(range(n - 1, 0, -1)) + [0]:
-            def down_body(j):
-                cols = rows_of(j, th_)
-                lhs = act[:, :, cols].reshape(8 * R, th_)
-                at = pl.ds(pl.multiple_of((z ^ k) * deep, deep), deep)
-                gd[k, cols, :] = dot(lhs, gp[:, :, at].reshape(8 * R, deep), TN).astype(BF)
-
-            tiles(half // th_, down_body)
+            if k in GRADS_RELAYED[1]:
+                pl.when(sect == 0)(functools.partial(down_grad, k))
+            else:
+                down_grad(k)
             dd = min(256, deep)
 
             def up_body(j):

time: 841 us -> 826 us (0.982)
  Pallas kernels: 820 us -> 806 us
    pallas_call x1, Pallas kernels: 493 us -> 480 us  [run_backward(): pl.pallas_call(functools.partial(backward_kernel, dims), out_shape=outs,...]
where the time goes in v8:
time: 826 us; the launch traced here: 825 us
  Pallas kernels  806 us (98%)
  local copies, waits for them, and re-layouts  13.2 us (2%)
    pallas_call x1, Pallas kernels, run_backward(): pl.pallas_call(functools.partial(backward_kernel, dims), out_shape=outs,...  480 us
    pallas_call x1, Pallas kernels, run_forward(): pl.pallas_call(functools.partial(forward_kernel, dims), out_shape=outs, i...  326 us

profile of v8, /device:TPU:0, one launch (start us, length us, event | category | flops | bytes accessed | tf_op | source)
XLA Modules:
  0.0 825.1 jit_solution(2867058265426842380)
XLA Ops:
  0.7 0.7 convert_select_fusion
  1.4 0.7 bitcast_convert_fusion
  2.1 0.1 tile.21
  2.2 0.7 tile.8
  2.9 0.1 tile.9
  2.9 0.1 pad.1.clone
  3.0 0.7 pad_maximum_fusion.note
  3.7 0.5 multiply_exponential_fusion.slopes
  4.2 326.4 %shard_map.169 = (f32[128,2048]{1,0:T(8,128)}, bf16[3,2048,512]{2,1,0:T(8,128)(2,1)}, bf16[4,512,512]{2,1,0:T(8,128)(2,1)}, bf16[2048,1024]{1,0:T(8,128)(2,1)}, ...) custom-call(bf16[128,2048]{1,0:T(8,128)(2,1)} %bitcast.31, ...), custom_call_target="tpu_custom_call" | custom-call | tf_op jit(solution)/shard_map/pallas_call | solution.py:700
  330.6 479.7 %shard_map.170 = (f32[128,2048]{1,0:T(8,128)}, f32[3,512,512]{2,1,0:T(8,128)}, f32[512,512]{1,0:T(8,128)}, f32[512,2048]{1,0:T(8,128)}, f32[2048,512]{1,0:T(8,12...) custom-call(bf16[128,2048]{1,0:T(8,128)(2,1)} %bitcast.32, ...), custom_call_target="tpu_custom_call" | custom-call | tf_op jit(solution)/shard_map/pallas_call | solution.py:1471
  810.3 0.0 copy-start.4
  810.3 0.0 copy-start.5
  810.3 0.0 copy-start.2
  810.4 2.5 broadcast_select_fusion
  812.8 0.0 copy-done.4
  812.8 0.7 dynamic-slice_bitcast_fusion
  813.5 0.7 constant_dynamic-slice_fusion
  814.2 0.0 copy-done.5
  814.2 0.6 slice_bitcast_fusion
  814.8 0.6 slice_bitcast_fusion.1
  815.3 0.0 copy-done.2
  815.3 0.0 copy-start.3
  815.3 0.0 copy-start.1
  815.3 1.7 copy.23
  817.0 0.3 copy-done.3
  817.3 1.0 copy.24
  818.3 1.1 copy-done.1
  819.4 0.0 copy-start
  819.4 2.1 copy.25
  821.5 1.6 copy-done
  823.1 2.0 copy.26
  (6 shorter events, 0.0 us)
Async XLA Ops:
  810.3 2.5 copy-start.4
  810.3 3.9 copy-start.5
  810.3 5.0 copy-start.2
  815.3 2.0 copy-start.3
  815.3 4.0 copy-start.1
  819.4 3.7 copy-start
